TPU v7x, 256 devices: a whole 4x4x8 slice. The times are simulated.
256 devices in a mesh: dom: 32 (over x, y, core), board: 8 (over z).
Axes of the slice: x: 4, y: 4, z: 8, core: 2. Of those that a mesh axis runs over, the one named last changes fastest.
Arguments:
- block: bfloat16 [64, 1048576], P(None, ('dom', 'board')), may hold values from -120 to 120, as said below
- tiles: bfloat16 [8192, 10, 128, 128], P(('dom', 'board')), may hold values from -0.15625 to 0.15625
- cols: int32 [8192, 10], P(('dom', 'board')), may hold values from 0 to 8191, as said below
- counts: int32 [8192], P(('dom', 'board')), may hold values from 2 to 10, as said below
Outputs:
- basis: bfloat16 [64, 1048576], P(None, ('dom', 'board'))
- projected: float32 [64, 64], replicated
Inputs may be any that keep to these rules, and one draw needn't show every extreme that they name: `block`: entries are below 120 in magnitude. `cols`: slot 0 of row r holds column r; slot 1 holds r + 8 or r - 8 (where that lies in the grid, else the nearest end); every column lies within 8 of its row. `counts`: slots at or past the count are ignored.
All inputs are finite; a program needn't handle non-finite values.
Results may differ from a plain program's by a relative error of at most 0.0072.
Values may be sent and summed in bfloat16 or wider, within the bound.
No kernel may reach another device: no remote copies, remote signals or barrier semaphores. Data moves between devices by JAX's collectives and lax.ppermute only.
A program may use at most 64 MiB of HBM per device.

v0:
```python
import jax
import jax.numpy as jnp
from jax import lax
from jax.sharding import PartitionSpec as P

DEG = 4
GHOST = 8


def extended(cells, sides, width):
    for axis, dim in sides:
        count = lax.axis_size(axis)
        ends = count - 1
        head = lax.slice_in_dim(cells, 0, width, axis=dim)
        tail = lax.slice_in_dim(cells, cells.shape[dim] - width, cells.shape[dim], axis=dim)
        cells = jnp.concatenate(
            [
                lax.ppermute(tail, axis, [(i, (i + 1) % count) for i in range(ends)]),
                cells,
                lax.ppermute(head, axis, [((i + 1) % count, i) for i in range(ends)]),
            ],
            axis=dim,
        )
    return cells


def apply_rows(field, tiles, cols, counts, base):
    rows_of = field.shape[0]
    width = tiles.shape[2]
    blocks = field.reshape(rows_of, -1, width)
    local = jnp.clip(cols - base, 0, blocks.shape[1] - 1)
    picked = jnp.take(blocks, local, axis=1)
    live = (lax.broadcasted_iota(jnp.int32, cols.shape, 1) < counts[:, None]).astype(field.dtype)
    picked = picked * live[None, :, :, None]
    result = jnp.einsum("krsj,rsij->kri", picked, tiles, preferred_element_type=jnp.float32)
    return result.reshape(rows_of, -1)


def one_hop(field, tiles, cols, counts, first):
    width = tiles.shape[2]
    padded = extended(field, ((("dom", "board"), 1),), GHOST * width)
    return apply_rows(padded, tiles, cols, counts, first - GHOST)


def body(block, tiles, cols, counts):
    td_rows = tiles.shape[0]
    width = tiles.shape[2]
    first = lax.axis_index(("dom", "board")) * td_rows
    older = block
    current = block
    for degree in range(DEG):
        image = one_hop(current, tiles, cols, counts, first)
        if degree > 0:
            image = 2.0 * image - older.astype(jnp.float32)
        older, current = (current, image.astype(jnp.bfloat16))
    nodes_all = lax.axis_size(("dom", "board")) * td_rows * width
    gram_local = jnp.dot(current, current.T, preferred_element_type=jnp.float32)
    gram = lax.psum(gram_local, ("dom", "board"))
    image = one_hop(current, tiles, cols, counts, first).astype(jnp.bfloat16)
    cross_local = jnp.dot(current, image.T, preferred_element_type=jnp.float32)
    cross = lax.psum(cross_local, ("dom", "board"))
    gram = gram / nodes_all
    cross = cross / nodes_all
    factor = jnp.linalg.cholesky(gram)
    identity = jnp.eye(gram.shape[0], dtype=jnp.float32)
    inverse = jax.scipy.linalg.solve_triangular(factor, identity, lower=True)
    basis = jnp.dot(inverse, current.astype(jnp.float32), precision=lax.Precision.HIGHEST).astype(
        jnp.bfloat16
    )
    half = jnp.dot(inverse, cross, precision=lax.Precision.HIGHEST)
    projected = jnp.dot(half, inverse.T, precision=lax.Precision.HIGHEST)
    return (basis, projected)


def solution(mesh):
    return jax.shard_map(
        body,
        mesh=mesh,
        in_specs=(
            P(None, ("dom", "board")),
            P(("dom", "board"), None, None, None),
            P(("dom", "board"), None),
            P(("dom", "board")),
        ),
        out_specs=(P(None, ("dom", "board")), P()),
        check_vma=False,
    )
```

profile of v0, /device:TPU:1, one launch (start us, length us, event | category | flops | bytes accessed | tf_op | source)
XLA Modules:
  0.0 267.4 jit_solution(1303580442261036877)
XLA Ops:
  0.6 1.0 fusion.64
  1.6 4.4 %collective-permute-start = (bf16[64,1024]{1,0:T(8,128)(2,1)S(1)}, bf16[64,1024]{1,0:T(8,128)(2,1)S(1)}, u32[]{:S(2)}, u32[]{:S(2)}) collective-permute-start(bf16[64,1024]{1,0:T(8,128)(2,1)S(1)} %get-tuple-element.15), channel_id=1, source_target_pairs={{0,1},{1,2},{2,3},{3,4},{4,5},{5,6},{6,7},{7,8},{8,9},{9,10},{10,1... | collective-permute-start | bytes 393224 | tf_op jit(solution)/shard_map/ppermute | solution.py:18
  6.0 6.4 %collective-permute-start.1 = (bf16[64,1024]{1,0:T(8,128)(2,1)S(1)}, bf16[64,1024]{1,0:T(8,128)(2,1)S(1)}, u32[]{:S(2)}, u32[]{:S(2)}) collective-permute-start(bf16[64,1024]{1,0:T(8,128)(2,1)S(1)} %get-tuple-element.16), channel_id=1, source_target_pairs={{1,0},{2,1},{3,2},{4,3},{5,4},{6,5},{7,6},{8,7},{9,8},{10,9},{11,1... | collective-permute-start | bytes 393224 | tf_op jit(solution)/shard_map/ppermute | solution.py:20
  12.4 0.7 compare_and_fusion
  13.2 0.7 fusion.53
  13.9 0.1 copy.33
  14.0 0.1 copy.37
  14.1 0.1 reshape.121
  14.2 0.0 collective-permute-done
  14.2 0.2 collective-permute-done.1
  14.4 1.3 copy_bitcast_fusion.4
  15.6 13.3 %gather_fusion = bf16[320,64,128]{2,1,0:T(8,128)(2,1)} fusion(bf16[64,48,128]{2,0,1:T(8,128)(2,1)S(1)} %copy_bitcast_fusion.4, s32[1024]{0:T(1024)S(1)} %pad_clamp_fusion), kind=kCustom, calls=%fused_computation.clone | custom fusion | bytes 10487040 | tf_op jit(solution)/shard_map/jit(_take)/gather | solution.py:32
  29.0 8.0 %fusion.38 = bf16[32,8,8,128]{3,2,1,0:T(8,128)(2,1)S(1)} fusion(bf16[32,10,128,128]{3,2,1,0:T(8,128)(2,1)} %param.7, bf16[32,10,64,128]{3,2,1,0:T(8,128)(2,1)} %bitcast.168, pred[32,10]{1,0:T(8,128)(4,1)S(1)} %copy.33, bf16[32,10]{1,0:T(8,128)(2,1)S(1)} %fusion.53), kind=kOutput, calls=%fused_computation.49 | convolution fusion | flops 676593664 | bytes 16253888 | tf_op jit(solution)/shard_map/krsj,rsij->kri/dot_general | solution.py:35
  36.9 0.1 copy.88
  37.1 1.9 collective-permute-start.2
  39.0 5.7 %collective-permute-start.3 = (bf16[64,1024]{1,0:T(8,128)(2,1)S(1)}, bf16[64,1024]{1,0:T(8,128)(2,1)S(1)}, u32[]{:S(2)}, u32[]{:S(2)}) collective-permute-start(bf16[64,1024]{1,0:T(8,128)(2,1)S(1)} %get-tuple-element.14), channel_id=1, source_target_pairs={{1,0},{2,1},{3,2},{4,3},{5,4},{6,5},{7,6},{8,7},{9,8},{10,9},{11,1... | collective-permute-start | bytes 393224 | tf_op jit(solution)/shard_map/ppermute | solution.py:20
  44.8 0.5 collective-permute-done.2
  45.3 1.2 collective-permute-done.3
  46.5 0.2 copy_bitcast_fusion.3
  46.7 13.3 %gather_fusion.1 = bf16[320,64,128]{2,1,0:T(8,128)(2,1)} fusion(bf16[64,48,128]{2,0,1:T(8,128)(2,1)S(1)} %copy_bitcast_fusion.3, s32[1024]{0:T(1024)S(1)} %pad_clamp_fusion), kind=kCustom, calls=%fused_computation.1.clone | custom fusion | bytes 10487040 | tf_op jit(solution)/shard_map/jit(_take)/gather | solution.py:32
  60.1 0.0 copy-start
  60.1 7.6 %fusion.35 = f32[32,8,8,128]{3,2,1,0:T(8,128)S(1)} fusion(bf16[32,10,128,128]{3,2,1,0:T(8,128)(2,1)} %param.7, bf16[32,10,64,128]{3,2,1,0:T(8,128)(2,1)} %bitcast.169, pred[32,10]{1,0:T(8,128)(4,1)S(1)} %copy.33, bf16[32,10]{1,0:T(8,128)(2,1)S(1)} %fusion.53), kind=kOutput, calls=%fused_computation.46 | convolution fusion | flops 676593664 | bytes 16778176 | tf_op jit(solution)/shard_map/krsj,rsij->kri/dot_general | solution.py:35
  67.7 0.0 copy-done
  67.7 0.1 fusion.42
  67.8 3.3 %collective-permute-start.4 = (bf16[64,1024]{1,0:T(8,128)(2,1)S(1)}, bf16[64,1024]{1,0:T(8,128)(2,1)S(1)}, u32[]{:S(2)}, u32[]{:S(2)}) collective-permute-start(bf16[64,1024]{1,0:T(8,128)(2,1)S(1)} %get-tuple-element.11), channel_id=1, source_target_pairs={{0,1},{1,2},{2,3},{3,4},{4,5},{5,6},{6,7},{7,8},{8,9},{9,10},{10,1... | collective-permute-start | bytes 393224 | tf_op jit(solution)/shard_map/ppermute | solution.py:18
  71.1 4.1 %collective-permute-start.5 = (bf16[64,1024]{1,0:T(8,128)(2,1)S(1)}, bf16[64,1024]{1,0:T(8,128)(2,1)S(1)}, u32[]{:S(2)}, u32[]{:S(2)}) collective-permute-start(bf16[64,1024]{1,0:T(8,128)(2,1)S(1)} %get-tuple-element.12), channel_id=1, source_target_pairs={{1,0},{2,1},{3,2},{4,3},{5,4},{6,5},{7,6},{8,7},{9,8},{10,9},{11,1... | collective-permute-start | bytes 393224 | tf_op jit(solution)/shard_map/ppermute | solution.py:20
  75.3 0.7 collective-permute-done.4
  76.0 1.2 collective-permute-done.5
  77.2 0.2 copy_bitcast_fusion.2
  77.4 13.3 %gather_fusion.2 = bf16[320,64,128]{2,1,0:T(8,128)(2,1)} fusion(bf16[64,48,128]{2,0,1:T(8,128)(2,1)S(1)} %copy_bitcast_fusion.2, s32[1024]{0:T(1024)S(1)} %pad_clamp_fusion), kind=kCustom, calls=%fused_computation.2.clone | custom fusion | bytes 10487040 | tf_op jit(solution)/shard_map/jit(_take)/gather | solution.py:32
  90.8 7.5 %fusion.33 = f32[32,8,8,128]{3,2,1,0:T(8,128)S(1)} fusion(bf16[32,10,128,128]{3,2,1,0:T(8,128)(2,1)} %param.7, bf16[32,10,64,128]{3,2,1,0:T(8,128)(2,1)} %bitcast.170, pred[32,10]{1,0:T(8,128)(4,1)S(1)} %copy.33, bf16[32,10]{1,0:T(8,128)(2,1)S(1)} %fusion.53), kind=kOutput, calls=%fused_computation.44 | convolution fusion | flops 676593664 | bytes 16778176 | tf_op jit(solution)/shard_map/krsj,rsij->kri/dot_general | solution.py:35
  98.3 0.1 fusion.41
  98.4 3.3 %collective-permute-start.6 = (bf16[64,1024]{1,0:T(8,128)(2,1)S(1)}, bf16[64,1024]{1,0:T(8,128)(2,1)S(1)}, u32[]{:S(2)}, u32[]{:S(2)}) collective-permute-start(bf16[64,1024]{1,0:T(8,128)(2,1)S(1)} %get-tuple-element.9), channel_id=1, source_target_pairs={{0,1},{1,2},{2,3},{3,4},{4,5},{5,6},{6,7},{7,8},{8,9},{9,10},{10,1... | collective-permute-start | bytes 393224 | tf_op jit(solution)/shard_map/ppermute | solution.py:18
  101.8 4.4 %collective-permute-start.7 = (bf16[64,1024]{1,0:T(8,128)(2,1)S(1)}, bf16[64,1024]{1,0:T(8,128)(2,1)S(1)}, u32[]{:S(2)}, u32[]{:S(2)}) collective-permute-start(bf16[64,1024]{1,0:T(8,128)(2,1)S(1)} %get-tuple-element.10), channel_id=1, source_target_pairs={{1,0},{2,1},{3,2},{4,3},{5,4},{6,5},{7,6},{8,7},{9,8},{10,9},{11,1... | collective-permute-start | bytes 393224 | tf_op jit(solution)/shard_map/ppermute | solution.py:20
  106.2 0.5 collective-permute-done.6
  106.7 1.2 collective-permute-done.7
  107.9 0.2 copy_bitcast_fusion.1
  108.1 13.3 %gather_fusion.3 = bf16[320,64,128]{2,1,0:T(8,128)(2,1)} fusion(bf16[64,48,128]{2,0,1:T(8,128)(2,1)S(1)} %copy_bitcast_fusion.1, s32[1024]{0:T(1024)S(1)} %pad_clamp_fusion), kind=kCustom, calls=%fused_computation.3.clone | custom fusion | bytes 10487040 | tf_op jit(solution)/shard_map/jit(_take)/gather | solution.py:32
  121.5 7.5 %fusion.31 = f32[32,8,8,128]{3,2,1,0:T(8,128)S(1)} fusion(bf16[32,10,128,128]{3,2,1,0:T(8,128)(2,1)} %param.7, bf16[32,10,64,128]{3,2,1,0:T(8,128)(2,1)} %bitcast.171, pred[32,10]{1,0:T(8,128)(4,1)S(1)} %copy.33, bf16[32,10]{1,0:T(8,128)(2,1)S(1)} %fusion.53), kind=kOutput, calls=%fused_computation.42 | convolution fusion | flops 676593664 | bytes 16778176 | tf_op jit(solution)/shard_map/krsj,rsij->kri/dot_general | solution.py:35
  129.0 0.1 fusion.40
  129.1 3.2 %collective-permute-start.8 = (bf16[64,1024]{1,0:T(8,128)(2,1)S(1)}, bf16[64,1024]{1,0:T(8,128)(2,1)S(1)}, u32[]{:S(2)}, u32[]{:S(2)}) collective-permute-start(bf16[64,1024]{1,0:T(8,128)(2,1)S(1)} %get-tuple-element.7), channel_id=1, source_target_pairs={{0,1},{1,2},{2,3},{3,4},{4,5},{5,6},{6,7},{7,8},{8,9},{9,10},{10,1... | collective-permute-start | bytes 393224 | tf_op jit(solution)/shard_map/ppermute | solution.py:18
  132.4 4.2 %collective-permute-start.9 = (bf16[64,1024]{1,0:T(8,128)(2,1)S(1)}, bf16[64,1024]{1,0:T(8,128)(2,1)S(1)}, u32[]{:S(2)}, u32[]{:S(2)}) collective-permute-start(bf16[64,1024]{1,0:T(8,128)(2,1)S(1)} %get-tuple-element.8), channel_id=1, source_target_pairs={{1,0},{2,1},{3,2},{4,3},{5,4},{6,5},{7,6},{8,7},{9,8},{10,9},{11,1... | collective-permute-start | bytes 393224 | tf_op jit(solution)/shard_map/ppermute | solution.py:20
  136.6 0.3 fusion.65
  136.9 0.4 collective-permute-done.8
  137.3 1.2 collective-permute-done.9
  138.5 0.2 copy_bitcast_fusion
  138.8 13.3 %gather_fusion.4 = bf16[320,64,128]{2,1,0:T(8,128)(2,1)} fusion(bf16[64,48,128]{2,0,1:T(8,128)(2,1)S(1)} %copy_bitcast_fusion, s32[1024]{0:T(1024)S(1)} %pad_clamp_fusion), kind=kCustom, calls=%fused_computation.4.clone | custom fusion | bytes 10487040 | tf_op jit(solution)/shard_map/jit(_take)/gather | solution.py:32
  152.1 8.0 %fusion.39 = bf16[32,8,8,128]{3,2,1,0:T(8,128)(2,1)S(1)} fusion(bf16[32,10,128,128]{3,2,1,0:T(8,128)(2,1)} %param.7, bf16[32,10,64,128]{3,2,1,0:T(8,128)(2,1)} %bitcast.167, pred[32,10]{1,0:T(8,128)(4,1)S(1)} %copy.33, bf16[32,10]{1,0:T(8,128)(2,1)S(1)} %fusion.53), kind=kOutput, calls=%fused_computation.50 | convolution fusion | flops 676593664 | bytes 16253888 | tf_op jit(solution)/shard_map/krsj,rsij->kri/dot_general | solution.py:35
  160.1 0.3 fusion.43
  160.4 92.3 %all-reduce = (f32[64,64]{0,1:T(8,128)S(1)}, f32[64,64]{0,1:T(8,128)S(1)}) all-reduce(f32[64,64]{0,1:T(8,128)S(1)} %fusion.65, f32[64,64]{0,1:T(8,128)S(1)} %fusion.43), channel_id=1, replica_groups=mesh['dom'=32,'board'=8] {'dom','board'}, use_global_device_ids=true, to_apply=%region_0.2 | all-reduce | flops 8192 | bytes 65536 | tf_op jit(solution)/shard_map/psum | solution.py:58
  252.7 0.1 copy.50
  252.7 5.8 %cholesky.17 = f32[64,64]{1,0:T(8,128)S(1)} custom-call(f32[64,64]{1,0:T(8,128)S(1)} %fusion.49), custom_call_target="Cholesky" | custom-call | tf_op jit(solution)/shard_map/jit(cholesky)/cholesky | solution.py:64
  258.6 0.6 compare_reduce_fusion
  259.3 0.7 fusion.46
  259.9 4.9 %custom-call.7 = f32[1,64,64]{1,2,0:T(8,128)S(1)} custom-call(f32[1,64,64]{2,1,0:T(8,128)S(1)} %fusion.46), custom_call_target="InvertDiagBlocksLowerTriangular" | custom-call | tf_op jit(solution)/shard_map/jit(_solve_triangular)/triangular_solve | solution.py:66
  264.8 0.2 fusion.47
  265.1 1.3 convolution_convert_fusion
  266.4 0.2 fusion.50
  266.6 0.8 fusion.66
  (8 shorter events, 0.1 us)
Async XLA Ops:
  1.6 12.6 %collective-permute-start = (bf16[64,1024]{1,0:T(8,128)(2,1)S(1)}, bf16[64,1024]{1,0:T(8,128)(2,1)S(1)}, u32[]{:S(2)}, u32[]{:S(2)}) collective-permute-start(bf16[64,1024]{1,0:T(8,128)(2,1)S(1)} %get-tuple-element.15), channel_id=1, source_target_pairs={{0,1},{1,2},{2,3},{3,4},{4,5},{5,6},{6,7},{7,8},{8,9},{9,10},{10,1... | collective-permute-start | bytes 393224 | tf_op jit(solution)/shard_map/ppermute | solution.py:18
  6.0 8.4 %collective-permute-start.1 = (bf16[64,1024]{1,0:T(8,128)(2,1)S(1)}, bf16[64,1024]{1,0:T(8,128)(2,1)S(1)}, u32[]{:S(2)}, u32[]{:S(2)}) collective-permute-start(bf16[64,1024]{1,0:T(8,128)(2,1)S(1)} %get-tuple-element.16), channel_id=1, source_target_pairs={{1,0},{2,1},{3,2},{4,3},{5,4},{6,5},{7,6},{8,7},{9,8},{10,9},{11,1... | collective-permute-start | bytes 393224 | tf_op jit(solution)/shard_map/ppermute | solution.py:20
  37.1 8.2 %collective-permute-start.2 = (bf16[64,1024]{1,0:T(8,128)(2,1)S(1)}, bf16[64,1024]{1,0:T(8,128)(2,1)S(1)}, u32[]{:S(2)}, u32[]{:S(2)}) collective-permute-start(bf16[64,1024]{1,0:T(8,128)(2,1)S(1)} %get-tuple-element.13), channel_id=1, source_target_pairs={{0,1},{1,2},{2,3},{3,4},{4,5},{5,6},{6,7},{7,8},{8,9},{9,10},{10,1... | collective-permute-start | bytes 393224 | tf_op jit(solution)/shard_map/ppermute | solution.py:18
  39.0 7.5 %collective-permute-start.3 = (bf16[64,1024]{1,0:T(8,128)(2,1)S(1)}, bf16[64,1024]{1,0:T(8,128)(2,1)S(1)}, u32[]{:S(2)}, u32[]{:S(2)}) collective-permute-start(bf16[64,1024]{1,0:T(8,128)(2,1)S(1)} %get-tuple-element.14), channel_id=1, source_target_pairs={{1,0},{2,1},{3,2},{4,3},{5,4},{6,5},{7,6},{8,7},{9,8},{10,9},{11,1... | collective-permute-start | bytes 393224 | tf_op jit(solution)/shard_map/ppermute | solution.py:20
  60.1 7.6 %copy-start = (bf16[64,4096]{1,0:T(8,128)(2,1)S(1)}, bf16[64,4096]{1,0:T(8,128)(2,1)}, u32[]{:S(2)}) copy-start(bf16[64,4096]{1,0:T(8,128)(2,1)} %param.6) | copy-start | bytes 1572868
  67.8 8.2 %collective-permute-start.4 = (bf16[64,1024]{1,0:T(8,128)(2,1)S(1)}, bf16[64,1024]{1,0:T(8,128)(2,1)S(1)}, u32[]{:S(2)}, u32[]{:S(2)}) collective-permute-start(bf16[64,1024]{1,0:T(8,128)(2,1)S(1)} %get-tuple-element.11), channel_id=1, source_target_pairs={{0,1},{1,2},{2,3},{3,4},{4,5},{5,6},{6,7},{7,8},{8,9},{9,10},{10,1... | collective-permute-start | bytes 393224 | tf_op jit(solution)/shard_map/ppermute | solution.py:18
  71.1 6.1 %collective-permute-start.5 = (bf16[64,1024]{1,0:T(8,128)(2,1)S(1)}, bf16[64,1024]{1,0:T(8,128)(2,1)S(1)}, u32[]{:S(2)}, u32[]{:S(2)}) collective-permute-start(bf16[64,1024]{1,0:T(8,128)(2,1)S(1)} %get-tuple-element.12), channel_id=1, source_target_pairs={{1,0},{2,1},{3,2},{4,3},{5,4},{6,5},{7,6},{8,7},{9,8},{10,9},{11,1... | collective-permute-start | bytes 393224 | tf_op jit(solution)/shard_map/ppermute | solution.py:20
  98.4 8.2 %collective-permute-start.6 = (bf16[64,1024]{1,0:T(8,128)(2,1)S(1)}, bf16[64,1024]{1,0:T(8,128)(2,1)S(1)}, u32[]{:S(2)}, u32[]{:S(2)}) collective-permute-start(bf16[64,1024]{1,0:T(8,128)(2,1)S(1)} %get-tuple-element.9), channel_id=1, source_target_pairs={{0,1},{1,2},{2,3},{3,4},{4,5},{5,6},{6,7},{7,8},{8,9},{9,10},{10,1... | collective-permute-start | bytes 393224 | tf_op jit(solution)/shard_map/ppermute | solution.py:18
  101.8 6.1 %collective-permute-start.7 = (bf16[64,1024]{1,0:T(8,128)(2,1)S(1)}, bf16[64,1024]{1,0:T(8,128)(2,1)S(1)}, u32[]{:S(2)}, u32[]{:S(2)}) collective-permute-start(bf16[64,1024]{1,0:T(8,128)(2,1)S(1)} %get-tuple-element.10), channel_id=1, source_target_pairs={{1,0},{2,1},{3,2},{4,3},{5,4},{6,5},{7,6},{8,7},{9,8},{10,9},{11,1... | collective-permute-start | bytes 393224 | tf_op jit(solution)/shard_map/ppermute | solution.py:20
  129.1 8.2 %collective-permute-start.8 = (bf16[64,1024]{1,0:T(8,128)(2,1)S(1)}, bf16[64,1024]{1,0:T(8,128)(2,1)S(1)}, u32[]{:S(2)}, u32[]{:S(2)}) collective-permute-start(bf16[64,1024]{1,0:T(8,128)(2,1)S(1)} %get-tuple-element.7), channel_id=1, source_target_pairs={{0,1},{1,2},{2,3},{3,4},{4,5},{5,6},{6,7},{7,8},{8,9},{9,10},{10,1... | collective-permute-start | bytes 393224 | tf_op jit(solution)/shard_map/ppermute | solution.py:18
  132.4 6.2 %collective-permute-start.9 = (bf16[64,1024]{1,0:T(8,128)(2,1)S(1)}, bf16[64,1024]{1,0:T(8,128)(2,1)S(1)}, u32[]{:S(2)}, u32[]{:S(2)}) collective-permute-start(bf16[64,1024]{1,0:T(8,128)(2,1)S(1)} %get-tuple-element.8), channel_id=1, source_target_pairs={{1,0},{2,1},{3,2},{4,3},{5,4},{6,5},{7,6},{8,7},{9,8},{10,9},{11,1... | collective-permute-start | bytes 393224 | tf_op jit(solution)/shard_map/ppermute | solution.py:20
where the time goes:
time: 268 us; the launch traced here: 267 us
  blocking collectives  92.3 us (34%)
  local copies, waits for them, and re-layouts  68.3 us (25%)
  matrix products  41.7 us (16%)
  starting transfers between devices  41.1 us (15%)
  other arithmetic  15.9 us (6%)
  waiting for transfers between devices  7.18 us (3%)
    psum x1, blocking collectives, body(): gram = lax.psum(gram_local, ('dom', 'board'))  92.3 us
    gather x5, local copies, waits for them, and re-layouts, apply_rows(): picked = jnp.take(blocks, local, axis=1)  66.7 us
    dot_general x5, matrix products, apply_rows(): jnp.einsum('krsj,rsij->kri', picked, tiles, preferred_element_type=jnp.fl...  38.5 us
    ppermute x5, starting transfers between devices, extended(): lax.ppermute(head, axis, [((i + 1) % count, i) for i in range(ends)])  25 us
    ppermute x5, starting transfers between devices, extended(): lax.ppermute(tail, axis, [(i, (i + 1) % count) for i in range(ends)])  16.2 us
    another operation x3, other arithmetic, body(): factor = jnp.linalg.cholesky(gram)  6.52 us
    another operation x2, other arithmetic, body(): inverse = jax.scipy.linalg.solve_triangular(factor, identity, lower=True)  5.55 us
  transfers between devices with their start and end apart: 10, of which 9 were waited for; matrix products, arithmetic and copies ran while one was open for 1% of the time, Pallas kernels for 0%

commit v1 on v0

v1 whole, which is shorter than its diff:
```python
import functools

import jax
import jax.numpy as jnp
import numpy as np
from jax import lax
from jax.experimental import pallas as pl
from jax.experimental.pallas import tpu as pltpu
from jax.sharding import PartitionSpec as P

DEG = 4
GHOST = 8
TB = 128
AX = ("dom", "board")
MIB = 1 << 20
NT_DIMS = (((1,), (1,)), ((), ()))
UNROLL = 4

VM = pl.BlockSpec(memory_space=pltpu.VMEM)
SM = pl.BlockSpec(memory_space=pltpu.SMEM)
ANY = pl.BlockSpec(memory_space=pl.ANY)


def call(kernel, out_shape, in_specs, out_specs, scratch=(), limit=24, flops=0, bytes_=0):
    return pl.pallas_call(
        kernel,
        out_shape=out_shape,
        in_specs=in_specs,
        out_specs=out_specs,
        scratch_shapes=scratch,
        compiler_params=pltpu.CompilerParams(vmem_limit_bytes=limit * MIB),
        cost_estimate=pl.CostEstimate(flops=flops, bytes_accessed=bytes_, transcendentals=0),
    )


def pair_dot(src, tiles, row, pair, left, right):
    lhs = jnp.concatenate(
        [src[:, pl.ds(pl.multiple_of(left, TB), TB)], src[:, pl.ds(pl.multiple_of(right, TB), TB)]], axis=1
    )
    rhs = jnp.concatenate([tiles[row, 2 * pair], tiles[row, 2 * pair + 1]], axis=1)
    return lax.dot_general(lhs, rhs, NT_DIMS, preferred_element_type=jnp.float32)


def row_sum(src, tiles, tab, row):
    total = None
    for pair in range(5):
        term = pair_dot(src, tiles, row, pair, tab[row, 2 * pair], tab[row, 2 * pair + 1])
        total = term if total is None else total + term
    return total


def own_products(src, tiles, tab, acc):
    rows = tiles.shape[0]

    def step(g, carry):
        for u in range(UNROLL):
            row = g * UNROLL + u
            acc[:, pl.ds(pl.multiple_of(row * TB, TB), TB)] = row_sum(src, tiles, tab, row)
        return carry

    lax.fori_loop(0, rows // UNROLL, step, 0)


def load_kernel(block, tiles_hbm, tab, tiles, acc, src, sems):
    rows = tiles.shape[0]
    parts = sems.shape[0]
    each = rows // parts
    copies = [
        pltpu.make_async_copy(tiles_hbm.at[pl.ds(p * each, each)], tiles.at[pl.ds(p * each, each)], sems.at[p])
        for p in range(parts)
    ]
    for c in copies:
        c.start()
    wide = block.shape[1]
    src[:, :wide] = block[...]
    src[:, wide:] = jnp.zeros_like(src[:, wide:])
    for c in copies:
        c.wait()
    own_products(src, tiles, tab, acc)


def own_kernel(src, tiles, tab, acc):
    own_products(src, tiles, tab, acc)


def halo_products(acc, older, r0, r1, tiles, tab, par, out, halo):
    rows = tiles.shape[0]
    edge = GHOST * TB
    odd = par[0]

    @pl.when(odd == 1)
    def _():
        halo[:, :edge] = r0[...]
        halo[:, edge : 2 * edge] = r1[...]

    @pl.when(odd == 0)
    def _():
        halo[:, :edge] = r1[...]
        halo[:, edge : 2 * edge] = r0[...]

    halo[:, 2 * edge :] = jnp.zeros_like(halo[:, 2 * edge :])

    def finish(row, value):
        at = pl.ds(pl.multiple_of(row * TB, TB), TB)
        if older is not None:
            value = 2.0 * value - older[:, at].astype(jnp.float32)
        out[:, at] = value.astype(jnp.bfloat16)

    def step(g, carry):
        for u in range(UNROLL):
            k = g * UNROLL + u
            row = jnp.where(k < GHOST, k, k + rows - 2 * GHOST)
            at = pl.ds(pl.multiple_of(row * TB, TB), TB)
            finish(row, acc[:, at] + row_sum(halo, tiles, tab, row))
        return carry

    lax.fori_loop(0, 2 * GHOST // UNROLL, step, 0)
    for row in range(GHOST, rows - GHOST):
        finish(row, acc[:, row * TB : (row + 1) * TB])


def halo_kernel(acc, older, r0, r1, tiles, tab, par, out, s0, s1, halo, *, cheb):
    wide = tiles.shape[0] * TB
    edge = GHOST * TB
    odd = par[0]
    halo_products(acc, older if cheb else None, r0, r1, tiles, tab, par, out, halo)
    out[:, wide:] = jnp.zeros_like(out[:, wide:])

    @pl.when(odd == 1)
    def _():
        s0[...] = out[:, :edge]
        s1[...] = out[:, wide - edge : wide]

    @pl.when(odd == 0)
    def _():
        s0[...] = out[:, wide - edge : wide]
        s1[...] = out[:, :edge]


def last_kernel(acc, y, r0, r1, tiles, tab, par, both, halo, image):
    wide = image.shape[1]
    halo_products(acc, None, r0, r1, tiles, tab, par, image, halo)
    values = jnp.concatenate([y[:, :wide], image[...]], axis=0)
    both[...] = lax.dot_general(y[:, :wide], values, NT_DIMS, preferred_element_type=jnp.float32)


def eliminate(gram):
    size = gram.shape[0]
    lanes = lax.broadcasted_iota(jnp.int32, (size, 2 * size), 1)
    sublanes = lax.broadcasted_iota(jnp.int32, (size, 2 * size), 0)
    work = jnp.concatenate([gram, jnp.zeros_like(gram)], axis=1)
    work = jnp.where(lanes == sublanes + size, 1.0, work)
    for k in range(size):
        row = work[k : k + 1, :]
        pivot = work[k : k + 1, k : k + 1]
        scaled = row * lax.rsqrt(pivot)
        factor = work[:, k : k + 1] / pivot
        rest = work - factor * row
        work = jnp.where(sublanes == k, scaled, jnp.where(sublanes > k, rest, work))
    return work[:, size:]


def split3(x):
    hi = x.astype(jnp.bfloat16)
    rest = x - hi.astype(jnp.float32)
    mid = rest.astype(jnp.bfloat16)
    low = (rest - mid.astype(jnp.float32)).astype(jnp.bfloat16)
    return hi, mid, low


def end_kernel(both, y, basis, projected, *, nodes_all):
    size = both.shape[0]
    values = both[...] / nodes_all
    inverse = eliminate(values[:, :size])
    cross = values[:, size:]
    half = jnp.dot(inverse, cross, precision=lax.Precision.HIGHEST, preferred_element_type=jnp.float32)
    projected[...] = lax.dot_general(
        half, inverse, NT_DIMS, precision=lax.Precision.HIGHEST, preferred_element_type=jnp.float32
    )
    parts = jnp.concatenate(split3(inverse), axis=0)
    chunk = 512

    def step(c, carry):
        at = pl.ds(pl.multiple_of(c * chunk, chunk), chunk)
        out = jnp.dot(parts, y[:, at], preferred_element_type=jnp.float32)
        basis[:, at] = (out[:size] + (out[size : 2 * size] + out[2 * size :])).astype(jnp.bfloat16)
        return carry

    lax.fori_loop(0, basis.shape[1] // chunk, step, 0)


def rotations(shape, axis):
    at = np.arange(int(np.prod(shape))).reshape(shape)
    return [
        list(zip(at.reshape(-1).tolist(), np.roll(at, -k, axis=axis).reshape(-1).tolist()))
        for k in range(1, shape[axis])
    ]


def all_sum(x, dom, board):
    shape = (dom // 8, 4, 2, board) if dom % 8 == 0 else (dom, 1, 1, board)
    for axis in (2, 1, 0, 3):
        pieces = [lax.ppermute(x, AX, perm) for perm in rotations(shape, axis)]
        for piece in pieces:
            x = x + piece
    return x


def body(block, tiles, cols, counts, *, dom, board):
    devices = dom * board
    size, wide = block.shape
    rows, slots = cols.shape
    edge = GHOST * TB
    padded = wide + TB
    bf16, f32 = jnp.bfloat16, jnp.float32
    shape = jax.ShapeDtypeStruct
    me = lax.axis_index(AX)
    first = me * rows
    odd = me % 2
    par = odd.reshape(1).astype(jnp.int32)

    even_pairs = [(i, i ^ 1) for i in range(devices)]
    odd_pairs = [(0, 0), (devices - 1, devices - 1)] + [(i, ((i + 1) ^ 1) - 1) for i in range(1, devices - 1)]

    def exchange(s0, s1):
        r1 = lax.ppermute(s1, AX, odd_pairs)
        r0 = lax.ppermute(s0, AX, even_pairs)
        return r0, r1

    live = lax.broadcasted_iota(jnp.int32, cols.shape, 1) < counts[:, None]
    near = cols - first
    inside = (near >= 0) & (near < rows)
    tab_own = jnp.where(live & inside, near, rows) * TB
    beyond = jnp.where(near < 0, near + GHOST, near - rows + GHOST)
    tab_halo = jnp.where(live & ~inside, beyond, 2 * GHOST) * TB

    head, tail = block[:, :edge], block[:, wide - edge :]
    r0, r1 = exchange(jnp.where(odd == 1, head, tail), jnp.where(odd == 1, tail, head))

    pair_flops = 2 * size * TB * TB
    own_flops = rows * slots * pair_flops
    halo_flops = own_flops // 2
    tile_bytes = tiles.size * 2
    acc_shape = shape((size, wide), f32)
    y_shape = shape((size, padded), bf16)
    edge_shape = shape((size, edge), bf16)
    halo_scratch = pltpu.VMEM((size, 2 * edge + TB), bf16)

    tiles_v, acc = call(
        load_kernel,
        [pltpu.VMEM(tiles.shape, bf16), acc_shape],
        [VM, ANY, SM],
        [VM, VM],
        [pltpu.VMEM((size, padded), bf16), pltpu.SemaphoreType.DMA((4,))],
        flops=own_flops,
        bytes_=tile_bytes,
    )(block, tiles, tab_own)

    older, y = block, block
    for degree in range(DEG):
        new, s0, s1 = call(
            functools.partial(halo_kernel, cheb=degree > 0),
            [y_shape, edge_shape, edge_shape],
            [VM, VM, VM, VM, VM, SM, SM],
            [VM, VM, VM],
            [halo_scratch],
            flops=halo_flops,
        )(acc, older, r0, r1, tiles_v, tab_halo, par)
        older, y = y, new
        r0, r1 = exchange(s0, s1)
        acc = call(own_kernel, acc_shape, [VM, VM, SM], VM, flops=own_flops)(y, tiles_v, tab_own)

    both = call(
        last_kernel,
        shape((size, 2 * size), f32),
        [VM, VM, VM, VM, VM, SM, SM],
        VM,
        [halo_scratch, pltpu.VMEM((size, wide), bf16)],
        flops=halo_flops,
    )(acc, y, r0, r1, tiles_v, tab_halo, par)
    both = all_sum(both, dom, board)
    basis, projected = call(
        functools.partial(end_kernel, nodes_all=devices * rows * TB),
        [shape((size, wide), bf16), shape((size, size), f32)],
        [VM, VM],
        [VM, VM],
        flops=6 * size * size * wide,
    )(both, y)
    return basis, projected


def solution(mesh):
    dom, board = mesh.shape["dom"], mesh.shape["board"]
    return jax.shard_map(
        functools.partial(body, dom=dom, board=board),
        mesh=mesh,
        in_specs=(
            P(None, AX),
            P(AX, None, None, None),
            P(AX, None),
            P(AX),
        ),
        out_specs=(P(None, AX), P()),
        check_vma=False,
    )
```

time: 268 us -> 127 us (0.47)
  the two profiles are of different devices: /device:TPU:1 before, /device:TPU:32 now
where the time goes in v1:
time: 127 us; the launch traced here: 126 us
  Pallas kernels  52.4 us (41%)
  starting transfers between devices  50.6 us (40%)
  waiting for transfers between devices  14.8 us (12%)
  local copies, waits for them, and re-layouts  5.82 us (5%)
  other arithmetic  1.77 us (1%)
    ppermute x14, starting transfers between devices, all_sum(): pieces = [lax.ppermute(x, AX, perm) for perm in rotations(shape, axis)]  26.2 us
    ppermute x5, starting transfers between devices, exchange(): r1 = lax.ppermute(s1, AX, odd_pairs)  21.9 us
    pallas_call x4, Pallas kernels, body(): call(own_kernel, acc_shape, [VM, VM, SM], VM, flops=own_flops)  21.4 us
    ppermute x14, waiting for transfers between devices, all_sum(): pieces = [lax.ppermute(x, AX, perm) for perm in rotations(shape, axis)]  14.8 us
    pallas_call x4, Pallas kernels, body(): call(functools.partial(halo_kernel, cheb=degree > 0), [y_shape, edge_shap...  12.8 us
    pallas_call x1, Pallas kernels, body(): call(functools.partial(end_kernel, nodes_all=devices * rows * TB), [shape...  8.52 us
    pallas_call x1, Pallas kernels, body(): call(load_kernel, [pltpu.VMEM(tiles.shape, bf16), acc_shape], [VM, ANY, S...  6.12 us
    unnamed x7, local copies, waits for them, and re-layouts  5.82 us
  transfers between devices with their start and end apart: 24, of which 8 were waited for; matrix products, arithmetic and copies ran while one was open for 1% of the time, Pallas kernels for 22%

profile of v1, /device:TPU:32, one launch (start us, length us, event | category | flops | bytes accessed | tf_op | source)
XLA Modules:
  0.0 126.4 jit_solution(12814783159157710252)
XLA Ops:
  0.6 1.0 broadcast_select_fusion
  1.6 3.8 %collective-permute-start.1 = (bf16[64,1024]{1,0:T(8,128)(2,1)S(1)}, bf16[64,1024]{1,0:T(8,128)(2,1)S(1)}, u32[]{:S(2)}, u32[]{:S(2)}) collective-permute-start(bf16[64,1024]{1,0:T(8,128)(2,1)S(1)} %get-tuple-element.30), channel_id=1, source_target_pairs={{0,0},{255,255},{1,2},{2,1},{3,4},{4,3},{5,6},{6,5},{7,8},{8,7},{9... | collective-permute-start | bytes 393224 | tf_op jit(solution)/shard_map/ppermute | solution.py:226
  5.5 0.1 collective-permute-start
  5.6 0.8 copy.6
  6.4 0.7 select_multiply_fusion
  7.1 4.0 %copy-done = bf16[32,10,128,128]{3,2,1,0:T(8,128)(2,1)S(1)} copy-done((bf16[32,10,128,128]{3,2,1,0:T(8,128)(2,1)S(1)}, bf16[32,10,128,128]{3,2,1,0:T(8,128)(2,1)}, u32[]{:S(2)}) %copy-start) | copy-done | bytes 10485784
  11.1 1.0 copy-done.1
  12.1 6.1 %shard_map.59 = (bf16[32,10,128,128]{3,2,1,0:T(8,128)(2,1)S(1)}, f32[64,4096]{1,0:T(8,128)S(1)}) custom-call(bf16[64,4096]{1,0:T(8,128)(2,1)S(1)} %copy-done.1, bf16[32,10,128,128]{3,2,1,0:T(8,128)(2,1)S(1)} %copy-done, s32[32,10]{1,0:T(8,128)S(1)} %get-tuple-element.33.tab), custom_call_target="tpu_custom_call" | custom-call | flops 671088640 | bytes 10485760 | tf_op jit(solution)/shard_map/pallas_call | solution.py:249
  18.3 0.0 collective-permute-done.1.r1
  18.3 0.0 collective-permute-done.r0
  18.3 0.0 copy-start.2
  18.3 3.2 %shard_map.60 = (bf16[64,4224]{1,0:T(8,128)(2,1)S(1)}, bf16[64,1024]{1,0:T(8,128)(2,1)S(1)}, bf16[64,1024]{1,0:T(8,128)(2,1)S(1)}) custom-call(f32[64,4096]{1,0:T(8,128)S(1)} %get-tuple-element.16.acc, bf16[64,4096]{1,0:T(8,128)(2,1)S(1)} %copy-done.1, bf16[64,1024]{1,0:T(8,128)(2,1)S(1)} %collective-permute-done.r0, ...), custom_call_target="tpu_custom_call" | custom-call | flops 335544320 | tf_op jit(solution)/shard_map/pallas_call | solution.py:261
  21.5 2.1 %collective-permute-start.2 = (bf16[64,1024]{1,0:T(8,128)(2,1)S(1)}, bf16[64,1024]{1,0:T(8,128)(2,1)S(1)}, u32[]{:S(2)}, u32[]{:S(2)}) collective-permute-start(bf16[64,1024]{1,0:T(8,128)(2,1)S(1)} %get-tuple-element.19), channel_id=1, source_target_pairs={{0,1},{1,0},{2,3},{3,2},{4,5},{5,4},{6,7},{7,6},{8,9},{9,8},{10,11... | collective-permute-start | bytes 393224 | tf_op jit(solution)/shard_map/ppermute | solution.py:227
  23.5 5.0 %collective-permute-start.3 = (bf16[64,1024]{1,0:T(8,128)(2,1)S(1)}, bf16[64,1024]{1,0:T(8,128)(2,1)S(1)}, u32[]{:S(2)}, u32[]{:S(2)}) collective-permute-start(bf16[64,1024]{1,0:T(8,128)(2,1)S(1)} %get-tuple-element.20), channel_id=1, source_target_pairs={{0,0},{255,255},{1,2},{2,1},{3,4},{4,3},{5,6},{6,5},{7,8},{8,7},{9... | collective-permute-start | bytes 393224 | tf_op jit(solution)/shard_map/ppermute | solution.py:226
  28.5 5.3 %shard_map.61.acc = f32[64,4096]{1,0:T(8,128)S(1)} custom-call(bf16[64,4224]{1,0:T(8,128)(2,1)S(1)} %get-tuple-element.18.src.older, bf16[32,10,128,128]{3,2,1,0:T(8,128)(2,1)S(1)} %get-tuple-element.17.tiles, s32[32,10]{1,0:T(8,128)S(1)} %get-tuple-element.33.tab), custom_call_target="tpu_custom_call" | custom-call | flops 671088640 | tf_op jit(solution)/shard_map/pallas_call | solution.py:271
  33.9 0.0 collective-permute-done.2.r0
  33.9 0.0 collective-permute-done.3.r1
  33.9 3.2 %shard_map.62 = (bf16[64,4224]{1,0:T(8,128)(2,1)S(1)}, bf16[64,1024]{1,0:T(8,128)(2,1)S(1)}, bf16[64,1024]{1,0:T(8,128)(2,1)S(1)}) custom-call(f32[64,4096]{1,0:T(8,128)S(1)} %shard_map.61.acc, bf16[64,4096]{1,0:T(8,128)(2,1)S(1)} %copy-done.2, bf16[64,1024]{1,0:T(8,128)(2,1)S(1)} %collective-permute-done.2.r0, ...), custom_call_target="tpu_custom_call" | custom-call | flops 335544320 | tf_op jit(solution)/shard_map/pallas_call | solution.py:261
  37.1 0.1 collective-permute-start.4
  37.2 4.6 %collective-permute-start.5 = (bf16[64,1024]{1,0:T(8,128)(2,1)S(1)}, bf16[64,1024]{1,0:T(8,128)(2,1)S(1)}, u32[]{:S(2)}, u32[]{:S(2)}) collective-permute-start(bf16[64,1024]{1,0:T(8,128)(2,1)S(1)} %get-tuple-element.23), channel_id=1, source_target_pairs={{0,0},{255,255},{1,2},{2,1},{3,4},{4,3},{5,6},{6,5},{7,8},{8,7},{9... | collective-permute-start | bytes 393224 | tf_op jit(solution)/shard_map/ppermute | solution.py:226
  41.8 5.3 %shard_map.63.acc = f32[64,4096]{1,0:T(8,128)S(1)} custom-call(bf16[64,4224]{1,0:T(8,128)(2,1)S(1)} %get-tuple-element.21.src.older, bf16[32,10,128,128]{3,2,1,0:T(8,128)(2,1)S(1)} %get-tuple-element.17.tiles, s32[32,10]{1,0:T(8,128)S(1)} %get-tuple-element.33.tab), custom_call_target="tpu_custom_call" | custom-call | flops 671088640 | tf_op jit(solution)/shard_map/pallas_call | solution.py:271
  47.2 0.0 collective-permute-done.4.r0
  47.2 0.0 collective-permute-done.5.r1
  47.2 3.2 %shard_map.64 = (bf16[64,4224]{1,0:T(8,128)(2,1)S(1)}, bf16[64,1024]{1,0:T(8,128)(2,1)S(1)}, bf16[64,1024]{1,0:T(8,128)(2,1)S(1)}) custom-call(f32[64,4096]{1,0:T(8,128)S(1)} %shard_map.63.acc, bf16[64,4224]{1,0:T(8,128)(2,1)S(1)} %get-tuple-element.18.src.older, bf16[64,1024]{1,0:T(8,128)(2,1)S(1)} %collective-permute-done.4.r0, ...), custom_call_target="tpu_custom_call" | custom-call | flops 335544320 | tf_op jit(solution)/shard_map/pallas_call | solution.py:261
  50.4 0.1 collective-permute-start.6
  50.5 4.4 %collective-permute-start.7 = (bf16[64,1024]{1,0:T(8,128)(2,1)S(1)}, bf16[64,1024]{1,0:T(8,128)(2,1)S(1)}, u32[]{:S(2)}, u32[]{:S(2)}) collective-permute-start(bf16[64,1024]{1,0:T(8,128)(2,1)S(1)} %get-tuple-element.26), channel_id=1, source_target_pairs={{0,0},{255,255},{1,2},{2,1},{3,4},{4,3},{5,6},{6,5},{7,8},{8,7},{9... | collective-permute-start | bytes 393224 | tf_op jit(solution)/shard_map/ppermute | solution.py:226
  54.9 5.3 %shard_map.65.acc = f32[64,4096]{1,0:T(8,128)S(1)} custom-call(bf16[64,4224]{1,0:T(8,128)(2,1)S(1)} %get-tuple-element.24.src, bf16[32,10,128,128]{3,2,1,0:T(8,128)(2,1)S(1)} %get-tuple-element.17.tiles, s32[32,10]{1,0:T(8,128)S(1)} %get-tuple-element.33.tab), custom_call_target="tpu_custom_call" | custom-call | flops 671088640 | tf_op jit(solution)/shard_map/pallas_call | solution.py:271
  60.3 0.0 collective-permute-done.6.r0
  60.3 0.0 collective-permute-done.7.r1
  60.3 3.2 %shard_map.66 = (bf16[64,4224]{1,0:T(8,128)(2,1)S(1)}, bf16[64,1024]{1,0:T(8,128)(2,1)S(1)}, bf16[64,1024]{1,0:T(8,128)(2,1)S(1)}) custom-call(f32[64,4096]{1,0:T(8,128)S(1)} %shard_map.65.acc, bf16[64,4224]{1,0:T(8,128)(2,1)S(1)} %get-tuple-element.21.src.older, bf16[64,1024]{1,0:T(8,128)(2,1)S(1)} %collective-permute-done.6.r0, ...), custom_call_target="tpu_custom_call" | custom-call | flops 335544320 | tf_op jit(solution)/shard_map/pallas_call | solution.py:261
  63.5 0.1 collective-permute-start.8
  63.6 4.1 %collective-permute-start.9 = (bf16[64,1024]{1,0:T(8,128)(2,1)S(1)}, bf16[64,1024]{1,0:T(8,128)(2,1)S(1)}, u32[]{:S(2)}, u32[]{:S(2)}) collective-permute-start(bf16[64,1024]{1,0:T(8,128)(2,1)S(1)} %get-tuple-element.29), channel_id=1, source_target_pairs={{0,0},{255,255},{1,2},{2,1},{3,4},{4,3},{5,6},{6,5},{7,8},{8,7},{9... | collective-permute-start | bytes 393224 | tf_op jit(solution)/shard_map/ppermute | solution.py:226
  67.7 5.3 %shard_map.67.acc = f32[64,4096]{1,0:T(8,128)S(1)} custom-call(bf16[64,4224]{1,0:T(8,128)(2,1)S(1)} %get-tuple-element.27.src.y, bf16[32,10,128,128]{3,2,1,0:T(8,128)(2,1)S(1)} %get-tuple-element.17.tiles, s32[32,10]{1,0:T(8,128)S(1)} %get-tuple-element.33.tab), custom_call_target="tpu_custom_call" | custom-call | flops 671088640 | tf_op jit(solution)/shard_map/pallas_call | solution.py:271
  73.1 0.0 collective-permute-done.8.r0
  73.1 0.0 collective-permute-done.9.r1
  73.1 3.6 %shard_map.68 = f32[64,128]{1,0:T(8,128)S(1)} custom-call(f32[64,4096]{1,0:T(8,128)S(1)} %shard_map.67.acc, bf16[64,4224]{1,0:T(8,128)(2,1)S(1)} %get-tuple-element.27.src.y, bf16[64,1024]{1,0:T(8,128)(2,1)S(1)} %collective-permute-done.8.r0, bf16[64,1024]{1,0:T(8,128)(2,1)S(1)} %collective-permute-done.9.r1, ...), custom_call_target="tpu_custom_call" | custom-call | flops 335544320 | tf_op jit(solution)/shard_map/pallas_call | solution.py:273
  76.7 0.1 collective-permute-start.10
  76.8 1.2 collective-permute-done.10
  78.0 4.3 %collective-permute-start.13 = (f32[64,128]{1,0:T(8,128)S(1)}, f32[64,128]{1,0:T(8,128)S(1)}, u32[]{:S(2)}, u32[]{:S(2)}) collective-permute-start(f32[64,128]{1,0:T(8,128)S(1)} %add.65), channel_id=1, source_target_pairs={{0,48},{1,49},{2,50},{3,51},{4,52},{5,53},{6,54},{7,55},{8,56},{9,... | collective-permute-start | bytes 98312 | tf_op jit(solution)/shard_map/ppermute | solution.py:203
  82.4 0.9 collective-permute-start.11
  83.3 0.6 collective-permute-done.13
  84.0 3.9 %collective-permute-done.12 = f32[64,128]{1,0:T(8,128)S(1)} collective-permute-done((f32[64,128]{1,0:T(8,128)S(1)}, f32[64,128]{1,0:T(8,128)S(1)}, u32[]{:S(2)}, u32[]{:S(2)}) %collective-permute-start.12) | collective-permute-done | bytes 32800 | tf_op jit(solution)/shard_map/ppermute | solution.py:203
  87.8 0.0 collective-permute-done.11
  87.9 5.0 %collective-permute-start.16 = (f32[64,128]{1,0:T(8,128)S(1)}, f32[64,128]{1,0:T(8,128)S(1)}, u32[]{:S(2)}, u32[]{:S(2)}) collective-permute-start(f32[64,128]{1,0:T(8,128)S(1)} %add_add_fusion.2), channel_id=1, source_target_pairs={{0,192},{1,193},{2,194},{3,195},{4,196},{5,197},{6,198},{7,199},{8... | collective-permute-start | bytes 98312 | tf_op jit(solution)/shard_map/ppermute | solution.py:203
  92.9 0.5 collective-permute-start.15
  93.4 0.9 collective-permute-start.14
  94.2 0.2 collective-permute-done.16
  94.5 3.8 %collective-permute-done.15 = f32[64,128]{1,0:T(8,128)S(1)} collective-permute-done((f32[64,128]{1,0:T(8,128)S(1)}, f32[64,128]{1,0:T(8,128)S(1)}, u32[]{:S(2)}, u32[]{:S(2)}) %collective-permute-start.15) | collective-permute-done | bytes 32800 | tf_op jit(solution)/shard_map/ppermute | solution.py:203
  98.3 0.3 collective-permute-done.14
  98.7 3.5 %collective-permute-start.23 = (f32[64,128]{1,0:T(8,128)S(1)}, f32[64,128]{1,0:T(8,128)S(1)}, u32[]{:S(2)}, u32[]{:S(2)}) collective-permute-start(f32[64,128]{1,0:T(8,128)S(1)} %add_add_fusion.1), channel_id=1, source_target_pairs={{0,7},{1,0},{2,1},{3,2},{4,3},{5,4},{6,5},{7,6},{8,15},{9,8},{10,9... | collective-permute-start | bytes 98312 | tf_op jit(solution)/shard_map/ppermute | solution.py:203
  102.1 1.7 %collective-permute-start.22 = (f32[64,128]{1,0:T(8,128)S(1)}, f32[64,128]{1,0:T(8,128)S(1)}, u32[]{:S(2)}, u32[]{:S(2)}) collective-permute-start(f32[64,128]{1,0:T(8,128)S(1)} %add_add_fusion.1), channel_id=1, source_target_pairs={{0,6},{1,7},{2,0},{3,1},{4,2},{5,3},{6,4},{7,5},{8,14},{9,15},{10,... | collective-permute-start | bytes 98312 | tf_op jit(solution)/shard_map/ppermute | solution.py:203
  103.8 0.5 collective-permute-start.21
  104.3 5.9 %collective-permute-start.20 = (f32[64,128]{1,0:T(8,128)S(1)}, f32[64,128]{1,0:T(8,128)S(1)}, u32[]{:S(2)}, u32[]{:S(2)}) collective-permute-start(f32[64,128]{1,0:T(8,128)S(1)} %add_add_fusion.1), channel_id=1, source_target_pairs={{0,4},{1,5},{2,6},{3,7},{4,0},{5,1},{6,2},{7,3},{8,12},{9,13},{10,... | collective-permute-start | bytes 98312 | tf_op jit(solution)/shard_map/ppermute | solution.py:203
  110.2 0.8 collective-permute-start.19
  111.0 0.0 collective-permute-done.23
  111.0 0.7 collective-permute-start.18
  111.7 0.0 collective-permute-done.22
  111.7 1.5 %collective-permute-start.17 = (f32[64,128]{1,0:T(8,128)S(1)}, f32[64,128]{1,0:T(8,128)S(1)}, u32[]{:S(2)}, u32[]{:S(2)}) collective-permute-start(f32[64,128]{1,0:T(8,128)S(1)} %add_add_fusion.1), channel_id=1, source_target_pairs={{0,1},{1,2},{2,3},{3,4},{4,5},{5,6},{6,7},{7,0},{8,9},{9,10},{10,1... | collective-permute-start | bytes 98312 | tf_op jit(solution)/shard_map/ppermute | solution.py:203
  113.2 0.0 collective-permute-done.21
  113.2 0.0 collective-permute-done.20
  113.2 4.1 %collective-permute-done.19 = f32[64,128]{1,0:T(8,128)S(1)} collective-permute-done((f32[64,128]{1,0:T(8,128)S(1)}, f32[64,128]{1,0:T(8,128)S(1)}, u32[]{:S(2)}, u32[]{:S(2)}) %collective-permute-start.19) | collective-permute-done | bytes 32800 | tf_op jit(solution)/shard_map/ppermute | solution.py:203
  117.3 0.6 collective-permute-done.18
  117.8 0.0 collective-permute-done.17
  117.9 8.5 %shard_map.69 = (bf16[64,4096]{1,0:T(8,128)(2,1)}, f32[64,64]{1,0:T(8,128)}) custom-call(f32[64,128]{1,0:T(8,128)S(1)} %add_add_fusion.both, bf16[64,4224]{1,0:T(8,128)(2,1)S(1)} %get-tuple-element.27.src.y), custom_call_target="tpu_custom_call" | custom-call | flops 100663296 | tf_op jit(solution)/shard_map/pallas_call | solution.py:282
  (8 shorter events, 0.1 us)
Async XLA Ops:
  1.6 16.6 %collective-permute-start.1 = (bf16[64,1024]{1,0:T(8,128)(2,1)S(1)}, bf16[64,1024]{1,0:T(8,128)(2,1)S(1)}, u32[]{:S(2)}, u32[]{:S(2)}) collective-permute-start(bf16[64,1024]{1,0:T(8,128)(2,1)S(1)} %get-tuple-element.30), channel_id=1, source_target_pairs={{0,0},{255,255},{1,2},{2,1},{3,4},{4,3},{5,6},{6,5},{7,8},{8,7},{9... | collective-permute-start | bytes 393224 | tf_op jit(solution)/shard_map/ppermute | solution.py:226
  5.5 12.8 %collective-permute-start = (bf16[64,1024]{1,0:T(8,128)(2,1)S(1)}, bf16[64,1024]{1,0:T(8,128)(2,1)S(1)}, u32[]{:S(2)}, u32[]{:S(2)}) collective-permute-start(bf16[64,1024]{1,0:T(8,128)(2,1)S(1)} %get-tuple-element.31), channel_id=1, source_target_pairs={{0,1},{1,0},{2,3},{3,2},{4,5},{5,4},{6,7},{7,6},{8,9},{9,8},{10,11... | collective-permute-start | bytes 393224 | tf_op jit(solution)/shard_map/ppermute | solution.py:227
  7.1 4.0 %copy-start = (bf16[32,10,128,128]{3,2,1,0:T(8,128)(2,1)S(1)}, bf16[32,10,128,128]{3,2,1,0:T(8,128)(2,1)}, u32[]{:S(2)}) copy-start(bf16[32,10,128,128]{3,2,1,0:T(8,128)(2,1)} %tiles_hbm.1) | copy-start | bytes 31457284
  11.1 1.0 copy-start.1
  18.3 15.6 %copy-start.2 = (bf16[64,4096]{1,0:T(8,128)(2,1)S(1)}, bf16[64,4096]{1,0:T(8,128)(2,1)}, u32[]{:S(2)}) copy-start(bf16[64,4096]{1,0:T(8,128)(2,1)} %older.3) | copy-start | bytes 1572868
  21.5 12.4 %collective-permute-start.2 = (bf16[64,1024]{1,0:T(8,128)(2,1)S(1)}, bf16[64,1024]{1,0:T(8,128)(2,1)S(1)}, u32[]{:S(2)}, u32[]{:S(2)}) collective-permute-start(bf16[64,1024]{1,0:T(8,128)(2,1)S(1)} %get-tuple-element.19), channel_id=1, source_target_pairs={{0,1},{1,0},{2,3},{3,2},{4,5},{5,4},{6,7},{7,6},{8,9},{9,8},{10,11... | collective-permute-start | bytes 393224 | tf_op jit(solution)/shard_map/ppermute | solution.py:227
  23.5 10.3 %collective-permute-start.3 = (bf16[64,1024]{1,0:T(8,128)(2,1)S(1)}, bf16[64,1024]{1,0:T(8,128)(2,1)S(1)}, u32[]{:S(2)}, u32[]{:S(2)}) collective-permute-start(bf16[64,1024]{1,0:T(8,128)(2,1)S(1)} %get-tuple-element.20), channel_id=1, source_target_pairs={{0,0},{255,255},{1,2},{2,1},{3,4},{4,3},{5,6},{6,5},{7,8},{8,7},{9... | collective-permute-start | bytes 393224 | tf_op jit(solution)/shard_map/ppermute | solution.py:226
  37.1 10.1 %collective-permute-start.4 = (bf16[64,1024]{1,0:T(8,128)(2,1)S(1)}, bf16[64,1024]{1,0:T(8,128)(2,1)S(1)}, u32[]{:S(2)}, u32[]{:S(2)}) collective-permute-start(bf16[64,1024]{1,0:T(8,128)(2,1)S(1)} %get-tuple-element.22), channel_id=1, source_target_pairs={{0,1},{1,0},{2,3},{3,2},{4,5},{5,4},{6,7},{7,6},{8,9},{9,8},{10,11... | collective-permute-start | bytes 393224 | tf_op jit(solution)/shard_map/ppermute | solution.py:227
  37.2 10.0 %collective-permute-start.5 = (bf16[64,1024]{1,0:T(8,128)(2,1)S(1)}, bf16[64,1024]{1,0:T(8,128)(2,1)S(1)}, u32[]{:S(2)}, u32[]{:S(2)}) collective-permute-start(bf16[64,1024]{1,0:T(8,128)(2,1)S(1)} %get-tuple-element.23), channel_id=1, source_target_pairs={{0,0},{255,255},{1,2},{2,1},{3,4},{4,3},{5,6},{6,5},{7,8},{8,7},{9... | collective-permute-start | bytes 393224 | tf_op jit(solution)/shard_map/ppermute | solution.py:226
  50.4 9.9 %collective-permute-start.6 = (bf16[64,1024]{1,0:T(8,128)(2,1)S(1)}, bf16[64,1024]{1,0:T(8,128)(2,1)S(1)}, u32[]{:S(2)}, u32[]{:S(2)}) collective-permute-start(bf16[64,1024]{1,0:T(8,128)(2,1)S(1)} %get-tuple-element.25), channel_id=1, source_target_pairs={{0,1},{1,0},{2,3},{3,2},{4,5},{5,4},{6,7},{7,6},{8,9},{9,8},{10,11... | collective-permute-start | bytes 393224 | tf_op jit(solution)/shard_map/ppermute | solution.py:227
  50.5 9.8 %collective-permute-start.7 = (bf16[64,1024]{1,0:T(8,128)(2,1)S(1)}, bf16[64,1024]{1,0:T(8,128)(2,1)S(1)}, u32[]{:S(2)}, u32[]{:S(2)}) collective-permute-start(bf16[64,1024]{1,0:T(8,128)(2,1)S(1)} %get-tuple-element.26), channel_id=1, source_target_pairs={{0,0},{255,255},{1,2},{2,1},{3,4},{4,3},{5,6},{6,5},{7,8},{8,7},{9... | collective-permute-start | bytes 393224 | tf_op jit(solution)/shard_map/ppermute | solution.py:226
  63.5 9.6 %collective-permute-start.8 = (bf16[64,1024]{1,0:T(8,128)(2,1)S(1)}, bf16[64,1024]{1,0:T(8,128)(2,1)S(1)}, u32[]{:S(2)}, u32[]{:S(2)}) collective-permute-start(bf16[64,1024]{1,0:T(8,128)(2,1)S(1)} %get-tuple-element.28), channel_id=1, source_target_pairs={{0,1},{1,0},{2,3},{3,2},{4,5},{5,4},{6,7},{7,6},{8,9},{9,8},{10,11... | collective-permute-start | bytes 393224 | tf_op jit(solution)/shard_map/ppermute | solution.py:227
  63.6 9.5 %collective-permute-start.9 = (bf16[64,1024]{1,0:T(8,128)(2,1)S(1)}, bf16[64,1024]{1,0:T(8,128)(2,1)S(1)}, u32[]{:S(2)}, u32[]{:S(2)}) collective-permute-start(bf16[64,1024]{1,0:T(8,128)(2,1)S(1)} %get-tuple-element.29), channel_id=1, source_target_pairs={{0,0},{255,255},{1,2},{2,1},{3,4},{4,3},{5,6},{6,5},{7,8},{8,7},{9... | collective-permute-start | bytes 393224 | tf_op jit(solution)/shard_map/ppermute | solution.py:226
  76.7 1.3 %collective-permute-start.10 = (f32[64,128]{1,0:T(8,128)S(1)}, f32[64,128]{1,0:T(8,128)S(1)}, u32[]{:S(2)}, u32[]{:S(2)}) collective-permute-start(f32[64,128]{1,0:T(8,128)S(1)} %shard_map.68), channel_id=1, source_target_pairs={{0,8},{1,9},{2,10},{3,11},{4,12},{5,13},{6,14},{7,15},{8,0},{9,1},... | collective-permute-start | bytes 98312 | tf_op jit(solution)/shard_map/ppermute | solution.py:203
  78.0 5.9 %collective-permute-start.13 = (f32[64,128]{1,0:T(8,128)S(1)}, f32[64,128]{1,0:T(8,128)S(1)}, u32[]{:S(2)}, u32[]{:S(2)}) collective-permute-start(f32[64,128]{1,0:T(8,128)S(1)} %add.65), channel_id=1, source_target_pairs={{0,48},{1,49},{2,50},{3,51},{4,52},{5,53},{6,54},{7,55},{8,56},{9,... | collective-permute-start | bytes 98312 | tf_op jit(solution)/shard_map/ppermute | solution.py:203
  82.4 5.5 %collective-permute-start.12 = (f32[64,128]{1,0:T(8,128)S(1)}, f32[64,128]{1,0:T(8,128)S(1)}, u32[]{:S(2)}, u32[]{:S(2)}) collective-permute-start(f32[64,128]{1,0:T(8,128)S(1)} %add.65), channel_id=1, source_target_pairs={{0,32},{1,33},{2,34},{3,35},{4,36},{5,37},{6,38},{7,39},{8,40},{9,... | collective-permute-start | bytes 98312 | tf_op jit(solution)/shard_map/ppermute | solution.py:203
  82.4 5.5 %collective-permute-start.11 = (f32[64,128]{1,0:T(8,128)S(1)}, f32[64,128]{1,0:T(8,128)S(1)}, u32[]{:S(2)}, u32[]{:S(2)}) collective-permute-start(f32[64,128]{1,0:T(8,128)S(1)} %add.65), channel_id=1, source_target_pairs={{0,16},{1,17},{2,18},{3,19},{4,20},{5,21},{6,22},{7,23},{8,24},{9,... | collective-permute-start | bytes 98312 | tf_op jit(solution)/shard_map/ppermute | solution.py:203
  87.9 6.6 %collective-permute-start.16 = (f32[64,128]{1,0:T(8,128)S(1)}, f32[64,128]{1,0:T(8,128)S(1)}, u32[]{:S(2)}, u32[]{:S(2)}) collective-permute-start(f32[64,128]{1,0:T(8,128)S(1)} %add_add_fusion.2), channel_id=1, source_target_pairs={{0,192},{1,193},{2,194},{3,195},{4,196},{5,197},{6,198},{7,199},{8... | collective-permute-start | bytes 98312 | tf_op jit(solution)/shard_map/ppermute | solution.py:203
  92.9 5.4 %collective-permute-start.15 = (f32[64,128]{1,0:T(8,128)S(1)}, f32[64,128]{1,0:T(8,128)S(1)}, u32[]{:S(2)}, u32[]{:S(2)}) collective-permute-start(f32[64,128]{1,0:T(8,128)S(1)} %add_add_fusion.2), channel_id=1, source_target_pairs={{0,128},{1,129},{2,130},{3,131},{4,132},{5,133},{6,134},{7,135},{8... | collective-permute-start | bytes 98312 | tf_op jit(solution)/shard_map/ppermute | solution.py:203
  93.4 5.3 %collective-permute-start.14 = (f32[64,128]{1,0:T(8,128)S(1)}, f32[64,128]{1,0:T(8,128)S(1)}, u32[]{:S(2)}, u32[]{:S(2)}) collective-permute-start(f32[64,128]{1,0:T(8,128)S(1)} %add_add_fusion.2), channel_id=1, source_target_pairs={{0,64},{1,65},{2,66},{3,67},{4,68},{5,69},{6,70},{7,71},{8,72},{9,... | collective-permute-start | bytes 98312 | tf_op jit(solution)/shard_map/ppermute | solution.py:203
  98.7 12.3 %collective-permute-start.23 = (f32[64,128]{1,0:T(8,128)S(1)}, f32[64,128]{1,0:T(8,128)S(1)}, u32[]{:S(2)}, u32[]{:S(2)}) collective-permute-start(f32[64,128]{1,0:T(8,128)S(1)} %add_add_fusion.1), channel_id=1, source_target_pairs={{0,7},{1,0},{2,1},{3,2},{4,3},{5,4},{6,5},{7,6},{8,15},{9,8},{10,9... | collective-permute-start | bytes 98312 | tf_op jit(solution)/shard_map/ppermute | solution.py:203
  102.1 9.6 %collective-permute-start.22 = (f32[64,128]{1,0:T(8,128)S(1)}, f32[64,128]{1,0:T(8,128)S(1)}, u32[]{:S(2)}, u32[]{:S(2)}) collective-permute-start(f32[64,128]{1,0:T(8,128)S(1)} %add_add_fusion.1), channel_id=1, source_target_pairs={{0,6},{1,7},{2,0},{3,1},{4,2},{5,3},{6,4},{7,5},{8,14},{9,15},{10,... | collective-permute-start | bytes 98312 | tf_op jit(solution)/shard_map/ppermute | solution.py:203
  103.8 9.3 %collective-permute-start.21 = (f32[64,128]{1,0:T(8,128)S(1)}, f32[64,128]{1,0:T(8,128)S(1)}, u32[]{:S(2)}, u32[]{:S(2)}) collective-permute-start(f32[64,128]{1,0:T(8,128)S(1)} %add_add_fusion.1), channel_id=1, source_target_pairs={{0,5},{1,6},{2,7},{3,0},{4,1},{5,2},{6,3},{7,4},{8,13},{9,14},{10,... | collective-permute-start | bytes 98312 | tf_op jit(solution)/shard_map/ppermute | solution.py:203
  104.3 8.8 %collective-permute-start.20 = (f32[64,128]{1,0:T(8,128)S(1)}, f32[64,128]{1,0:T(8,128)S(1)}, u32[]{:S(2)}, u32[]{:S(2)}) collective-permute-start(f32[64,128]{1,0:T(8,128)S(1)} %add_add_fusion.1), channel_id=1, source_target_pairs={{0,4},{1,5},{2,6},{3,7},{4,0},{5,1},{6,2},{7,3},{8,12},{9,13},{10,... | collective-permute-start | bytes 98312 | tf_op jit(solution)/shard_map/ppermute | solution.py:203
  110.2 7.1 %collective-permute-start.19 = (f32[64,128]{1,0:T(8,128)S(1)}, f32[64,128]{1,0:T(8,128)S(1)}, u32[]{:S(2)}, u32[]{:S(2)}) collective-permute-start(f32[64,128]{1,0:T(8,128)S(1)} %add_add_fusion.1), channel_id=1, source_target_pairs={{0,3},{1,4},{2,5},{3,6},{4,7},{5,0},{6,1},{7,2},{8,11},{9,12},{10,... | collective-permute-start | bytes 98312 | tf_op jit(solution)/shard_map/ppermute | solution.py:203
  111.0 6.8 %collective-permute-start.18 = (f32[64,128]{1,0:T(8,128)S(1)}, f32[64,128]{1,0:T(8,128)S(1)}, u32[]{:S(2)}, u32[]{:S(2)}) collective-permute-start(f32[64,128]{1,0:T(8,128)S(1)} %add_add_fusion.1), channel_id=1, source_target_pairs={{0,2},{1,3},{2,4},{3,5},{4,6},{5,7},{6,0},{7,1},{8,10},{9,11},{10,... | collective-permute-start | bytes 98312 | tf_op jit(solution)/shard_map/ppermute | solution.py:203
  111.7 6.1 %collective-permute-start.17 = (f32[64,128]{1,0:T(8,128)S(1)}, f32[64,128]{1,0:T(8,128)S(1)}, u32[]{:S(2)}, u32[]{:S(2)}) collective-permute-start(f32[64,128]{1,0:T(8,128)S(1)} %add_add_fusion.1), channel_id=1, source_target_pairs={{0,1},{1,2},{2,3},{3,4},{4,5},{5,6},{6,7},{7,0},{8,9},{9,10},{10,1... | collective-permute-start | bytes 98312 | tf_op jit(solution)/shard_map/ppermute | solution.py:203

commit v2 on v0

v2 whole, which is shorter than its diff:
```python
import functools

import jax
import jax.numpy as jnp
import numpy as np
from jax import lax
from jax.experimental import pallas as pl
from jax.experimental.pallas import tpu as pltpu
from jax.sharding import PartitionSpec as P

DEG = 4
GHOST = 8
TB = 128
AX = ("dom", "board")
MIB = 1 << 20
NN_DIMS = (((1,), (0,)), ((), ()))
NT_DIMS = (((1,), (1,)), ((), ()))
GROUP = 8
SMALL = 4

VM = pl.BlockSpec(memory_space=pltpu.VMEM)
SM = pl.BlockSpec(memory_space=pltpu.SMEM)
HBM = pl.BlockSpec(memory_space=pltpu.HBM)

OWN, SLOT, BLOCK, NEED, MISC = 0, 10, 20, 30, 31
TABLE = (32, 128)


def call(kernel, out_shape, in_specs, out_specs, scratch=(), limit=24, flops=0, bytes_=0):
    return pl.pallas_call(
        kernel,
        out_shape=out_shape,
        in_specs=in_specs,
        out_specs=out_specs,
        scratch_shapes=scratch,
        compiler_params=pltpu.CompilerParams(vmem_limit_bytes=limit * MIB),
        cost_estimate=pl.CostEstimate(flops=flops, bytes_accessed=bytes_, transcendentals=0),
    )


def stay(x):
    return pltpu.with_memory_space_constraint(x, pltpu.HBM)


def block_at(ref, offset):
    return ref[:, pl.ds(pl.multiple_of(offset, TB), TB)]


def own_row(src, tiles, tab, row, slots):
    total = None
    for pair in range(slots // 2):
        lhs = jnp.concatenate(
            [block_at(src, tab[OWN + 2 * pair, row]), block_at(src, tab[OWN + 2 * pair + 1, row])], axis=1
        )
        rhs = tiles(row, pair)
        term = lax.dot_general(lhs, rhs, NN_DIMS, preferred_element_type=jnp.float32)
        total = term if total is None else total + term
    return total


def gather_field(src, s0, mid, s1):
    edge, inner = s0.shape[1], mid.shape[1]
    src[:, :edge] = s0[...]
    src[:, edge : edge + inner] = mid[...]
    src[:, edge + inner : 2 * edge + inner] = s1[...]
    src[:, 2 * edge + inner :] = jnp.zeros_like(src[:, 2 * edge + inner :])


def own_products(src, pair_of, tab, old, acc, new, cheb, slots, rows, before=None, group=GROUP):
    def place(u, value):
        at = pl.ds(pl.multiple_of(u * TB, TB), TB)
        if cheb:
            value = 2.0 * value - old[:, at].astype(jnp.float32)
        new[:, at] = value.astype(jnp.bfloat16)

    def side(u, value):
        acc[:, pl.ds(pl.multiple_of(u * TB, TB), TB)] = value

    def sweep(first, out, count, store):
        def step(g, carry):
            if before is not None:
                before(first + g * group)
            values = [own_row(src, pair_of, tab, first + g * group + u, slots) for u in range(group)]
            for u in range(group):
                store(out + g * group + u, values[u])
            return carry

        lax.fori_loop(0, count // group, step, 0)

    lead, trail = tab[MISC, 0], tab[MISC, 1]
    sweep(lead, 0, GHOST, side)
    sweep(GHOST, 0, rows - 2 * GHOST, place)
    sweep(trail, GHOST, GHOST, side)


def held_pairs(tiles):
    return lambda row, pair: tiles[row, 2 * pair * TB : 2 * (pair + 1) * TB, :]


def fill_table(cols, counts, place, lines, rows, slots):
    first, odd, core = place[0], place[1], place[2]
    lead = (1 - odd) * (rows - GHOST)
    near = cols[...] - first
    live = lax.broadcasted_iota(jnp.int32, near.shape, 0) < counts[...]
    inside = (near >= 0) & (near < rows)
    spot = jnp.where(near < GHOST, near + lead, jnp.where(near >= rows - GHOST, near - lead, near))
    lines[OWN : OWN + slots, :rows] = jnp.where(live & inside, spot, rows) * TB
    out = jnp.where(live & ~inside, 1, 0)
    there = jnp.where(near < 0, near + GHOST + GHOST * (1 - odd), near - rows + GHOST * odd) * TB
    empty = jnp.zeros((1, rows), jnp.int32)
    found = empty
    slot_lines, block_lines = [empty] * slots, [empty + 2 * GHOST * TB] * slots
    for s in range(slots):
        here = out[s : s + 1]
        for q in range(s + 1):
            hit = (here == 1) & (found == q)
            slot_lines[q] = jnp.where(hit, s * TB, slot_lines[q])
            block_lines[q] = jnp.where(hit, there[s : s + 1], block_lines[q])
        found = found + here
    for q in range(slots):
        lines[SLOT + q : SLOT + q + 1, :rows] = slot_lines[q]
        lines[BLOCK + q : BLOCK + q + 1, :rows] = block_lines[q]
    lines[NEED : NEED + 1, :rows] = found
    lane = lax.broadcasted_iota(jnp.int32, (1, rows), 1)
    lines[MISC : MISC + 1, :rows] = jnp.where(lane == 0, lead, jnp.where(lane == 1, rows - GHOST - lead, core))


def load_kernel(
    s0, s1, block, tiles_hbm, cols_hbm, counts_hbm, place, tiles, acc, mid0, new, tab, src, raw, cols, counts, lines,
    sems, small_sems,
):
    rows, slots = raw.shape[0], raw.shape[1]
    edge = GHOST * TB
    chunk = GROUP
    little = [
        pltpu.make_async_copy(cols_hbm, cols, small_sems.at[0]),
        pltpu.make_async_copy(counts_hbm, counts, small_sems.at[1]),
        pltpu.make_async_copy(block.at[:, pl.ds(edge, mid0.shape[1])], mid0, small_sems.at[2]),
    ]
    for copy in little:
        copy.start()

    def piece(start):
        return pltpu.make_async_copy(
            tiles_hbm.at[pl.ds(start, chunk)], raw.at[pl.ds(start, chunk)], sems.at[lax.div(start, chunk)]
        )

    lead = (1 - place[1]) * (rows - GHOST)
    for c in range(GHOST // chunk):
        piece(lead + c * chunk).start()
    for c in range(GHOST // chunk, (rows - GHOST) // chunk):
        piece(c * chunk).start()
    for c in range(GHOST // chunk):
        piece(rows - GHOST - lead + c * chunk).start()
    little[0].wait()
    little[1].wait()
    fill_table(cols, counts, place, lines, rows, slots)
    to_scalars = pltpu.make_async_copy(lines, tab, small_sems.at[3])
    to_scalars.start()
    little[2].wait()
    gather_field(src, s0, mid0, s1)
    to_scalars.wait()

    def pair_of(row, pair):
        turned = jnp.concatenate([raw[row, 2 * pair].T, raw[row, 2 * pair + 1].T], axis=0)
        tiles[row, 2 * pair * TB : 2 * (pair + 1) * TB, :] = turned
        return turned

    own_products(
        src, pair_of, tab, None, acc, new, False, slots, rows, before=lambda start: piece(start).wait(), group=chunk
    )


def own_kernel(s0, mid, s1, old, tiles, tab, acc, new, src, *, slots):
    gather_field(src, s0, mid, s1)
    own_products(src, held_pairs(tiles), tab, old, acc, new, True, slots, tiles.shape[0])


def own_last_kernel(s0, mid, s1, tiles, tab, acc, both, src, new, *, slots):
    gather_field(src, s0, mid, s1)
    own_products(src, held_pairs(tiles), tab, None, acc, new, False, slots, tiles.shape[0])
    edge, inner = s0.shape[1], mid.shape[1]
    size = mid.shape[0]
    mids = mid[...]
    total = lax.dot_general(
        mids, jnp.concatenate([mids, new[...]], axis=0), NT_DIMS, preferred_element_type=jnp.float32
    )
    gram = jnp.zeros((size, size), jnp.float32)
    for side in (s0[...], s1[...]):
        gram = gram + lax.dot_general(side, side, NT_DIMS, preferred_element_type=jnp.float32)
    both[...] = total + jnp.concatenate([gram, jnp.zeros_like(gram)], axis=1)


def halo_products(acc, r0, r1, tiles, tab, halo, sums, slots):
    edge = GHOST * TB
    halo[:, :edge] = r0[...]
    halo[:, edge : 2 * edge] = r1[...]
    halo[:, 2 * edge :] = jnp.zeros_like(halo[:, 2 * edge :])

    first = (tab[MISC, 0], tab[MISC, 1])

    def term(k, pair):
        row = first[k // GHOST] + k % GHOST
        lhs = jnp.concatenate(
            [block_at(halo, tab[BLOCK + 2 * pair, row]), block_at(halo, tab[BLOCK + 2 * pair + 1, row])], axis=1
        )
        rhs = jnp.concatenate(
            [tiles[row, pl.ds(pl.multiple_of(tab[SLOT + 2 * pair + e, row], TB), TB), :] for e in (0, 1)], axis=0
        )
        return lax.dot_general(lhs, rhs, NN_DIMS, preferred_element_type=jnp.float32)

    for half in (0, GHOST):
        terms = [term(half + u, 0) for u in range(GHOST)]
        for u in range(GHOST):
            at = slice((half + u) * TB, (half + u + 1) * TB)
            sums[:, at] = acc[:, at] + terms[u]
    for g in range(2 * GHOST // SMALL):
        start = first[g * SMALL // GHOST] + g * SMALL % GHOST
        need = tab[NEED, start]
        for u in range(1, SMALL):
            need = jnp.maximum(need, tab[NEED, start + u])

        def more(pair, carry, g=g):
            terms = [term(g * SMALL + u, pair) for u in range(SMALL)]
            for u in range(SMALL):
                at = slice((g * SMALL + u) * TB, (g * SMALL + u + 1) * TB)
                sums[:, at] += terms[u]
            return carry

        lax.fori_loop(1, lax.div(need + 1, 2), more, 0)


def halo_kernel(acc, old0, old1, r0, r1, tiles, tab, s0, s1, halo, sums, *, cheb, slots):
    edge = GHOST * TB
    halo_products(acc, r0, r1, tiles, tab, halo, sums, slots)
    for side, old, new in ((0, old0, s0), (1, old1, s1)):
        value = sums[:, side * edge : (side + 1) * edge]
        if cheb:
            value = 2.0 * value - old[...].astype(jnp.float32)
        new[...] = value.astype(jnp.bfloat16)


def halo_last_kernel(acc, s0, s1, r0, r1, tiles, tab, both, keep, give, whole, halo, sums, *, slots):
    edge = GHOST * TB
    size = both.shape[0]
    halo_products(acc, r0, r1, tiles, tab, halo, sums, slots)
    cross = both[:, size:]
    for side, y in ((0, s0), (1, s1)):
        image = sums[:, side * edge : (side + 1) * edge].astype(jnp.bfloat16)
        cross = cross + lax.dot_general(y[...], image, NT_DIMS, preferred_element_type=jnp.float32)
    whole[...] = jnp.concatenate([both[:, :size], cross], axis=1)
    half = size // 2
    mine = pl.multiple_of(tab[MISC, 2] * half, half)
    keep[...] = whole[pl.ds(mine, half), :]
    give[...] = whole[pl.ds(pl.multiple_of(half - mine, half), half), :]


def eliminate(gram):
    size = gram.shape[0]
    step, sub = 4, 8
    lanes = lax.broadcasted_iota(jnp.int32, (sub, 2 * size), 1)
    inner = lax.broadcasted_iota(jnp.int32, (sub, 2 * size), 0)
    wide = jnp.concatenate([gram, jnp.zeros_like(gram)], axis=1)
    work = [
        jnp.where(lanes == inner + g * sub + size, 1.0, wide[g * sub : (g + 1) * sub]) for g in range(size // sub)
    ]
    for k in range(0, size, step):
        g0, off = divmod(k, sub)
        cols = [
            {g: jnp.broadcast_to(work[g][:, k + j : k + j + 1], (sub, 2 * size)) for g in range(g0, size // sub)}
            for j in range(step)
        ]
        rows = [work[g0][off + j : off + j + 1] for j in range(step)]
        units = []
        finals = []
        for j in range(step):
            pivot = cols[j][g0][off + j : off + j + 1]
            inverse = 1.0 / pivot
            unit = rows[j] * inverse
            units.append(unit)
            finals.append(rows[j] * lax.rsqrt(pivot))
            for m in range(j + 1, step):
                rows[m] = rows[m] - cols[j][g0][off + m : off + m + 1] * unit
                factor = cols[m][g0][off + j : off + j + 1] * inverse
                cols[m] = {g: cols[m][g] - cols[j][g] * factor for g in cols[m]}
        for g in range(g0, size // sub):
            value = work[g]
            for j in range(step):
                value = value - cols[j][g] * units[j]
            if g == g0:
                value = jnp.where(inner >= off + step, value, work[g])
                for j in range(step):
                    value = jnp.where(inner == off + j, finals[j], value)
            work[g] = value
    return jnp.concatenate(work, axis=0)[:, size:]


def split3(x):
    hi = x.astype(jnp.bfloat16)
    rest = x - hi.astype(jnp.float32)
    mid = rest.astype(jnp.bfloat16)
    low = (rest - mid.astype(jnp.float32)).astype(jnp.bfloat16)
    return hi, mid, low


def end_kernel(mine, other, s0, mid, s1, tab, basis, projected, both, *, nodes_all):
    size = both.shape[0]
    half = size // 2
    at = pl.multiple_of(tab[MISC, 2] * half, half)
    both[pl.ds(at, half), :] = mine[...]
    both[pl.ds(pl.multiple_of(half - at, half), half), :] = other[...]
    edge, inner = s0.shape[1], mid.shape[1]
    values = both[...] / nodes_all
    inverse = eliminate(values[:, :size])
    cross = values[:, size:]
    parts = jnp.concatenate(split3(inverse), axis=0)

    def piece(y):
        out = jnp.dot(parts, y, preferred_element_type=jnp.float32)
        return (out[:size] + (out[size : 2 * size] + out[2 * size :])).astype(jnp.bfloat16)

    lead = pl.multiple_of(tab[MISC, 0] * TB, TB)
    trail = pl.multiple_of(tab[MISC, 1] * TB, TB)
    basis[:, pl.ds(lead, edge)] = piece(s0[...])
    basis[:, pl.ds(trail, edge)] = piece(s1[...])
    for c in range(0, inner, edge):
        basis[:, edge + c : 2 * edge + c] = piece(mid[:, c : c + edge])
    half = jnp.dot(inverse, cross, precision=lax.Precision.HIGHEST, preferred_element_type=jnp.float32)
    projected[...] = lax.dot_general(
        half, inverse, NT_DIMS, precision=lax.Precision.HIGHEST, preferred_element_type=jnp.float32
    )


def rotations(shape, axis):
    at = np.arange(int(np.prod(shape))).reshape(shape)
    return [
        list(zip(at.reshape(-1).tolist(), np.roll(at, -k, axis=axis).reshape(-1).tolist()))
        for k in range(1, shape[axis])
    ]


def all_sum(keep, give, dom, board):
    shape = (dom // 8, 4, 2, board)
    (swap,) = rotations(shape, 2)
    x = keep + lax.ppermute(give, AX, swap)
    planes = np.arange(dom * board).reshape(-1, 2 * board).T.tolist()
    spread = jnp.broadcast_to(x[None], (dom // 2,) + x.shape)
    x = lax.all_to_all(spread, AX, 0, 0, axis_index_groups=planes).sum(0)
    spread = jnp.broadcast_to(x[None], (board,) + x.shape)
    x = lax.all_to_all(spread, "board", 0, 0).sum(0)
    return x, lax.ppermute(x, AX, swap)


def body(block, tiles, cols, counts, *, dom, board):
    devices = dom * board
    size, wide = block.shape
    rows, slots = cols.shape
    edge = GHOST * TB
    inner = wide - 2 * edge
    bf16, f32 = jnp.bfloat16, jnp.float32
    shape = jax.ShapeDtypeStruct
    me = lax.axis_index(AX)
    odd = me % 2
    core = (me // board) % 2
    place = jnp.stack([me * rows, odd, core]).astype(jnp.int32)

    even_pairs = [(i, i ^ 1) for i in range(devices)]
    odd_pairs = [(i, (((i + 1) ^ 1) - 1) % devices) for i in range(devices)]

    def exchange(s0, s1):
        return lax.ppermute(s0, AX, even_pairs), lax.ppermute(s1, AX, odd_pairs)

    head, tail = block[:, :edge], block[:, wide - edge :]
    s0, s1 = jnp.where(odd == 1, head, tail), jnp.where(odd == 1, tail, head)
    r0, r1 = exchange(s0, s1)

    own_flops = 2 * rows * slots * size * TB * TB
    halo_flops = own_flops // 8
    acc_shape = shape((size, 2 * edge), f32)
    mid_shape = shape((size, inner), bf16)
    edge_shape = shape((size, edge), bf16)
    field = pltpu.VMEM((size, wide + TB), bf16)
    halo_scratch = [pltpu.VMEM((size, 2 * edge + TB), bf16), pltpu.VMEM((size, 2 * edge), f32)]

    tiles_v, acc, mid, new, tab = call(
        load_kernel,
        [shape((rows, slots * TB, TB), bf16), acc_shape, mid_shape, mid_shape, pltpu.SMEM(TABLE, jnp.int32)],
        [VM, VM, HBM, HBM, HBM, HBM, SM],
        [VM, VM, VM, VM, SM],
        [
            field,
            pltpu.VMEM(tiles.shape, bf16),
            pltpu.VMEM((slots, rows), jnp.int32),
            pltpu.VMEM((1, rows), jnp.int32),
            pltpu.VMEM(TABLE, jnp.int32),
            pltpu.SemaphoreType.DMA((rows // GROUP,)),
            pltpu.SemaphoreType.DMA((4,)),
        ],
        limit=40,
        flops=own_flops,
        bytes_=tiles.size * 2,
    )(s0, s1, *(stay(v) for v in (block, tiles, cols.T, counts.reshape(1, rows))), place)

    tab = pltpu.with_memory_space_constraint(tab, pltpu.SMEM)
    older = (s0, mid, s1)
    for degree in range(DEG):
        old0, old_mid, old1 = older
        older = (s0, mid, s1)
        s0, s1 = call(
            functools.partial(halo_kernel, cheb=degree > 0, slots=slots),
            [edge_shape, edge_shape],
            [VM, VM, VM, VM, VM, VM, SM],
            [VM, VM],
            halo_scratch,
            flops=halo_flops,
        )(acc, old0, old1, r0, r1, tiles_v, tab)
        mid = new
        r0, r1 = exchange(s0, s1)
        if degree < DEG - 1:
            acc, new = call(
                functools.partial(own_kernel, slots=slots),
                [acc_shape, mid_shape],
                [VM, VM, VM, VM, VM, SM],
                [VM, VM],
                [field],
                flops=own_flops,
            )(s0, mid, s1, older[1], tiles_v, tab)
        else:
            acc, both = call(
                functools.partial(own_last_kernel, slots=slots),
                [acc_shape, shape((size, 2 * size), f32)],
                [VM, VM, VM, VM, SM],
                [VM, VM],
                [field, pltpu.VMEM((size, inner), bf16)],
                flops=own_flops,
            )(s0, mid, s1, tiles_v, tab)

    half_shape = shape((size // 2, 2 * size), f32)
    keep, give = call(
        functools.partial(halo_last_kernel, slots=slots),
        [half_shape, half_shape],
        [VM, VM, VM, VM, VM, VM, SM, VM],
        [VM, VM],
        [pltpu.VMEM((size, 2 * size), f32)] + halo_scratch,
        flops=halo_flops,
    )(acc, s0, s1, r0, r1, tiles_v, tab, both)
    mine, other = all_sum(keep, give, dom, board)
    basis, projected = call(
        functools.partial(end_kernel, nodes_all=devices * rows * TB),
        [shape((size, wide), bf16), shape((size, size), f32)],
        [VM, VM, VM, VM, VM, SM],
        [VM, VM],
        [pltpu.VMEM((size, 2 * size), f32)],
        flops=6 * size * size * wide,
    )(mine, other, s0, mid, s1, tab)
    return basis, projected


def solution(mesh):
    dom, board = mesh.shape["dom"], mesh.shape["board"]
    return jax.shard_map(
        functools.partial(body, dom=dom, board=board),
        mesh=mesh,
        in_specs=(
            P(None, AX),
            P(AX, None, None, None),
            P(AX, None),
            P(AX),
        ),
        out_specs=(P(None, AX), P()),
        check_vma=False,
    )
```

time: 268 us -> 95.1 us (0.35)
  blocking collectives: 92.3 us -> 20.7 us
  local copies, waits for them, and re-layouts: 68.3 us -> 0.03 us
  matrix products: 41.7 us -> 0 us
  Pallas kernels: 0 us -> 23.7 us
  other arithmetic: 15.9 us -> 1.11 us
    psum x1 -> x0, blocking collectives: 92.3 us -> none  [body(): gram = lax.psum(gram_local, ('dom', 'board'))]
    gather x5 -> x0, local copies, waits for them, and re-layouts: 66.7 us -> none  [apply_rows(): picked = jnp.take(blocks, local, axis=1)]
    dot_general x10 -> x0, matrix products: 41.4 us -> none  [the longest x5 38.5 us: apply_rows(): jnp.einsum('krsj,rsij->kri', picked, tiles, preferred_element_type=jnp.fl...]
    pallas_call x0 -> x11, Pallas kernels: none -> 23.7 us  [the longest x1 7.44 us: body(): call(load_kernel, [shape((rows, slots * TB, TB), bf16), acc_shape, mid_sh...]
    all_to_all x0 -> x2, blocking collectives: none -> 20.7 us  [the longest x1 10.3 us: all_sum(): x = lax.all_to_all(spread, AX, 0, 0, axis_index_groups=planes).sum(0)]
    another operation x5 -> x1, other arithmetic: 12.1 us -> 0.08 us  [body(): place = jnp.stack([me * rows, odd, core]).astype(jnp.int32)]
    ppermute x10 -> x12, starting transfers between devices: 41.1 us -> 42.3 us  [the longest x10 20.5 us: exchange(): return (lax.ppermute(s0, AX, even_pairs), lax.ppermute(s1, AX, odd_pairs))]
    ppermute x10 -> x12, waiting for transfers between devices: 7.18 us -> 6.49 us  [the longest x10 4.81 us: exchange(): return (lax.ppermute(s0, AX, even_pairs), lax.ppermute(s1, AX, odd_pairs))]
  transfers between devices with their start and end apart: 10 -> 12, of which waited for: 9 -> 5; matrix products, arithmetic and copies ran while one was open for 1% -> 0% of each run, Pallas kernels for 0% -> 19%
where the time goes in v2:
time: 95.1 us
  starting transfers between devices  42.3 us (44%)
  Pallas kernels  23.7 us (25%)
  blocking collectives  20.7 us (22%)
  waiting for transfers between devices  6.49 us (7%)
  other arithmetic  1.11 us (1%)
    ppermute x10, starting transfers between devices, exchange(): return (lax.ppermute(s0, AX, even_pairs), lax.ppermute(s1, AX, odd_pairs))  20.5 us
    ppermute x1, starting transfers between devices, all_sum(): x = keep + lax.ppermute(give, AX, swap)  18.9 us
    all_to_all x1, blocking collectives, all_sum(): x = lax.all_to_all(spread, AX, 0, 0, axis_index_groups=planes).sum(0)  10.3 us
    all_to_all x1, blocking collectives, all_sum(): x = lax.all_to_all(spread, 'board', 0, 0).sum(0)  10.3 us
    pallas_call x1, Pallas kernels, body(): call(load_kernel, [shape((rows, slots * TB, TB), bf16), acc_shape, mid_sh...  7.44 us
    pallas_call x3, Pallas kernels, body(): call(functools.partial(own_kernel, slots=slots), [acc_shape, mid_shape],...  7.4 us
    ppermute x10, waiting for transfers between devices, exchange(): return (lax.ppermute(s0, AX, even_pairs), lax.ppermute(s1, AX, odd_pairs))  4.81 us
    pallas_call x1, Pallas kernels, body(): call(functools.partial(end_kernel, nodes_all=devices * rows * TB), [shape...  3.55 us
  transfers between devices with their start and end apart: 12, of which 5 were waited for; matrix products, arithmetic and copies ran while one was open for 0% of the time, Pallas kernels for 19%

profile of v2, /device:TPU:1, one launch (start us, length us, event | category | flops | bytes accessed | tf_op | source)
XLA Modules:
  0.0 95.1 jit_solution(8302732736252752119)
XLA Ops:
  0.6 1.0 %broadcast_select_fusion = (bf16[64,1024]{1,0:T(8,128)(2,1)S(1)}, bf16[64,1024]{1,0:T(8,128)(2,1)S(1)}) fusion(pred[]{:T(512)S(6)} %eq.7, bf16[64,4096]{1,0:T(8,128)(2,1)} %block.1), kind=kLoop, calls=%fused_computation | loop fusion | flops 131072 | bytes 524289 | tf_op jit(solution)/shard_map/jit(_where)/select_n | solution.py:374
  1.6 7.1 %collective-permute-start.1 = (bf16[64,1024]{1,0:T(8,128)(2,1)S(1)}, bf16[64,1024]{1,0:T(8,128)(2,1)S(1)}, u32[]{:S(2)}, u32[]{:S(2)}) collective-permute-start(bf16[64,1024]{1,0:T(8,128)(2,1)S(1)} %get-tuple-element.48.s1.old1), channel_id=1, source_target_pairs={{0,255},{1,2},{2,1},{3,4},{4,3},{5,6},{6,5},{7,8},{8,7},{9,10},{10... | collective-permute-start | bytes 393224 | tf_op jit(solution)/shard_map/ppermute | solution.py:371
  8.7 0.0 collective-permute-start
  8.7 0.1 pad_add_fusion.place
  8.8 7.4 %shard_map.59 = (bf16[32,1280,128]{2,1,0:T(8,128)(2,1)S(1)}, f32[64,2048]{1,0:T(8,128)S(1)}, bf16[64,2048]{1,0:T(8,128)(2,1)S(1)}, bf16[64,2048]{1,0:T(8,128)(2,1)S(1)}, s32[32,128]{1,0:T(8,128)S(4)}) custom-call(bf16[64,1024]{1,0:T(8,128)(2,1)S(1)} %get-tuple-element.49.s0.old0, bf16[64,1024]{1,0:T(8,128)(2,1)S(1)} %get-tuple-element.48.s1.old1, ...), custom_call_target="tpu_custom_call" | custom-call | flops 671088640 | bytes 10485760 | tf_op jit(solution)/shard_map/pallas_call | solution.py:385
  16.2 0.0 collective-permute-done.1.r1
  16.2 0.0 collective-permute-done.r0
  16.2 0.4 shard_map.60
  16.7 1.9 %collective-permute-start.2 = (bf16[64,1024]{1,0:T(8,128)(2,1)S(1)}, bf16[64,1024]{1,0:T(8,128)(2,1)S(1)}, u32[]{:S(2)}, u32[]{:S(2)}) collective-permute-start(bf16[64,1024]{1,0:T(8,128)(2,1)S(1)} %get-tuple-element.28.s0.old0), channel_id=1, source_target_pairs={{0,1},{1,0},{2,3},{3,2},{4,5},{5,4},{6,7},{7,6},{8,9},{9,8},{10,11... | collective-permute-start | bytes 393224 | tf_op jit(solution)/shard_map/ppermute | solution.py:371
  18.6 1.0 %collective-permute-start.3 = (bf16[64,1024]{1,0:T(8,128)(2,1)S(1)}, bf16[64,1024]{1,0:T(8,128)(2,1)S(1)}, u32[]{:S(2)}, u32[]{:S(2)}) collective-permute-start(bf16[64,1024]{1,0:T(8,128)(2,1)S(1)} %get-tuple-element.30.s1.old1), channel_id=1, source_target_pairs={{0,255},{1,2},{2,1},{3,4},{4,3},{5,6},{6,5},{7,8},{8,7},{9,10},{10... | collective-permute-start | bytes 393224 | tf_op jit(solution)/shard_map/ppermute | solution.py:371
  19.6 2.5 %shard_map.61 = (f32[64,2048]{1,0:T(8,128)S(1)}, bf16[64,2048]{1,0:T(8,128)(2,1)S(1)}) custom-call(bf16[64,1024]{1,0:T(8,128)(2,1)S(1)} %get-tuple-element.28.s0.old0, bf16[64,2048]{1,0:T(8,128)(2,1)S(1)} %get-tuple-element.29.mid.old, bf16[64,1024]{1,0:T(8,128)(2,1)S(1)} %get-tuple-element.30.s1.old1, bf16[64,2048]{1,0:T(8,128)(2,1)S(1)} %get-tuple-element.31.old, ...), custom_call_target="tpu_custom_call" | custom-call | flops 671088640 | tf_op jit(solution)/shard_map/pallas_call | solution.py:420
  22.1 0.0 collective-permute-done.2.r0
  22.1 2.9 %collective-permute-done.3.r1 = bf16[64,1024]{1,0:T(8,128)(2,1)S(1)} collective-permute-done((bf16[64,1024]{1,0:T(8,128)(2,1)S(1)}, bf16[64,1024]{1,0:T(8,128)(2,1)S(1)}, u32[]{:S(2)}, u32[]{:S(2)}) %collective-permute-start.3) | collective-permute-done | bytes 131104 | tf_op jit(solution)/shard_map/ppermute | solution.py:371
  25.1 0.5 shard_map.62
  25.6 0.1 collective-permute-start.4
  25.7 1.8 %collective-permute-start.5 = (bf16[64,1024]{1,0:T(8,128)(2,1)S(1)}, bf16[64,1024]{1,0:T(8,128)(2,1)S(1)}, u32[]{:S(2)}, u32[]{:S(2)}) collective-permute-start(bf16[64,1024]{1,0:T(8,128)(2,1)S(1)} %get-tuple-element.35.s1.old1), channel_id=1, source_target_pairs={{0,255},{1,2},{2,1},{3,4},{4,3},{5,6},{6,5},{7,8},{8,7},{9,10},{10... | collective-permute-start | bytes 393224 | tf_op jit(solution)/shard_map/ppermute | solution.py:371
  27.5 2.5 %shard_map.63 = (f32[64,2048]{1,0:T(8,128)S(1)}, bf16[64,2048]{1,0:T(8,128)(2,1)S(1)}) custom-call(bf16[64,1024]{1,0:T(8,128)(2,1)S(1)} %get-tuple-element.33.s0.old0, bf16[64,2048]{1,0:T(8,128)(2,1)S(1)} %get-tuple-element.34.mid.old, bf16[64,1024]{1,0:T(8,128)(2,1)S(1)} %get-tuple-element.35.s1.old1, bf16[64,2048]{1,0:T(8,128)(2,1)S(1)} %get-tuple-element.29.mid.old, ...), custom_call_target="tpu_custom_call" | custom-call | flops 671088640 | tf_op jit(solution)/shard_map/pallas_call | solution.py:420
  29.9 0.0 collective-permute-done.4.r0
  30.0 1.7 %collective-permute-done.5.r1 = bf16[64,1024]{1,0:T(8,128)(2,1)S(1)} collective-permute-done((bf16[64,1024]{1,0:T(8,128)(2,1)S(1)}, bf16[64,1024]{1,0:T(8,128)(2,1)S(1)}, u32[]{:S(2)}, u32[]{:S(2)}) %collective-permute-start.5) | collective-permute-done | bytes 131104 | tf_op jit(solution)/shard_map/ppermute | solution.py:371
  31.6 0.5 shard_map.64
  32.1 0.3 collective-permute-start.6
  32.4 3.2 %collective-permute-start.7 = (bf16[64,1024]{1,0:T(8,128)(2,1)S(1)}, bf16[64,1024]{1,0:T(8,128)(2,1)S(1)}, u32[]{:S(2)}, u32[]{:S(2)}) collective-permute-start(bf16[64,1024]{1,0:T(8,128)(2,1)S(1)} %get-tuple-element.39.s1), channel_id=1, source_target_pairs={{0,255},{1,2},{2,1},{3,4},{4,3},{5,6},{6,5},{7,8},{8,7},{9,10},{10... | collective-permute-start | bytes 393224 | tf_op jit(solution)/shard_map/ppermute | solution.py:371
  35.6 2.5 %shard_map.65 = (f32[64,2048]{1,0:T(8,128)S(1)}, bf16[64,2048]{1,0:T(8,128)(2,1)S(1)}) custom-call(bf16[64,1024]{1,0:T(8,128)(2,1)S(1)} %get-tuple-element.37.s0, bf16[64,2048]{1,0:T(8,128)(2,1)S(1)} %get-tuple-element.38.mid, bf16[64,1024]{1,0:T(8,128)(2,1)S(1)} %get-tuple-element.39.s1, bf16[64,2048]{1,0:T(8,128)(2,1)S(1)} %get-tuple-element.34.mid.old, ...), custom_call_target="tpu_custom_call" | custom-call | flops 671088640 | tf_op jit(solution)/shard_map/pallas_call | solution.py:420
  38.0 0.0 collective-permute-done.6.r0
  38.1 0.2 collective-permute-done.7.r1
  38.2 0.5 shard_map.66
  38.7 0.2 collective-permute-start.8
  38.9 4.9 %collective-permute-start.9 = (bf16[64,1024]{1,0:T(8,128)(2,1)S(1)}, bf16[64,1024]{1,0:T(8,128)(2,1)S(1)}, u32[]{:S(2)}, u32[]{:S(2)}) collective-permute-start(bf16[64,1024]{1,0:T(8,128)(2,1)S(1)} %get-tuple-element.43.s1), channel_id=1, source_target_pairs={{0,255},{1,2},{2,1},{3,4},{4,3},{5,6},{6,5},{7,8},{8,7},{9,10},{10... | collective-permute-start | bytes 393224 | tf_op jit(solution)/shard_map/ppermute | solution.py:371
  43.8 2.8 %shard_map.67 = (f32[64,2048]{1,0:T(8,128)S(1)}, f32[64,128]{1,0:T(8,128)S(1)}) custom-call(bf16[64,1024]{1,0:T(8,128)(2,1)S(1)} %get-tuple-element.41.s0, bf16[64,2048]{1,0:T(8,128)(2,1)S(1)} %get-tuple-element.42.mid, bf16[64,1024]{1,0:T(8,128)(2,1)S(1)} %get-tuple-element.43.s1, bf16[32,1280,128]{2,1,0:T(8,128)(2,1)S(1)} %get-tuple-element.26.tiles, ...), custom_call_target="tpu_custom_call" | custom-call | flops 671088640 | tf_op jit(solution)/shard_map/pallas_call | solution.py:429
  46.6 0.0 collective-permute-done.8.r0
  46.6 0.0 collective-permute-done.9.r1
  46.6 0.7 shard_map.68
  47.3 18.9 %collective-permute-start.10 = (f32[32,128]{1,0:T(8,128)S(1)}, f32[32,128]{1,0:T(8,128)S(1)}, u32[]{:S(2)}, u32[]{:S(2)}) collective-permute-start(f32[32,128]{1,0:T(8,128)S(1)} %get-tuple-element.47), channel_id=1, source_target_pairs={{0,8},{1,9},{2,10},{3,11},{4,12},{5,13},{6,14},{7,15},{8,0},{9,1},... | collective-permute-start | bytes 49160 | tf_op jit(solution)/shard_map/ppermute | solution.py:345
  66.2 0.8 collective-permute-done.10
  67.0 10.3 %all_to_all.10 = f32[16,32,128]{2,1,0:T(8,128)S(1)} all-to-all(f32[16,32,128]{2,1,0:T(8,128)S(1)} %broadcast_in_dim.4), channel_id=1, replica_groups={{0,16,32,48,64,80,96,112,128,144,160,176,192,208,224,240},{1,17,33,49,6..., dimensions={0} | all-to-all | bytes 524288 | tf_op jit(solution)/shard_map/all_to_all | solution.py:348
  77.4 10.3 %all_to_all.11 = f32[8,32,128]{2,1,0:T(8,128)S(1)} all-to-all(f32[8,32,128]{2,1,0:T(8,128)S(1)} %broadcast_in_dim.5), channel_id=1, replica_groups=mesh['dom'=32,'board'=8] {'board'}, dimensions={0} | all-to-all | bytes 262144 | tf_op jit(solution)/shard_map/all_to_all | solution.py:350
  87.8 2.9 %collective-permute-start.11 = (f32[32,128]{1,0:T(8,128)S(1)}, f32[32,128]{1,0:T(8,128)S(1)}, u32[]{:S(2)}, u32[]{:S(2)}) collective-permute-start(f32[32,128]{1,0:T(8,128)S(1)} %reduce_sum.19.mine), channel_id=1, source_target_pairs={{0,8},{1,9},{2,10},{3,11},{4,12},{5,13},{6,14},{7,15},{8,0},{9,1},... | collective-permute-start | bytes 49160 | tf_op jit(solution)/shard_map/ppermute | solution.py:351
  90.7 0.8 collective-permute-done.11.other
  91.5 3.5 %shard_map.69 = (bf16[64,4096]{1,0:T(8,128)(2,1)}, f32[64,64]{1,0:T(8,128)}) custom-call(f32[32,128]{1,0:T(8,128)S(1)} %reduce_sum.19.mine, f32[32,128]{1,0:T(8,128)S(1)} %collective-permute-done.11.other, bf16[64,1024]{1,0:T(8,128)(2,1)S(1)} %get-tuple-element.41.s0, bf16[64,2048]{1,0:T(8,128)(2,1)S(1)} %get-tuple-element.42.mid, ...), custom_call_target="tpu_custom_call" | custom-call | flops 100663296 | tf_op jit(solution)/shard_map/pallas_call | solution.py:448
  (5 shorter events, 0.1 us)
Async XLA Ops:
  1.6 14.6 %collective-permute-start.1 = (bf16[64,1024]{1,0:T(8,128)(2,1)S(1)}, bf16[64,1024]{1,0:T(8,128)(2,1)S(1)}, u32[]{:S(2)}, u32[]{:S(2)}) collective-permute-start(bf16[64,1024]{1,0:T(8,128)(2,1)S(1)} %get-tuple-element.48.s1.old1), channel_id=1, source_target_pairs={{0,255},{1,2},{2,1},{3,4},{4,3},{5,6},{6,5},{7,8},{8,7},{9,10},{10... | collective-permute-start | bytes 393224 | tf_op jit(solution)/shard_map/ppermute | solution.py:371
  8.7 7.5 %collective-permute-start = (bf16[64,1024]{1,0:T(8,128)(2,1)S(1)}, bf16[64,1024]{1,0:T(8,128)(2,1)S(1)}, u32[]{:S(2)}, u32[]{:S(2)}) collective-permute-start(bf16[64,1024]{1,0:T(8,128)(2,1)S(1)} %get-tuple-element.49.s0.old0), channel_id=1, source_target_pairs={{0,1},{1,0},{2,3},{3,2},{4,5},{5,4},{6,7},{7,6},{8,9},{9,8},{10,11... | collective-permute-start | bytes 393224 | tf_op jit(solution)/shard_map/ppermute | solution.py:371
  16.7 5.4 %collective-permute-start.2 = (bf16[64,1024]{1,0:T(8,128)(2,1)S(1)}, bf16[64,1024]{1,0:T(8,128)(2,1)S(1)}, u32[]{:S(2)}, u32[]{:S(2)}) collective-permute-start(bf16[64,1024]{1,0:T(8,128)(2,1)S(1)} %get-tuple-element.28.s0.old0), channel_id=1, source_target_pairs={{0,1},{1,0},{2,3},{3,2},{4,5},{5,4},{6,7},{7,6},{8,9},{9,8},{10,11... | collective-permute-start | bytes 393224 | tf_op jit(solution)/shard_map/ppermute | solution.py:371
  18.6 6.5 %collective-permute-start.3 = (bf16[64,1024]{1,0:T(8,128)(2,1)S(1)}, bf16[64,1024]{1,0:T(8,128)(2,1)S(1)}, u32[]{:S(2)}, u32[]{:S(2)}) collective-permute-start(bf16[64,1024]{1,0:T(8,128)(2,1)S(1)} %get-tuple-element.30.s1.old1), channel_id=1, source_target_pairs={{0,255},{1,2},{2,1},{3,4},{4,3},{5,6},{6,5},{7,8},{8,7},{9,10},{10... | collective-permute-start | bytes 393224 | tf_op jit(solution)/shard_map/ppermute | solution.py:371
  25.6 4.4 %collective-permute-start.4 = (bf16[64,1024]{1,0:T(8,128)(2,1)S(1)}, bf16[64,1024]{1,0:T(8,128)(2,1)S(1)}, u32[]{:S(2)}, u32[]{:S(2)}) collective-permute-start(bf16[64,1024]{1,0:T(8,128)(2,1)S(1)} %get-tuple-element.33.s0.old0), channel_id=1, source_target_pairs={{0,1},{1,0},{2,3},{3,2},{4,5},{5,4},{6,7},{7,6},{8,9},{9,8},{10,11... | collective-permute-start | bytes 393224 | tf_op jit(solution)/shard_map/ppermute | solution.py:371
  25.7 6.0 %collective-permute-start.5 = (bf16[64,1024]{1,0:T(8,128)(2,1)S(1)}, bf16[64,1024]{1,0:T(8,128)(2,1)S(1)}, u32[]{:S(2)}, u32[]{:S(2)}) collective-permute-start(bf16[64,1024]{1,0:T(8,128)(2,1)S(1)} %get-tuple-element.35.s1.old1), channel_id=1, source_target_pairs={{0,255},{1,2},{2,1},{3,4},{4,3},{5,6},{6,5},{7,8},{8,7},{9,10},{10... | collective-permute-start | bytes 393224 | tf_op jit(solution)/shard_map/ppermute | solution.py:371
  32.1 5.9 %collective-permute-start.6 = (bf16[64,1024]{1,0:T(8,128)(2,1)S(1)}, bf16[64,1024]{1,0:T(8,128)(2,1)S(1)}, u32[]{:S(2)}, u32[]{:S(2)}) collective-permute-start(bf16[64,1024]{1,0:T(8,128)(2,1)S(1)} %get-tuple-element.37.s0), channel_id=1, source_target_pairs={{0,1},{1,0},{2,3},{3,2},{4,5},{5,4},{6,7},{7,6},{8,9},{9,8},{10,11... | collective-permute-start | bytes 393224 | tf_op jit(solution)/shard_map/ppermute | solution.py:371
  32.4 5.8 %collective-permute-start.7 = (bf16[64,1024]{1,0:T(8,128)(2,1)S(1)}, bf16[64,1024]{1,0:T(8,128)(2,1)S(1)}, u32[]{:S(2)}, u32[]{:S(2)}) collective-permute-start(bf16[64,1024]{1,0:T(8,128)(2,1)S(1)} %get-tuple-element.39.s1), channel_id=1, source_target_pairs={{0,255},{1,2},{2,1},{3,4},{4,3},{5,6},{6,5},{7,8},{8,7},{9,10},{10... | collective-permute-start | bytes 393224 | tf_op jit(solution)/shard_map/ppermute | solution.py:371
  38.7 7.9 %collective-permute-start.8 = (bf16[64,1024]{1,0:T(8,128)(2,1)S(1)}, bf16[64,1024]{1,0:T(8,128)(2,1)S(1)}, u32[]{:S(2)}, u32[]{:S(2)}) collective-permute-start(bf16[64,1024]{1,0:T(8,128)(2,1)S(1)} %get-tuple-element.41.s0), channel_id=1, source_target_pairs={{0,1},{1,0},{2,3},{3,2},{4,5},{5,4},{6,7},{7,6},{8,9},{9,8},{10,11... | collective-permute-start | bytes 393224 | tf_op jit(solution)/shard_map/ppermute | solution.py:371
  38.9 7.7 %collective-permute-start.9 = (bf16[64,1024]{1,0:T(8,128)(2,1)S(1)}, bf16[64,1024]{1,0:T(8,128)(2,1)S(1)}, u32[]{:S(2)}, u32[]{:S(2)}) collective-permute-start(bf16[64,1024]{1,0:T(8,128)(2,1)S(1)} %get-tuple-element.43.s1), channel_id=1, source_target_pairs={{0,255},{1,2},{2,1},{3,4},{4,3},{5,6},{6,5},{7,8},{8,7},{9,10},{10... | collective-permute-start | bytes 393224 | tf_op jit(solution)/shard_map/ppermute | solution.py:371
  47.3 19.7 %collective-permute-start.10 = (f32[32,128]{1,0:T(8,128)S(1)}, f32[32,128]{1,0:T(8,128)S(1)}, u32[]{:S(2)}, u32[]{:S(2)}) collective-permute-start(f32[32,128]{1,0:T(8,128)S(1)} %get-tuple-element.47), channel_id=1, source_target_pairs={{0,8},{1,9},{2,10},{3,11},{4,12},{5,13},{6,14},{7,15},{8,0},{9,1},... | collective-permute-start | bytes 49160 | tf_op jit(solution)/shard_map/ppermute | solution.py:345
  87.8 3.8 %collective-permute-start.11 = (f32[32,128]{1,0:T(8,128)S(1)}, f32[32,128]{1,0:T(8,128)S(1)}, u32[]{:S(2)}, u32[]{:S(2)}) collective-permute-start(f32[32,128]{1,0:T(8,128)S(1)} %reduce_sum.19.mine), channel_id=1, source_target_pairs={{0,8},{1,9},{2,10},{3,11},{4,12},{5,13},{6,14},{7,15},{8,0},{9,1},... | collective-permute-start | bytes 49160 | tf_op jit(solution)/shard_map/ppermute | solution.py:351

commit v3 on v2

--- a/solution.py
+++ b/solution.py
@@ -126,12 +126,14 @@
 
 
 def load_kernel(
-    s0, s1, block, tiles_hbm, cols_hbm, counts_hbm, place, tiles, acc, mid0, new, tab, src, raw, cols, counts, lines,
-    sems, small_sems,
+    s0, s1, block, tiles_hbm, cols_hbm, counts_hbm, tiles, acc, mid0, new, tab, src, raw, cols, counts, lines,
+    sems, small_sems, *, board,
 ):
     rows, slots = raw.shape[0], raw.shape[1]
     edge = GHOST * TB
     chunk = GROUP
+    me = lax.axis_index(AX)
+    place = (me * rows, lax.rem(me, 2), lax.rem(lax.div(me, board), 2))
     little = [
         pltpu.make_async_copy(cols_hbm, cols, small_sems.at[0]),
         pltpu.make_async_copy(counts_hbm, counts, small_sems.at[1]),
@@ -257,7 +259,7 @@
 
 def eliminate(gram):
     size = gram.shape[0]
-    step, sub = 4, 8
+    step, sub = 8, 8
     lanes = lax.broadcasted_iota(jnp.int32, (sub, 2 * size), 1)
     inner = lax.broadcasted_iota(jnp.int32, (sub, 2 * size), 0)
     wide = jnp.concatenate([gram, jnp.zeros_like(gram)], axis=1)
@@ -361,13 +363,12 @@
     shape = jax.ShapeDtypeStruct
     me = lax.axis_index(AX)
     odd = me % 2
-    core = (me // board) % 2
-    place = jnp.stack([me * rows, odd, core]).astype(jnp.int32)
 
     even_pairs = [(i, i ^ 1) for i in range(devices)]
     odd_pairs = [(i, (((i + 1) ^ 1) - 1) % devices) for i in range(devices)]
-
-    def exchange(s0, s1):
+    last_pairs = [(0, 0)] + odd_pairs[1:-1] + [(devices - 1, devices - 1)]
+
+    def exchange(s0, s1, odd_pairs=odd_pairs):
         return lax.ppermute(s0, AX, even_pairs), lax.ppermute(s1, AX, odd_pairs)
 
     head, tail = block[:, :edge], block[:, wide - edge :]
@@ -383,9 +384,9 @@
     halo_scratch = [pltpu.VMEM((size, 2 * edge + TB), bf16), pltpu.VMEM((size, 2 * edge), f32)]
 
     tiles_v, acc, mid, new, tab = call(
-        load_kernel,
+        functools.partial(load_kernel, board=board),
         [shape((rows, slots * TB, TB), bf16), acc_shape, mid_shape, mid_shape, pltpu.SMEM(TABLE, jnp.int32)],
-        [VM, VM, HBM, HBM, HBM, HBM, SM],
+        [VM, VM, HBM, HBM, HBM, HBM],
         [VM, VM, VM, VM, SM],
         [
             field,
@@ -399,7 +400,7 @@
         limit=40,
         flops=own_flops,
         bytes_=tiles.size * 2,
-    )(s0, s1, *(stay(v) for v in (block, tiles, cols.T, counts.reshape(1, rows))), place)
+    )(s0, s1, *(stay(v) for v in (block, tiles, cols.T, counts.reshape(1, rows))))
 
     tab = pltpu.with_memory_space_constraint(tab, pltpu.SMEM)
     older = (s0, mid, s1)
@@ -415,7 +416,7 @@
             flops=halo_flops,
         )(acc, old0, old1, r0, r1, tiles_v, tab)
         mid = new
-        r0, r1 = exchange(s0, s1)
+        r0, r1 = exchange(s0, s1, odd_pairs if degree < DEG - 1 else last_pairs)
         if degree < DEG - 1:
             acc, new = call(
                 functools.partial(own_kernel, slots=slots),

time: 95.1 us -> 93.5 us (0.983)
  starting transfers between devices: 42.3 us -> 34.6 us
  blocking collectives: 20.7 us -> 24.2 us
  Pallas kernels: 23.7 us -> 25.2 us
  waiting for transfers between devices: 6.49 us -> 7.6 us
    ppermute x1, starting transfers between devices: 18.9 us -> 13 us  [all_sum(): x = keep + lax.ppermute(give, AX, swap)]
    all_to_all x1, blocking collectives: 10.3 us -> 13.9 us  [all_sum(): x = lax.all_to_all(spread, AX, 0, 0, axis_index_groups=planes).sum(0)]
    pallas_call x4, Pallas kernels: 1.83 us -> 4.02 us  [body(): call(functools.partial(halo_kernel, cheb=degree > 0, slots=slots), [edge_...]
    ppermute x10, starting transfers between devices: 20.5 us -> 18.5 us  [exchange(): return (lax.ppermute(s0, AX, even_pairs), lax.ppermute(s1, AX, odd_pairs))]
    ppermute x10, waiting for transfers between devices: 4.81 us -> 5.92 us  [exchange(): return (lax.ppermute(s0, AX, even_pairs), lax.ppermute(s1, AX, odd_pairs))]
  transfers between devices with their start and end apart: 12 -> 12, of which waited for: 5 -> 5; matrix products, arithmetic and copies ran while one was open for 0% -> 0% of each run, Pallas kernels for 19% -> 18%
where the time goes in v3:
time: 93.5 us
  starting transfers between devices  34.6 us (37%)
  Pallas kernels  25.2 us (27%)
  blocking collectives  24.2 us (26%)
  waiting for transfers between devices  7.6 us (8%)
  other arithmetic  1.03 us (1%)
    ppermute x10, starting transfers between devices, exchange(): return (lax.ppermute(s0, AX, even_pairs), lax.ppermute(s1, AX, odd_pairs))  18.5 us
    all_to_all x1, blocking collectives, all_sum(): x = lax.all_to_all(spread, AX, 0, 0, axis_index_groups=planes).sum(0)  13.9 us
    ppermute x1, starting transfers between devices, all_sum(): x = keep + lax.ppermute(give, AX, swap)  13 us
    all_to_all x1, blocking collectives, all_sum(): x = lax.all_to_all(spread, 'board', 0, 0).sum(0)  10.3 us
    pallas_call x3, Pallas kernels, body(): call(functools.partial(own_kernel, slots=slots), [acc_shape, mid_shape],...  7.28 us
    pallas_call x1, Pallas kernels, body(): call(functools.partial(load_kernel, board=board), [shape((rows, slots * T...  6.9 us
    ppermute x10, waiting for transfers between devices, exchange(): return (lax.ppermute(s0, AX, even_pairs), lax.ppermute(s1, AX, odd_pairs))  5.92 us
    pallas_call x4, Pallas kernels, body(): call(functools.partial(halo_kernel, cheb=degree > 0, slots=slots), [edge_...  4.02 us
  transfers between devices with their start and end apart: 12, of which 5 were waited for; matrix products, arithmetic and copies ran while one was open for 0% of the time, Pallas kernels for 18%

profile of v3, /device:TPU:1, one launch (start us, length us, event | category | flops | bytes accessed | tf_op | source)
XLA Modules:
  0.0 93.5 jit_solution(16158891996745306005)
XLA Ops:
  0.6 1.0 %broadcast_select_fusion = (bf16[64,1024]{1,0:T(8,128)(2,1)S(1)}, bf16[64,1024]{1,0:T(8,128)(2,1)S(1)}) fusion(pred[]{:T(512)S(6)} %eq.6, bf16[64,4096]{1,0:T(8,128)(2,1)} %block.1), kind=kLoop, calls=%fused_computation | loop fusion | flops 131072 | bytes 524289 | tf_op jit(solution)/shard_map/jit(_where)/select_n | solution.py:375
  1.6 7.1 %collective-permute-start.1 = (bf16[64,1024]{1,0:T(8,128)(2,1)S(1)}, bf16[64,1024]{1,0:T(8,128)(2,1)S(1)}, u32[]{:S(2)}, u32[]{:S(2)}) collective-permute-start(bf16[64,1024]{1,0:T(8,128)(2,1)S(1)} %get-tuple-element.48.s1.old1), channel_id=1, source_target_pairs={{0,255},{1,2},{2,1},{3,4},{4,3},{5,6},{6,5},{7,8},{8,7},{9,10},{10... | collective-permute-start | bytes 393224 | tf_op jit(solution)/shard_map/ppermute | solution.py:372
  8.7 0.0 collective-permute-start
  8.7 6.9 %shard_map.59 = (bf16[32,1280,128]{2,1,0:T(8,128)(2,1)S(1)}, f32[64,2048]{1,0:T(8,128)S(1)}, bf16[64,2048]{1,0:T(8,128)(2,1)S(1)}, bf16[64,2048]{1,0:T(8,128)(2,1)S(1)}, s32[32,128]{1,0:T(8,128)S(4)}) custom-call(bf16[64,1024]{1,0:T(8,128)(2,1)S(1)} %get-tuple-element.49.s0.old0, bf16[64,1024]{1,0:T(8,128)(2,1)S(1)} %get-tuple-element.48.s1.old1, ...), custom_call_target="tpu_custom_call" | custom-call | flops 671088640 | bytes 10485760 | tf_op jit(solution)/shard_map/pallas_call | solution.py:386
  15.6 0.0 collective-permute-done.1.r1
  15.6 0.0 collective-permute-done.r0
  15.6 1.0 %shard_map.60 = (bf16[64,1024]{1,0:T(8,128)(2,1)S(1)}, bf16[64,1024]{1,0:T(8,128)(2,1)S(1)}) custom-call(f32[64,2048]{1,0:T(8,128)S(1)} %get-tuple-element.25.acc, bf16[64,1024]{1,0:T(8,128)(2,1)S(1)} %get-tuple-element.49.s0.old0, bf16[64,1024]{1,0:T(8,128)(2,1)S(1)} %get-tuple-element.48.s1.old1, bf16[64,1024]{1,0:T(8,128)(2,1)S(1)} %collective-permute-done.r0, ...), custom_call_target="tpu_custom_call" | custom-call | flops 83886080 | tf_op jit(solution)/shard_map/pallas_call | solution.py:410
  16.6 1.0 %collective-permute-start.2 = (bf16[64,1024]{1,0:T(8,128)(2,1)S(1)}, bf16[64,1024]{1,0:T(8,128)(2,1)S(1)}, u32[]{:S(2)}, u32[]{:S(2)}) collective-permute-start(bf16[64,1024]{1,0:T(8,128)(2,1)S(1)} %get-tuple-element.28.s0.old0), channel_id=1, source_target_pairs={{0,1},{1,0},{2,3},{3,2},{4,5},{5,4},{6,7},{7,6},{8,9},{9,8},{10,11... | collective-permute-start | bytes 393224 | tf_op jit(solution)/shard_map/ppermute | solution.py:372
  17.6 1.0 %collective-permute-start.3 = (bf16[64,1024]{1,0:T(8,128)(2,1)S(1)}, bf16[64,1024]{1,0:T(8,128)(2,1)S(1)}, u32[]{:S(2)}, u32[]{:S(2)}) collective-permute-start(bf16[64,1024]{1,0:T(8,128)(2,1)S(1)} %get-tuple-element.30.s1.old1), channel_id=1, source_target_pairs={{0,255},{1,2},{2,1},{3,4},{4,3},{5,6},{6,5},{7,8},{8,7},{9,10},{10... | collective-permute-start | bytes 393224 | tf_op jit(solution)/shard_map/ppermute | solution.py:372
  18.6 2.4 %shard_map.61 = (f32[64,2048]{1,0:T(8,128)S(1)}, bf16[64,2048]{1,0:T(8,128)(2,1)S(1)}) custom-call(bf16[64,1024]{1,0:T(8,128)(2,1)S(1)} %get-tuple-element.28.s0.old0, bf16[64,2048]{1,0:T(8,128)(2,1)S(1)} %get-tuple-element.29.mid.old, bf16[64,1024]{1,0:T(8,128)(2,1)S(1)} %get-tuple-element.30.s1.old1, bf16[64,2048]{1,0:T(8,128)(2,1)S(1)} %get-tuple-element.31.old, ...), custom_call_target="tpu_custom_call" | custom-call | flops 671088640 | tf_op jit(solution)/shard_map/pallas_call | solution.py:421
  21.1 0.0 collective-permute-done.2.r0
  21.1 2.4 %collective-permute-done.3.r1 = bf16[64,1024]{1,0:T(8,128)(2,1)S(1)} collective-permute-done((bf16[64,1024]{1,0:T(8,128)(2,1)S(1)}, bf16[64,1024]{1,0:T(8,128)(2,1)S(1)}, u32[]{:S(2)}, u32[]{:S(2)}) %collective-permute-start.3) | collective-permute-done | bytes 131104 | tf_op jit(solution)/shard_map/ppermute | solution.py:372
  23.4 1.0 %shard_map.62 = (bf16[64,1024]{1,0:T(8,128)(2,1)S(1)}, bf16[64,1024]{1,0:T(8,128)(2,1)S(1)}) custom-call(f32[64,2048]{1,0:T(8,128)S(1)} %get-tuple-element.32.acc, bf16[64,1024]{1,0:T(8,128)(2,1)S(1)} %get-tuple-element.49.s0.old0, bf16[64,1024]{1,0:T(8,128)(2,1)S(1)} %get-tuple-element.48.s1.old1, bf16[64,1024]{1,0:T(8,128)(2,1)S(1)} %collective-permute-done.2.r0, ...), custom_call_target="tpu_custom_call" | custom-call | flops 83886080 | tf_op jit(solution)/shard_map/pallas_call | solution.py:410
  24.5 0.1 collective-permute-start.4
  24.6 1.5 %collective-permute-start.5 = (bf16[64,1024]{1,0:T(8,128)(2,1)S(1)}, bf16[64,1024]{1,0:T(8,128)(2,1)S(1)}, u32[]{:S(2)}, u32[]{:S(2)}) collective-permute-start(bf16[64,1024]{1,0:T(8,128)(2,1)S(1)} %get-tuple-element.35.s1.old1), channel_id=1, source_target_pairs={{0,255},{1,2},{2,1},{3,4},{4,3},{5,6},{6,5},{7,8},{8,7},{9,10},{10... | collective-permute-start | bytes 393224 | tf_op jit(solution)/shard_map/ppermute | solution.py:372
  26.1 2.4 %shard_map.63 = (f32[64,2048]{1,0:T(8,128)S(1)}, bf16[64,2048]{1,0:T(8,128)(2,1)S(1)}) custom-call(bf16[64,1024]{1,0:T(8,128)(2,1)S(1)} %get-tuple-element.33.s0.old0, bf16[64,2048]{1,0:T(8,128)(2,1)S(1)} %get-tuple-element.34.mid.old, bf16[64,1024]{1,0:T(8,128)(2,1)S(1)} %get-tuple-element.35.s1.old1, bf16[64,2048]{1,0:T(8,128)(2,1)S(1)} %get-tuple-element.29.mid.old, ...), custom_call_target="tpu_custom_call" | custom-call | flops 671088640 | tf_op jit(solution)/shard_map/pallas_call | solution.py:421
  28.5 0.0 collective-permute-done.4.r0
  28.5 2.0 %collective-permute-done.5.r1 = bf16[64,1024]{1,0:T(8,128)(2,1)S(1)} collective-permute-done((bf16[64,1024]{1,0:T(8,128)(2,1)S(1)}, bf16[64,1024]{1,0:T(8,128)(2,1)S(1)}, u32[]{:S(2)}, u32[]{:S(2)}) %collective-permute-start.5) | collective-permute-done | bytes 131104 | tf_op jit(solution)/shard_map/ppermute | solution.py:372
  30.5 1.0 %shard_map.64 = (bf16[64,1024]{1,0:T(8,128)(2,1)S(1)}, bf16[64,1024]{1,0:T(8,128)(2,1)S(1)}) custom-call(f32[64,2048]{1,0:T(8,128)S(1)} %get-tuple-element.36.acc, bf16[64,1024]{1,0:T(8,128)(2,1)S(1)} %get-tuple-element.28.s0.old0, bf16[64,1024]{1,0:T(8,128)(2,1)S(1)} %get-tuple-element.30.s1.old1, bf16[64,1024]{1,0:T(8,128)(2,1)S(1)} %collective-permute-done.4.r0, ...), custom_call_target="tpu_custom_call" | custom-call | flops 83886080 | tf_op jit(solution)/shard_map/pallas_call | solution.py:410
  31.6 0.3 collective-permute-start.6
  31.8 1.7 %collective-permute-start.7 = (bf16[64,1024]{1,0:T(8,128)(2,1)S(1)}, bf16[64,1024]{1,0:T(8,128)(2,1)S(1)}, u32[]{:S(2)}, u32[]{:S(2)}) collective-permute-start(bf16[64,1024]{1,0:T(8,128)(2,1)S(1)} %get-tuple-element.39.s1), channel_id=1, source_target_pairs={{0,255},{1,2},{2,1},{3,4},{4,3},{5,6},{6,5},{7,8},{8,7},{9,10},{10... | collective-permute-start | bytes 393224 | tf_op jit(solution)/shard_map/ppermute | solution.py:372
  33.6 2.4 %shard_map.65 = (f32[64,2048]{1,0:T(8,128)S(1)}, bf16[64,2048]{1,0:T(8,128)(2,1)S(1)}) custom-call(bf16[64,1024]{1,0:T(8,128)(2,1)S(1)} %get-tuple-element.37.s0, bf16[64,2048]{1,0:T(8,128)(2,1)S(1)} %get-tuple-element.38.mid, bf16[64,1024]{1,0:T(8,128)(2,1)S(1)} %get-tuple-element.39.s1, bf16[64,2048]{1,0:T(8,128)(2,1)S(1)} %get-tuple-element.34.mid.old, ...), custom_call_target="tpu_custom_call" | custom-call | flops 671088640 | tf_op jit(solution)/shard_map/pallas_call | solution.py:421
  36.0 0.0 collective-permute-done.6.r0
  36.0 1.5 %collective-permute-done.7.r1 = bf16[64,1024]{1,0:T(8,128)(2,1)S(1)} collective-permute-done((bf16[64,1024]{1,0:T(8,128)(2,1)S(1)}, bf16[64,1024]{1,0:T(8,128)(2,1)S(1)}, u32[]{:S(2)}, u32[]{:S(2)}) %collective-permute-start.7) | collective-permute-done | bytes 131104 | tf_op jit(solution)/shard_map/ppermute | solution.py:372
  37.5 1.0 %shard_map.66 = (bf16[64,1024]{1,0:T(8,128)(2,1)S(1)}, bf16[64,1024]{1,0:T(8,128)(2,1)S(1)}) custom-call(f32[64,2048]{1,0:T(8,128)S(1)} %get-tuple-element.40.acc, bf16[64,1024]{1,0:T(8,128)(2,1)S(1)} %get-tuple-element.33.s0.old0, bf16[64,1024]{1,0:T(8,128)(2,1)S(1)} %get-tuple-element.35.s1.old1, bf16[64,1024]{1,0:T(8,128)(2,1)S(1)} %collective-permute-done.6.r0, ...), custom_call_target="tpu_custom_call" | custom-call | flops 83886080 | tf_op jit(solution)/shard_map/pallas_call | solution.py:410
  38.6 0.1 collective-permute-start.8
  38.7 5.7 %collective-permute-start.9 = (bf16[64,1024]{1,0:T(8,128)(2,1)S(1)}, bf16[64,1024]{1,0:T(8,128)(2,1)S(1)}, u32[]{:S(2)}, u32[]{:S(2)}) collective-permute-start(bf16[64,1024]{1,0:T(8,128)(2,1)S(1)} %get-tuple-element.43.s1), channel_id=1, source_target_pairs={{0,0},{1,2},{2,1},{3,4},{4,3},{5,6},{6,5},{7,8},{8,7},{9,10},{10,9... | collective-permute-start | bytes 393224 | tf_op jit(solution)/shard_map/ppermute | solution.py:372
  44.4 2.7 %shard_map.67 = (f32[64,2048]{1,0:T(8,128)S(1)}, f32[64,128]{1,0:T(8,128)S(1)}) custom-call(bf16[64,1024]{1,0:T(8,128)(2,1)S(1)} %get-tuple-element.41.s0, bf16[64,2048]{1,0:T(8,128)(2,1)S(1)} %get-tuple-element.42.mid, bf16[64,1024]{1,0:T(8,128)(2,1)S(1)} %get-tuple-element.43.s1, bf16[32,1280,128]{2,1,0:T(8,128)(2,1)S(1)} %get-tuple-element.26.tiles, ...), custom_call_target="tpu_custom_call" | custom-call | flops 671088640 | tf_op jit(solution)/shard_map/pallas_call | solution.py:430
  47.1 0.0 collective-permute-done.8.r0
  47.1 0.0 collective-permute-done.9.r1
  47.1 1.2 %shard_map.68 = (f32[32,128]{1,0:T(8,128)S(1)}, f32[32,128]{1,0:T(8,128)S(1)}) custom-call(f32[64,2048]{1,0:T(8,128)S(1)} %get-tuple-element.44.acc, bf16[64,1024]{1,0:T(8,128)(2,1)S(1)} %get-tuple-element.41.s0, bf16[64,1024]{1,0:T(8,128)(2,1)S(1)} %get-tuple-element.43.s1, bf16[64,1024]{1,0:T(8,128)(2,1)S(1)} %collective-permute-done.8.r0, ...), custom_call_target="tpu_custom_call" | custom-call | flops 83886080 | tf_op jit(solution)/shard_map/pallas_call | solution.py:440
  48.4 13.0 %collective-permute-start.10 = (f32[32,128]{1,0:T(8,128)S(1)}, f32[32,128]{1,0:T(8,128)S(1)}, u32[]{:S(2)}, u32[]{:S(2)}) collective-permute-start(f32[32,128]{1,0:T(8,128)S(1)} %get-tuple-element.47), channel_id=1, source_target_pairs={{0,8},{1,9},{2,10},{3,11},{4,12},{5,13},{6,14},{7,15},{8,0},{9,1},... | collective-permute-start | bytes 49160 | tf_op jit(solution)/shard_map/ppermute | solution.py:347
  61.4 0.8 collective-permute-done.10
  62.3 13.9 %all_to_all.10 = f32[16,32,128]{2,1,0:T(8,128)S(1)} all-to-all(f32[16,32,128]{2,1,0:T(8,128)S(1)} %broadcast_in_dim.4), channel_id=1, replica_groups={{0,16,32,48,64,80,96,112,128,144,160,176,192,208,224,240},{1,17,33,49,6..., dimensions={0} | all-to-all | bytes 524288 | tf_op jit(solution)/shard_map/all_to_all | solution.py:350
  76.2 10.3 %all_to_all.11 = f32[8,32,128]{2,1,0:T(8,128)S(1)} all-to-all(f32[8,32,128]{2,1,0:T(8,128)S(1)} %broadcast_in_dim.5), channel_id=1, replica_groups=mesh['dom'=32,'board'=8] {'board'}, dimensions={0} | all-to-all | bytes 262144 | tf_op jit(solution)/shard_map/all_to_all | solution.py:352
  86.5 3.1 %collective-permute-start.11 = (f32[32,128]{1,0:T(8,128)S(1)}, f32[32,128]{1,0:T(8,128)S(1)}, u32[]{:S(2)}, u32[]{:S(2)}) collective-permute-start(f32[32,128]{1,0:T(8,128)S(1)} %reduce_sum.19.mine), channel_id=1, source_target_pairs={{0,8},{1,9},{2,10},{3,11},{4,12},{5,13},{6,14},{7,15},{8,0},{9,1},... | collective-permute-start | bytes 49160 | tf_op jit(solution)/shard_map/ppermute | solution.py:353
  89.6 0.8 collective-permute-done.11.other
  90.5 3.0 %shard_map.69 = (bf16[64,4096]{1,0:T(8,128)(2,1)}, f32[64,64]{1,0:T(8,128)}) custom-call(f32[32,128]{1,0:T(8,128)S(1)} %reduce_sum.19.mine, f32[32,128]{1,0:T(8,128)S(1)} %collective-permute-done.11.other, bf16[64,1024]{1,0:T(8,128)(2,1)S(1)} %get-tuple-element.41.s0, bf16[64,2048]{1,0:T(8,128)(2,1)S(1)} %get-tuple-element.42.mid, ...), custom_call_target="tpu_custom_call" | custom-call | flops 100663296 | tf_op jit(solution)/shard_map/pallas_call | solution.py:449
  (5 shorter events, 0.1 us)
Async XLA Ops:
  1.6 14.0 %collective-permute-start.1 = (bf16[64,1024]{1,0:T(8,128)(2,1)S(1)}, bf16[64,1024]{1,0:T(8,128)(2,1)S(1)}, u32[]{:S(2)}, u32[]{:S(2)}) collective-permute-start(bf16[64,1024]{1,0:T(8,128)(2,1)S(1)} %get-tuple-element.48.s1.old1), channel_id=1, source_target_pairs={{0,255},{1,2},{2,1},{3,4},{4,3},{5,6},{6,5},{7,8},{8,7},{9,10},{10... | collective-permute-start | bytes 393224 | tf_op jit(solution)/shard_map/ppermute | solution.py:372
  8.7 6.9 %collective-permute-start = (bf16[64,1024]{1,0:T(8,128)(2,1)S(1)}, bf16[64,1024]{1,0:T(8,128)(2,1)S(1)}, u32[]{:S(2)}, u32[]{:S(2)}) collective-permute-start(bf16[64,1024]{1,0:T(8,128)(2,1)S(1)} %get-tuple-element.49.s0.old0), channel_id=1, source_target_pairs={{0,1},{1,0},{2,3},{3,2},{4,5},{5,4},{6,7},{7,6},{8,9},{9,8},{10,11... | collective-permute-start | bytes 393224 | tf_op jit(solution)/shard_map/ppermute | solution.py:372
  16.6 4.5 %collective-permute-start.2 = (bf16[64,1024]{1,0:T(8,128)(2,1)S(1)}, bf16[64,1024]{1,0:T(8,128)(2,1)S(1)}, u32[]{:S(2)}, u32[]{:S(2)}) collective-permute-start(bf16[64,1024]{1,0:T(8,128)(2,1)S(1)} %get-tuple-element.28.s0.old0), channel_id=1, source_target_pairs={{0,1},{1,0},{2,3},{3,2},{4,5},{5,4},{6,7},{7,6},{8,9},{9,8},{10,11... | collective-permute-start | bytes 393224 | tf_op jit(solution)/shard_map/ppermute | solution.py:372
  17.6 5.8 %collective-permute-start.3 = (bf16[64,1024]{1,0:T(8,128)(2,1)S(1)}, bf16[64,1024]{1,0:T(8,128)(2,1)S(1)}, u32[]{:S(2)}, u32[]{:S(2)}) collective-permute-start(bf16[64,1024]{1,0:T(8,128)(2,1)S(1)} %get-tuple-element.30.s1.old1), channel_id=1, source_target_pairs={{0,255},{1,2},{2,1},{3,4},{4,3},{5,6},{6,5},{7,8},{8,7},{9,10},{10... | collective-permute-start | bytes 393224 | tf_op jit(solution)/shard_map/ppermute | solution.py:372
  24.5 4.0 %collective-permute-start.4 = (bf16[64,1024]{1,0:T(8,128)(2,1)S(1)}, bf16[64,1024]{1,0:T(8,128)(2,1)S(1)}, u32[]{:S(2)}, u32[]{:S(2)}) collective-permute-start(bf16[64,1024]{1,0:T(8,128)(2,1)S(1)} %get-tuple-element.33.s0.old0), channel_id=1, source_target_pairs={{0,1},{1,0},{2,3},{3,2},{4,5},{5,4},{6,7},{7,6},{8,9},{9,8},{10,11... | collective-permute-start | bytes 393224 | tf_op jit(solution)/shard_map/ppermute | solution.py:372
  24.6 6.0 %collective-permute-start.5 = (bf16[64,1024]{1,0:T(8,128)(2,1)S(1)}, bf16[64,1024]{1,0:T(8,128)(2,1)S(1)}, u32[]{:S(2)}, u32[]{:S(2)}) collective-permute-start(bf16[64,1024]{1,0:T(8,128)(2,1)S(1)} %get-tuple-element.35.s1.old1), channel_id=1, source_target_pairs={{0,255},{1,2},{2,1},{3,4},{4,3},{5,6},{6,5},{7,8},{8,7},{9,10},{10... | collective-permute-start | bytes 393224 | tf_op jit(solution)/shard_map/ppermute | solution.py:372
  31.6 4.4 %collective-permute-start.6 = (bf16[64,1024]{1,0:T(8,128)(2,1)S(1)}, bf16[64,1024]{1,0:T(8,128)(2,1)S(1)}, u32[]{:S(2)}, u32[]{:S(2)}) collective-permute-start(bf16[64,1024]{1,0:T(8,128)(2,1)S(1)} %get-tuple-element.37.s0), channel_id=1, source_target_pairs={{0,1},{1,0},{2,3},{3,2},{4,5},{5,4},{6,7},{7,6},{8,9},{9,8},{10,11... | collective-permute-start | bytes 393224 | tf_op jit(solution)/shard_map/ppermute | solution.py:372
  31.8 5.7 %collective-permute-start.7 = (bf16[64,1024]{1,0:T(8,128)(2,1)S(1)}, bf16[64,1024]{1,0:T(8,128)(2,1)S(1)}, u32[]{:S(2)}, u32[]{:S(2)}) collective-permute-start(bf16[64,1024]{1,0:T(8,128)(2,1)S(1)} %get-tuple-element.39.s1), channel_id=1, source_target_pairs={{0,255},{1,2},{2,1},{3,4},{4,3},{5,6},{6,5},{7,8},{8,7},{9,10},{10... | collective-permute-start | bytes 393224 | tf_op jit(solution)/shard_map/ppermute | solution.py:372
  38.6 8.5 %collective-permute-start.8 = (bf16[64,1024]{1,0:T(8,128)(2,1)S(1)}, bf16[64,1024]{1,0:T(8,128)(2,1)S(1)}, u32[]{:S(2)}, u32[]{:S(2)}) collective-permute-start(bf16[64,1024]{1,0:T(8,128)(2,1)S(1)} %get-tuple-element.41.s0), channel_id=1, source_target_pairs={{0,1},{1,0},{2,3},{3,2},{4,5},{5,4},{6,7},{7,6},{8,9},{9,8},{10,11... | collective-permute-start | bytes 393224 | tf_op jit(solution)/shard_map/ppermute | solution.py:372
  38.7 8.5 %collective-permute-start.9 = (bf16[64,1024]{1,0:T(8,128)(2,1)S(1)}, bf16[64,1024]{1,0:T(8,128)(2,1)S(1)}, u32[]{:S(2)}, u32[]{:S(2)}) collective-permute-start(bf16[64,1024]{1,0:T(8,128)(2,1)S(1)} %get-tuple-element.43.s1), channel_id=1, source_target_pairs={{0,0},{1,2},{2,1},{3,4},{4,3},{5,6},{6,5},{7,8},{8,7},{9,10},{10,9... | collective-permute-start | bytes 393224 | tf_op jit(solution)/shard_map/ppermute | solution.py:372
  48.4 13.9 %collective-permute-start.10 = (f32[32,128]{1,0:T(8,128)S(1)}, f32[32,128]{1,0:T(8,128)S(1)}, u32[]{:S(2)}, u32[]{:S(2)}) collective-permute-start(f32[32,128]{1,0:T(8,128)S(1)} %get-tuple-element.47), channel_id=1, source_target_pairs={{0,8},{1,9},{2,10},{3,11},{4,12},{5,13},{6,14},{7,15},{8,0},{9,1},... | collective-permute-start | bytes 49160 | tf_op jit(solution)/shard_map/ppermute | solution.py:347
  86.5 3.9 %collective-permute-start.11 = (f32[32,128]{1,0:T(8,128)S(1)}, f32[32,128]{1,0:T(8,128)S(1)}, u32[]{:S(2)}, u32[]{:S(2)}) collective-permute-start(f32[32,128]{1,0:T(8,128)S(1)} %reduce_sum.19.mine), channel_id=1, source_target_pairs={{0,8},{1,9},{2,10},{3,11},{4,12},{5,13},{6,14},{7,15},{8,0},{9,1},... | collective-permute-start | bytes 49160 | tf_op jit(solution)/shard_map/ppermute | solution.py:353

commit v4 on v3

--- a/solution.py
+++ b/solution.py
@@ -173,12 +173,12 @@
     )
 
 
-def own_kernel(s0, mid, s1, old, tiles, tab, acc, new, src, *, slots):
+def own_kernel(s1, mid, s0, old, tiles, tab, acc, new, src, *, slots):
     gather_field(src, s0, mid, s1)
     own_products(src, held_pairs(tiles), tab, old, acc, new, True, slots, tiles.shape[0])
 
 
-def own_last_kernel(s0, mid, s1, tiles, tab, acc, both, src, new, *, slots):
+def own_last_kernel(s1, mid, s0, tiles, tab, acc, both, src, new, *, slots):
     gather_field(src, s0, mid, s1)
     own_products(src, held_pairs(tiles), tab, None, acc, new, False, slots, tiles.shape[0])
     edge, inner = s0.shape[1], mid.shape[1]
@@ -232,7 +232,7 @@
         lax.fori_loop(1, lax.div(need + 1, 2), more, 0)
 
 
-def halo_kernel(acc, old0, old1, r0, r1, tiles, tab, s0, s1, halo, sums, *, cheb, slots):
+def halo_kernel(acc, old0, old1, r0, r1, tiles, tab, s1, s0, halo, sums, *, cheb, slots):
     edge = GHOST * TB
     halo_products(acc, r0, r1, tiles, tab, halo, sums, slots)
     for side, old, new in ((0, old0, s0), (1, old1, s1)):
@@ -369,7 +369,9 @@
     last_pairs = [(0, 0)] + odd_pairs[1:-1] + [(devices - 1, devices - 1)]
 
     def exchange(s0, s1, odd_pairs=odd_pairs):
-        return lax.ppermute(s0, AX, even_pairs), lax.ppermute(s1, AX, odd_pairs)
+        r1 = lax.ppermute(s1, AX, odd_pairs)
+        r0 = lax.ppermute(s0, AX, even_pairs)
+        return r0, r1
 
     head, tail = block[:, :edge], block[:, wide - edge :]
     s0, s1 = jnp.where(odd == 1, head, tail), jnp.where(odd == 1, tail, head)
@@ -407,7 +409,7 @@
     for degree in range(DEG):
         old0, old_mid, old1 = older
         older = (s0, mid, s1)
-        s0, s1 = call(
+        s1, s0 = call(
             functools.partial(halo_kernel, cheb=degree > 0, slots=slots),
             [edge_shape, edge_shape],
             [VM, VM, VM, VM, VM, VM, SM],
@@ -425,7 +427,7 @@
                 [VM, VM],
                 [field],
                 flops=own_flops,
-            )(s0, mid, s1, older[1], tiles_v, tab)
+            )(s1, mid, s0, older[1], tiles_v, tab)
         else:
             acc, both = call(
                 functools.partial(own_last_kernel, slots=slots),
@@ -434,7 +436,7 @@
                 [VM, VM],
                 [field, pltpu.VMEM((size, inner), bf16)],
                 flops=own_flops,
-            )(s0, mid, s1, tiles_v, tab)
+            )(s1, mid, s0, tiles_v, tab)
 
     half_shape = shape((size // 2, 2 * size), f32)
     keep, give = call(

time: 93.5 us -> 91.1 us (0.974); the launches traced: 93.5 us -> 89.9 us
  Pallas kernels: 25.2 us -> 22.4 us
  blocking collectives: 24.2 us -> 21.4 us
  waiting for transfers between devices: 7.6 us -> 9.41 us
    ppermute x10, starting transfers between devices: 18.5 us -> 21.3 us  [the longest x5 21.1 us: exchange(): r1 = lax.ppermute(s1, AX, odd_pairs)]
    all_to_all x1, blocking collectives: 13.9 us -> 11.1 us  [all_sum(): x = lax.all_to_all(spread, AX, 0, 0, axis_index_groups=planes).sum(0)]
    ppermute x1, starting transfers between devices: 13 us -> 10.4 us  [all_sum(): x = keep + lax.ppermute(give, AX, swap)]
    pallas_call x4, Pallas kernels: 4.02 us -> 1.82 us  [body(): call(functools.partial(halo_kernel, cheb=degree > 0, slots=slots), [edge_...]
    ppermute x10, waiting for transfers between devices: 5.92 us -> 7.73 us  [the longest x5 5.22 us: exchange(): r1 = lax.ppermute(s1, AX, odd_pairs)]
  transfers between devices with their start and end apart: 12 -> 12, of which waited for: 5 -> 9; matrix products, arithmetic and copies ran while one was open for 0% -> 0% of each run, Pallas kernels for 18% -> 19%
where the time goes in v4:
time: 91.1 us; the launch traced here: 89.9 us
  starting transfers between devices  34.8 us (38%)
  Pallas kernels  22.4 us (25%)
  blocking collectives  21.4 us (23%)
  waiting for transfers between devices  9.41 us (10%)
  other arithmetic  1.03 us (1%)
    ppermute x5, starting transfers between devices, exchange(): r1 = lax.ppermute(s1, AX, odd_pairs)  21.1 us
    all_to_all x1, blocking collectives, all_sum(): x = lax.all_to_all(spread, AX, 0, 0, axis_index_groups=planes).sum(0)  11.1 us
    ppermute x1, starting transfers between devices, all_sum(): x = keep + lax.ppermute(give, AX, swap)  10.4 us
    all_to_all x1, blocking collectives, all_sum(): x = lax.all_to_all(spread, 'board', 0, 0).sum(0)  10.3 us
    pallas_call x3, Pallas kernels, body(): call(functools.partial(own_kernel, slots=slots), [acc_shape, mid_shape],...  7.32 us
    pallas_call x1, Pallas kernels, body(): call(functools.partial(load_kernel, board=board), [shape((rows, slots * T...  6.89 us
    ppermute x5, waiting for transfers between devices, exchange(): r1 = lax.ppermute(s1, AX, odd_pairs)  5.22 us
    ppermute x1, starting transfers between devices, all_sum(): return (x, lax.ppermute(x, AX, swap))  3.09 us
  transfers between devices with their start and end apart: 12, of which 9 were waited for; matrix products, arithmetic and copies ran while one was open for 0% of the time, Pallas kernels for 19%

profile of v4, /device:TPU:1, one launch (start us, length us, event | category | flops | bytes accessed | tf_op | source)
XLA Modules:
  0.0 89.9 jit_solution(3918743910826478500)
XLA Ops:
  0.6 1.0 %broadcast_select_fusion = (bf16[64,1024]{1,0:T(8,128)(2,1)S(1)}, bf16[64,1024]{1,0:T(8,128)(2,1)S(1)}) fusion(pred[]{:T(512)S(6)} %eq.6, bf16[64,4096]{1,0:T(8,128)(2,1)} %block.1), kind=kLoop, calls=%fused_computation | loop fusion | flops 131072 | bytes 524289 | tf_op jit(solution)/shard_map/jit(_where)/select_n | solution.py:377
  1.6 7.1 %collective-permute-start.1 = (bf16[64,1024]{1,0:T(8,128)(2,1)S(1)}, bf16[64,1024]{1,0:T(8,128)(2,1)S(1)}, u32[]{:S(2)}, u32[]{:S(2)}) collective-permute-start(bf16[64,1024]{1,0:T(8,128)(2,1)S(1)} %get-tuple-element.48.s1.old1), channel_id=1, source_target_pairs={{0,255},{1,2},{2,1},{3,4},{4,3},{5,6},{6,5},{7,8},{8,7},{9,10},{10... | collective-permute-start | bytes 393224 | tf_op jit(solution)/shard_map/ppermute | solution.py:372
  8.7 0.0 collective-permute-start
  8.7 6.9 %shard_map.59 = (bf16[32,1280,128]{2,1,0:T(8,128)(2,1)S(1)}, f32[64,2048]{1,0:T(8,128)S(1)}, bf16[64,2048]{1,0:T(8,128)(2,1)S(1)}, bf16[64,2048]{1,0:T(8,128)(2,1)S(1)}, s32[32,128]{1,0:T(8,128)S(4)}) custom-call(bf16[64,1024]{1,0:T(8,128)(2,1)S(1)} %get-tuple-element.49.s0.old0, bf16[64,1024]{1,0:T(8,128)(2,1)S(1)} %get-tuple-element.48.s1.old1, ...), custom_call_target="tpu_custom_call" | custom-call | flops 671088640 | bytes 10485760 | tf_op jit(solution)/shard_map/pallas_call | solution.py:388
  15.6 0.0 collective-permute-done.1.r1
  15.6 0.0 collective-permute-done.r0
  15.6 0.4 shard_map.60
  16.1 2.1 %collective-permute-start.3 = (bf16[64,1024]{1,0:T(8,128)(2,1)S(1)}, bf16[64,1024]{1,0:T(8,128)(2,1)S(1)}, u32[]{:S(2)}, u32[]{:S(2)}) collective-permute-start(bf16[64,1024]{1,0:T(8,128)(2,1)S(1)} %get-tuple-element.28.s1.old1), channel_id=1, source_target_pairs={{0,255},{1,2},{2,1},{3,4},{4,3},{5,6},{6,5},{7,8},{8,7},{9,10},{10... | collective-permute-start | bytes 393224 | tf_op jit(solution)/shard_map/ppermute | solution.py:372
  18.2 0.1 collective-permute-start.2
  18.3 2.4 %shard_map.61 = (f32[64,2048]{1,0:T(8,128)S(1)}, bf16[64,2048]{1,0:T(8,128)(2,1)S(1)}) custom-call(bf16[64,1024]{1,0:T(8,128)(2,1)S(1)} %get-tuple-element.28.s1.old1, bf16[64,2048]{1,0:T(8,128)(2,1)S(1)} %get-tuple-element.29.mid.old, bf16[64,1024]{1,0:T(8,128)(2,1)S(1)} %get-tuple-element.30.s0.old0, bf16[64,2048]{1,0:T(8,128)(2,1)S(1)} %get-tuple-element.31.old, ...), custom_call_target="tpu_custom_call" | custom-call | flops 671088640 | tf_op jit(solution)/shard_map/pallas_call | solution.py:423
  20.7 2.4 %collective-permute-done.3.r1 = bf16[64,1024]{1,0:T(8,128)(2,1)S(1)} collective-permute-done((bf16[64,1024]{1,0:T(8,128)(2,1)S(1)}, bf16[64,1024]{1,0:T(8,128)(2,1)S(1)}, u32[]{:S(2)}, u32[]{:S(2)}) %collective-permute-start.3) | collective-permute-done | bytes 131104 | tf_op jit(solution)/shard_map/ppermute | solution.py:372
  23.1 0.0 collective-permute-done.2.r0
  23.1 0.5 shard_map.62
  23.6 2.2 %collective-permute-start.5 = (bf16[64,1024]{1,0:T(8,128)(2,1)S(1)}, bf16[64,1024]{1,0:T(8,128)(2,1)S(1)}, u32[]{:S(2)}, u32[]{:S(2)}) collective-permute-start(bf16[64,1024]{1,0:T(8,128)(2,1)S(1)} %get-tuple-element.33.s1.old1), channel_id=1, source_target_pairs={{0,255},{1,2},{2,1},{3,4},{4,3},{5,6},{6,5},{7,8},{8,7},{9,10},{10... | collective-permute-start | bytes 393224 | tf_op jit(solution)/shard_map/ppermute | solution.py:372
  25.8 0.0 collective-permute-start.4
  25.8 2.4 %shard_map.63 = (f32[64,2048]{1,0:T(8,128)S(1)}, bf16[64,2048]{1,0:T(8,128)(2,1)S(1)}) custom-call(bf16[64,1024]{1,0:T(8,128)(2,1)S(1)} %get-tuple-element.33.s1.old1, bf16[64,2048]{1,0:T(8,128)(2,1)S(1)} %get-tuple-element.34.mid.old, bf16[64,1024]{1,0:T(8,128)(2,1)S(1)} %get-tuple-element.35.s0.old0, bf16[64,2048]{1,0:T(8,128)(2,1)S(1)} %get-tuple-element.29.mid.old, ...), custom_call_target="tpu_custom_call" | custom-call | flops 671088640 | tf_op jit(solution)/shard_map/pallas_call | solution.py:423
  28.2 1.4 %collective-permute-done.5.r1 = bf16[64,1024]{1,0:T(8,128)(2,1)S(1)} collective-permute-done((bf16[64,1024]{1,0:T(8,128)(2,1)S(1)}, bf16[64,1024]{1,0:T(8,128)(2,1)S(1)}, u32[]{:S(2)}, u32[]{:S(2)}) %collective-permute-start.5) | collective-permute-done | bytes 131104 | tf_op jit(solution)/shard_map/ppermute | solution.py:372
  29.7 0.2 collective-permute-done.4.r0
  29.9 0.5 shard_map.64
  30.4 2.4 %collective-permute-start.7 = (bf16[64,1024]{1,0:T(8,128)(2,1)S(1)}, bf16[64,1024]{1,0:T(8,128)(2,1)S(1)}, u32[]{:S(2)}, u32[]{:S(2)}) collective-permute-start(bf16[64,1024]{1,0:T(8,128)(2,1)S(1)} %get-tuple-element.37.s1), channel_id=1, source_target_pairs={{0,255},{1,2},{2,1},{3,4},{4,3},{5,6},{6,5},{7,8},{8,7},{9,10},{10... | collective-permute-start | bytes 393224 | tf_op jit(solution)/shard_map/ppermute | solution.py:372
  32.8 0.0 collective-permute-start.6
  32.8 2.4 %shard_map.65 = (f32[64,2048]{1,0:T(8,128)S(1)}, bf16[64,2048]{1,0:T(8,128)(2,1)S(1)}) custom-call(bf16[64,1024]{1,0:T(8,128)(2,1)S(1)} %get-tuple-element.37.s1, bf16[64,2048]{1,0:T(8,128)(2,1)S(1)} %get-tuple-element.38.mid, bf16[64,1024]{1,0:T(8,128)(2,1)S(1)} %get-tuple-element.39.s0, bf16[64,2048]{1,0:T(8,128)(2,1)S(1)} %get-tuple-element.34.mid.old, ...), custom_call_target="tpu_custom_call" | custom-call | flops 671088640 | tf_op jit(solution)/shard_map/pallas_call | solution.py:423
  35.2 1.0 %collective-permute-done.7.r1 = bf16[64,1024]{1,0:T(8,128)(2,1)S(1)} collective-permute-done((bf16[64,1024]{1,0:T(8,128)(2,1)S(1)}, bf16[64,1024]{1,0:T(8,128)(2,1)S(1)}, u32[]{:S(2)}, u32[]{:S(2)}) %collective-permute-start.7) | collective-permute-done | bytes 131104 | tf_op jit(solution)/shard_map/ppermute | solution.py:372
  36.2 0.3 collective-permute-done.6.r0
  36.6 0.5 shard_map.66
  37.1 7.3 %collective-permute-start.9 = (bf16[64,1024]{1,0:T(8,128)(2,1)S(1)}, bf16[64,1024]{1,0:T(8,128)(2,1)S(1)}, u32[]{:S(2)}, u32[]{:S(2)}) collective-permute-start(bf16[64,1024]{1,0:T(8,128)(2,1)S(1)} %get-tuple-element.41.s1), channel_id=1, source_target_pairs={{0,0},{1,2},{2,1},{3,4},{4,3},{5,6},{6,5},{7,8},{8,7},{9,10},{10,9... | collective-permute-start | bytes 393224 | tf_op jit(solution)/shard_map/ppermute | solution.py:372
  44.4 0.1 collective-permute-start.8
  44.5 2.7 %shard_map.67 = (f32[64,2048]{1,0:T(8,128)S(1)}, f32[64,128]{1,0:T(8,128)S(1)}) custom-call(bf16[64,1024]{1,0:T(8,128)(2,1)S(1)} %get-tuple-element.41.s1, bf16[64,2048]{1,0:T(8,128)(2,1)S(1)} %get-tuple-element.42.mid, bf16[64,1024]{1,0:T(8,128)(2,1)S(1)} %get-tuple-element.43.s0, bf16[32,1280,128]{2,1,0:T(8,128)(2,1)S(1)} %get-tuple-element.26.tiles, ...), custom_call_target="tpu_custom_call" | custom-call | flops 671088640 | tf_op jit(solution)/shard_map/pallas_call | solution.py:432
  47.2 0.4 collective-permute-done.9.r1
  47.6 1.9 %collective-permute-done.8.r0 = bf16[64,1024]{1,0:T(8,128)(2,1)S(1)} collective-permute-done((bf16[64,1024]{1,0:T(8,128)(2,1)S(1)}, bf16[64,1024]{1,0:T(8,128)(2,1)S(1)}, u32[]{:S(2)}, u32[]{:S(2)}) %collective-permute-start.8) | collective-permute-done | bytes 131104 | tf_op jit(solution)/shard_map/ppermute | solution.py:373
  49.5 0.7 shard_map.68
  50.2 10.4 %collective-permute-start.10 = (f32[32,128]{1,0:T(8,128)S(1)}, f32[32,128]{1,0:T(8,128)S(1)}, u32[]{:S(2)}, u32[]{:S(2)}) collective-permute-start(f32[32,128]{1,0:T(8,128)S(1)} %get-tuple-element.47), channel_id=1, source_target_pairs={{0,8},{1,9},{2,10},{3,11},{4,12},{5,13},{6,14},{7,15},{8,0},{9,1},... | collective-permute-start | bytes 49160 | tf_op jit(solution)/shard_map/ppermute | solution.py:347
  60.6 0.8 collective-permute-done.10
  61.5 11.1 %all_to_all.10 = f32[16,32,128]{2,1,0:T(8,128)S(1)} all-to-all(f32[16,32,128]{2,1,0:T(8,128)S(1)} %broadcast_in_dim.4), channel_id=1, replica_groups={{0,16,32,48,64,80,96,112,128,144,160,176,192,208,224,240},{1,17,33,49,6..., dimensions={0} | all-to-all | bytes 524288 | tf_op jit(solution)/shard_map/all_to_all | solution.py:350
  72.6 10.3 %all_to_all.11 = f32[8,32,128]{2,1,0:T(8,128)S(1)} all-to-all(f32[8,32,128]{2,1,0:T(8,128)S(1)} %broadcast_in_dim.5), channel_id=1, replica_groups=mesh['dom'=32,'board'=8] {'board'}, dimensions={0} | all-to-all | bytes 262144 | tf_op jit(solution)/shard_map/all_to_all | solution.py:352
  83.0 3.1 %collective-permute-start.11 = (f32[32,128]{1,0:T(8,128)S(1)}, f32[32,128]{1,0:T(8,128)S(1)}, u32[]{:S(2)}, u32[]{:S(2)}) collective-permute-start(f32[32,128]{1,0:T(8,128)S(1)} %reduce_sum.19.mine), channel_id=1, source_target_pairs={{0,8},{1,9},{2,10},{3,11},{4,12},{5,13},{6,14},{7,15},{8,0},{9,1},... | collective-permute-start | bytes 49160 | tf_op jit(solution)/shard_map/ppermute | solution.py:353
  86.1 0.8 collective-permute-done.11.other
  86.9 3.0 %shard_map.69 = (bf16[64,4096]{1,0:T(8,128)(2,1)}, f32[64,64]{1,0:T(8,128)}) custom-call(f32[32,128]{1,0:T(8,128)S(1)} %reduce_sum.19.mine, f32[32,128]{1,0:T(8,128)S(1)} %collective-permute-done.11.other, bf16[64,1024]{1,0:T(8,128)(2,1)S(1)} %get-tuple-element.43.s0, bf16[64,2048]{1,0:T(8,128)(2,1)S(1)} %get-tuple-element.42.mid, ...), custom_call_target="tpu_custom_call" | custom-call | flops 100663296 | tf_op jit(solution)/shard_map/pallas_call | solution.py:451
  (5 shorter events, 0.1 us)
Async XLA Ops:
  1.6 14.0 %collective-permute-start.1 = (bf16[64,1024]{1,0:T(8,128)(2,1)S(1)}, bf16[64,1024]{1,0:T(8,128)(2,1)S(1)}, u32[]{:S(2)}, u32[]{:S(2)}) collective-permute-start(bf16[64,1024]{1,0:T(8,128)(2,1)S(1)} %get-tuple-element.48.s1.old1), channel_id=1, source_target_pairs={{0,255},{1,2},{2,1},{3,4},{4,3},{5,6},{6,5},{7,8},{8,7},{9,10},{10... | collective-permute-start | bytes 393224 | tf_op jit(solution)/shard_map/ppermute | solution.py:372
  8.7 6.9 %collective-permute-start = (bf16[64,1024]{1,0:T(8,128)(2,1)S(1)}, bf16[64,1024]{1,0:T(8,128)(2,1)S(1)}, u32[]{:S(2)}, u32[]{:S(2)}) collective-permute-start(bf16[64,1024]{1,0:T(8,128)(2,1)S(1)} %get-tuple-element.49.s0.old0), channel_id=1, source_target_pairs={{0,1},{1,0},{2,3},{3,2},{4,5},{5,4},{6,7},{7,6},{8,9},{9,8},{10,11... | collective-permute-start | bytes 393224 | tf_op jit(solution)/shard_map/ppermute | solution.py:373
  16.1 7.1 %collective-permute-start.3 = (bf16[64,1024]{1,0:T(8,128)(2,1)S(1)}, bf16[64,1024]{1,0:T(8,128)(2,1)S(1)}, u32[]{:S(2)}, u32[]{:S(2)}) collective-permute-start(bf16[64,1024]{1,0:T(8,128)(2,1)S(1)} %get-tuple-element.28.s1.old1), channel_id=1, source_target_pairs={{0,255},{1,2},{2,1},{3,4},{4,3},{5,6},{6,5},{7,8},{8,7},{9,10},{10... | collective-permute-start | bytes 393224 | tf_op jit(solution)/shard_map/ppermute | solution.py:372
  18.2 4.9 %collective-permute-start.2 = (bf16[64,1024]{1,0:T(8,128)(2,1)S(1)}, bf16[64,1024]{1,0:T(8,128)(2,1)S(1)}, u32[]{:S(2)}, u32[]{:S(2)}) collective-permute-start(bf16[64,1024]{1,0:T(8,128)(2,1)S(1)} %get-tuple-element.30.s0.old0), channel_id=1, source_target_pairs={{0,1},{1,0},{2,3},{3,2},{4,5},{5,4},{6,7},{7,6},{8,9},{9,8},{10,11... | collective-permute-start | bytes 393224 | tf_op jit(solution)/shard_map/ppermute | solution.py:373
  23.6 6.1 %collective-permute-start.5 = (bf16[64,1024]{1,0:T(8,128)(2,1)S(1)}, bf16[64,1024]{1,0:T(8,128)(2,1)S(1)}, u32[]{:S(2)}, u32[]{:S(2)}) collective-permute-start(bf16[64,1024]{1,0:T(8,128)(2,1)S(1)} %get-tuple-element.33.s1.old1), channel_id=1, source_target_pairs={{0,255},{1,2},{2,1},{3,4},{4,3},{5,6},{6,5},{7,8},{8,7},{9,10},{10... | collective-permute-start | bytes 393224 | tf_op jit(solution)/shard_map/ppermute | solution.py:372
  25.8 4.1 %collective-permute-start.4 = (bf16[64,1024]{1,0:T(8,128)(2,1)S(1)}, bf16[64,1024]{1,0:T(8,128)(2,1)S(1)}, u32[]{:S(2)}, u32[]{:S(2)}) collective-permute-start(bf16[64,1024]{1,0:T(8,128)(2,1)S(1)} %get-tuple-element.35.s0.old0), channel_id=1, source_target_pairs={{0,1},{1,0},{2,3},{3,2},{4,5},{5,4},{6,7},{7,6},{8,9},{9,8},{10,11... | collective-permute-start | bytes 393224 | tf_op jit(solution)/shard_map/ppermute | solution.py:373
  30.4 5.9 %collective-permute-start.7 = (bf16[64,1024]{1,0:T(8,128)(2,1)S(1)}, bf16[64,1024]{1,0:T(8,128)(2,1)S(1)}, u32[]{:S(2)}, u32[]{:S(2)}) collective-permute-start(bf16[64,1024]{1,0:T(8,128)(2,1)S(1)} %get-tuple-element.37.s1), channel_id=1, source_target_pairs={{0,255},{1,2},{2,1},{3,4},{4,3},{5,6},{6,5},{7,8},{8,7},{9,10},{10... | collective-permute-start | bytes 393224 | tf_op jit(solution)/shard_map/ppermute | solution.py:372
  32.8 3.8 %collective-permute-start.6 = (bf16[64,1024]{1,0:T(8,128)(2,1)S(1)}, bf16[64,1024]{1,0:T(8,128)(2,1)S(1)}, u32[]{:S(2)}, u32[]{:S(2)}) collective-permute-start(bf16[64,1024]{1,0:T(8,128)(2,1)S(1)} %get-tuple-element.39.s0), channel_id=1, source_target_pairs={{0,1},{1,0},{2,3},{3,2},{4,5},{5,4},{6,7},{7,6},{8,9},{9,8},{10,11... | collective-permute-start | bytes 393224 | tf_op jit(solution)/shard_map/ppermute | solution.py:373
  37.1 10.5 %collective-permute-start.9 = (bf16[64,1024]{1,0:T(8,128)(2,1)S(1)}, bf16[64,1024]{1,0:T(8,128)(2,1)S(1)}, u32[]{:S(2)}, u32[]{:S(2)}) collective-permute-start(bf16[64,1024]{1,0:T(8,128)(2,1)S(1)} %get-tuple-element.41.s1), channel_id=1, source_target_pairs={{0,0},{1,2},{2,1},{3,4},{4,3},{5,6},{6,5},{7,8},{8,7},{9,10},{10,9... | collective-permute-start | bytes 393224 | tf_op jit(solution)/shard_map/ppermute | solution.py:372
  44.4 5.1 %collective-permute-start.8 = (bf16[64,1024]{1,0:T(8,128)(2,1)S(1)}, bf16[64,1024]{1,0:T(8,128)(2,1)S(1)}, u32[]{:S(2)}, u32[]{:S(2)}) collective-permute-start(bf16[64,1024]{1,0:T(8,128)(2,1)S(1)} %get-tuple-element.43.s0), channel_id=1, source_target_pairs={{0,1},{1,0},{2,3},{3,2},{4,5},{5,4},{6,7},{7,6},{8,9},{9,8},{10,11... | collective-permute-start | bytes 393224 | tf_op jit(solution)/shard_map/ppermute | solution.py:373
  50.2 11.2 %collective-permute-start.10 = (f32[32,128]{1,0:T(8,128)S(1)}, f32[32,128]{1,0:T(8,128)S(1)}, u32[]{:S(2)}, u32[]{:S(2)}) collective-permute-start(f32[32,128]{1,0:T(8,128)S(1)} %get-tuple-element.47), channel_id=1, source_target_pairs={{0,8},{1,9},{2,10},{3,11},{4,12},{5,13},{6,14},{7,15},{8,0},{9,1},... | collective-permute-start | bytes 49160 | tf_op jit(solution)/shard_map/ppermute | solution.py:347
  83.0 3.9 %collective-permute-start.11 = (f32[32,128]{1,0:T(8,128)S(1)}, f32[32,128]{1,0:T(8,128)S(1)}, u32[]{:S(2)}, u32[]{:S(2)}) collective-permute-start(f32[32,128]{1,0:T(8,128)S(1)} %reduce_sum.19.mine), channel_id=1, source_target_pairs={{0,8},{1,9},{2,10},{3,11},{4,12},{5,13},{6,14},{7,15},{8,0},{9,1},... | collective-permute-start | bytes 49160 | tf_op jit(solution)/shard_map/ppermute | solution.py:353

commit v5 on v4

--- a/solution.py
+++ b/solution.py
@@ -122,7 +122,7 @@
         lines[BLOCK + q : BLOCK + q + 1, :rows] = block_lines[q]
     lines[NEED : NEED + 1, :rows] = found
     lane = lax.broadcasted_iota(jnp.int32, (1, rows), 1)
-    lines[MISC : MISC + 1, :rows] = jnp.where(lane == 0, lead, jnp.where(lane == 1, rows - GHOST - lead, core))
+    lines[MISC : MISC + 1, :rows] = jnp.where(lane == 0, lead, jnp.where(lane == 1, rows - GHOST - lead, jnp.where(lane == 2, core, place[3])))
 
 
 def load_kernel(
@@ -133,7 +133,9 @@
     edge = GHOST * TB
     chunk = GROUP
     me = lax.axis_index(AX)
-    place = (me * rows, lax.rem(me, 2), lax.rem(lax.div(me, board), 2))
+    turn = 8 * board
+    apart = jnp.where((me == turn - 1) | (me == turn), 1, 0)
+    place = (me * rows, lax.rem(me, 2), lax.rem(lax.div(me, board), 2), apart)
     little = [
         pltpu.make_async_copy(cols_hbm, cols, small_sems.at[0]),
         pltpu.make_async_copy(counts_hbm, counts, small_sems.at[1]),
@@ -178,7 +180,7 @@
     own_products(src, held_pairs(tiles), tab, old, acc, new, True, slots, tiles.shape[0])
 
 
-def own_last_kernel(s1, mid, s0, tiles, tab, acc, both, src, new, *, slots):
+def own_last_kernel(s2, s1, mid, s0, tiles, tab, acc, both, src, new, *, slots):
     gather_field(src, s0, mid, s1)
     own_products(src, held_pairs(tiles), tab, None, acc, new, False, slots, tiles.shape[0])
     edge, inner = s0.shape[1], mid.shape[1]
@@ -193,10 +195,16 @@
     both[...] = total + jnp.concatenate([gram, jnp.zeros_like(gram)], axis=1)
 
 
-def halo_products(acc, r0, r1, tiles, tab, halo, sums, slots):
+def halo_products(acc, r0, r1, tiles, tab, halo, sums, slots, r2=None):
     edge = GHOST * TB
     halo[:, :edge] = r0[...]
     halo[:, edge : 2 * edge] = r1[...]
+    if r2 is not None:
+
+        @pl.when(tab[MISC, 3] == 1)
+        def _():
+            halo[:, edge : 2 * edge] = r2[...]
+
     halo[:, 2 * edge :] = jnp.zeros_like(halo[:, 2 * edge :])
 
     first = (tab[MISC, 0], tab[MISC, 1])
@@ -232,7 +240,8 @@
         lax.fori_loop(1, lax.div(need + 1, 2), more, 0)
 
 
-def halo_kernel(acc, old0, old1, r0, r1, tiles, tab, s1, s0, halo, sums, *, cheb, slots):
+def halo_kernel(acc, old0, old1, r0, r1, tiles, tab, *rest, cheb, slots):
+    *again, s1, s0, halo, sums = rest
     edge = GHOST * TB
     halo_products(acc, r0, r1, tiles, tab, halo, sums, slots)
     for side, old, new in ((0, old0, s0), (1, old1, s1)):
@@ -240,12 +249,14 @@
         if cheb:
             value = 2.0 * value - old[...].astype(jnp.float32)
         new[...] = value.astype(jnp.bfloat16)
-
-
-def halo_last_kernel(acc, s0, s1, r0, r1, tiles, tab, both, keep, give, whole, halo, sums, *, slots):
+    for s2 in again:
+        s2[...] = s1[...]
+
+
+def halo_last_kernel(acc, s0, s1, r0, r1, r2, tiles, tab, both, keep, give, whole, halo, sums, *, slots):
     edge = GHOST * TB
     size = both.shape[0]
-    halo_products(acc, r0, r1, tiles, tab, halo, sums, slots)
+    halo_products(acc, r0, r1, tiles, tab, halo, sums, slots, r2)
     cross = both[:, size:]
     for side, y in ((0, s0), (1, s1)):
         image = sums[:, side * edge : (side + 1) * edge].astype(jnp.bfloat16)
@@ -366,7 +377,16 @@
 
     even_pairs = [(i, i ^ 1) for i in range(devices)]
     odd_pairs = [(i, (((i + 1) ^ 1) - 1) % devices) for i in range(devices)]
-    last_pairs = [(0, 0)] + odd_pairs[1:-1] + [(devices - 1, devices - 1)]
+    turn = 8 * board
+    last_pairs = dict(odd_pairs)
+    last_pairs.update({0: turn, turn: 0, turn - 1: devices - 1, devices - 1: turn - 1})
+    last_pairs = sorted(last_pairs.items())
+    third_pairs = {i: i ^ board for i in range(devices)}
+    third_pairs.update({turn - 1: turn, turn: turn - 1})
+    for alone, beside in (((turn - 1) ^ board, -1), (turn ^ board, 1)):
+        one = alone + beside
+        third_pairs.update({one: one ^ board, one ^ board: alone, alone: one})
+    third_pairs = sorted(third_pairs.items())
 
     def exchange(s0, s1, odd_pairs=odd_pairs):
         r1 = lax.ppermute(s1, AX, odd_pairs)
@@ -409,16 +429,19 @@
     for degree in range(DEG):
         old0, old_mid, old1 = older
         older = (s0, mid, s1)
-        s1, s0 = call(
+        final = degree == DEG - 1
+        *again, s1, s0 = call(
             functools.partial(halo_kernel, cheb=degree > 0, slots=slots),
-            [edge_shape, edge_shape],
+            [edge_shape] * (3 if final else 2),
             [VM, VM, VM, VM, VM, VM, SM],
-            [VM, VM],
+            [VM] * (3 if final else 2),
             halo_scratch,
             flops=halo_flops,
         )(acc, old0, old1, r0, r1, tiles_v, tab)
         mid = new
-        r0, r1 = exchange(s0, s1, odd_pairs if degree < DEG - 1 else last_pairs)
+        if final:
+            r2 = lax.ppermute(again[0], AX, third_pairs)
+        r0, r1 = exchange(s0, s1, last_pairs if final else odd_pairs)
         if degree < DEG - 1:
             acc, new = call(
                 functools.partial(own_kernel, slots=slots),
@@ -432,21 +455,21 @@
             acc, both = call(
                 functools.partial(own_last_kernel, slots=slots),
                 [acc_shape, shape((size, 2 * size), f32)],
-                [VM, VM, VM, VM, SM],
+                [VM, VM, VM, VM, VM, SM],
                 [VM, VM],
                 [field, pltpu.VMEM((size, inner), bf16)],
                 flops=own_flops,
-            )(s1, mid, s0, tiles_v, tab)
+            )(again[0], s1, mid, s0, tiles_v, tab)
 
     half_shape = shape((size // 2, 2 * size), f32)
     keep, give = call(
         functools.partial(halo_last_kernel, slots=slots),
         [half_shape, half_shape],
-        [VM, VM, VM, VM, VM, VM, SM, VM],
+        [VM, VM, VM, VM, VM, VM, VM, SM, VM],
         [VM, VM],
         [pltpu.VMEM((size, 2 * size), f32)] + halo_scratch,
         flops=halo_flops,
-    )(acc, s0, s1, r0, r1, tiles_v, tab, both)
+    )(acc, s0, s1, r0, r1, r2, tiles_v, tab, both)
     mine, other = all_sum(keep, give, dom, board)
     basis, projected = call(
         functools.partial(end_kernel, nodes_all=devices * rows * TB),

time: 91.1 us -> 89.2 us (0.979)
  starting transfers between devices: 34.8 us -> 33.1 us
    ppermute x0 -> x1, starting transfers between devices: none -> 15.8 us  [body(): r2 = lax.ppermute(again[0], AX, third_pairs)]
    ppermute x1, starting transfers between devices: 10.4 us -> 0.58 us  [all_sum(): x = keep + lax.ppermute(give, AX, swap)]
    ppermute x5, starting transfers between devices: 21.1 us -> 13.5 us  [exchange(): r1 = lax.ppermute(s1, AX, odd_pairs)]
    ppermute x5, waiting for transfers between devices: 5.22 us -> 7.75 us  [exchange(): r1 = lax.ppermute(s1, AX, odd_pairs)]
    ppermute x5, waiting for transfers between devices: 2.51 us -> 0.73 us  [exchange(): r0 = lax.ppermute(s0, AX, even_pairs)]
  transfers between devices with their start and end apart: 12 -> 13, of which waited for: 9 -> 7; matrix products, arithmetic and copies ran while one was open for 0% -> 0% of each run, Pallas kernels for 19% -> 19%
where the time goes in v5:
time: 89.2 us; the launch traced here: 88.9 us
  starting transfers between devices  33.1 us (37%)
  Pallas kernels  22.4 us (25%)
  blocking collectives  21.4 us (24%)
  waiting for transfers between devices  10.2 us (11%)
  other arithmetic  1.03 us (1%)
    ppermute x1, starting transfers between devices, body(): r2 = lax.ppermute(again[0], AX, third_pairs)  15.8 us
    ppermute x5, starting transfers between devices, exchange(): r1 = lax.ppermute(s1, AX, odd_pairs)  13.5 us
    all_to_all x1, blocking collectives, all_sum(): x = lax.all_to_all(spread, 'board', 0, 0).sum(0)  11 us
    all_to_all x1, blocking collectives, all_sum(): x = lax.all_to_all(spread, AX, 0, 0, axis_index_groups=planes).sum(0)  10.3 us
    ppermute x5, waiting for transfers between devices, exchange(): r1 = lax.ppermute(s1, AX, odd_pairs)  7.75 us
    pallas_call x3, Pallas kernels, body(): call(functools.partial(own_kernel, slots=slots), [acc_shape, mid_shape],...  7.3 us
    pallas_call x1, Pallas kernels, body(): call(functools.partial(load_kernel, board=board), [shape((rows, slots * T...  6.89 us
    ppermute x1, starting transfers between devices, all_sum(): return (x, lax.ppermute(x, AX, swap))  3.12 us
  transfers between devices with their start and end apart: 13, of which 7 were waited for; matrix products, arithmetic and copies ran while one was open for 0% of the time, Pallas kernels for 19%

profile of v5, /device:TPU:1, one launch (start us, length us, event | category | flops | bytes accessed | tf_op | source)
XLA Modules:
  0.0 88.9 jit_solution(149657645571848338)
XLA Ops:
  0.6 1.0 %broadcast_select_fusion = (bf16[64,1024]{1,0:T(8,128)(2,1)S(1)}, bf16[64,1024]{1,0:T(8,128)(2,1)S(1)}) fusion(pred[]{:T(512)S(6)} %eq.6, bf16[64,4096]{1,0:T(8,128)(2,1)} %block.1), kind=kLoop, calls=%fused_computation | loop fusion | flops 131072 | bytes 524289 | tf_op jit(solution)/shard_map/jit(_where)/select_n | solution.py:397
  1.6 7.1 %collective-permute-start.1 = (bf16[64,1024]{1,0:T(8,128)(2,1)S(1)}, bf16[64,1024]{1,0:T(8,128)(2,1)S(1)}, u32[]{:S(2)}, u32[]{:S(2)}) collective-permute-start(bf16[64,1024]{1,0:T(8,128)(2,1)S(1)} %get-tuple-element.50.s1.old1), channel_id=1, source_target_pairs={{0,255},{1,2},{2,1},{3,4},{4,3},{5,6},{6,5},{7,8},{8,7},{9,10},{10... | collective-permute-start | bytes 393224 | tf_op jit(solution)/shard_map/ppermute | solution.py:392
  8.7 0.0 collective-permute-start
  8.7 6.9 %shard_map.59 = (bf16[32,1280,128]{2,1,0:T(8,128)(2,1)S(1)}, f32[64,2048]{1,0:T(8,128)S(1)}, bf16[64,2048]{1,0:T(8,128)(2,1)S(1)}, bf16[64,2048]{1,0:T(8,128)(2,1)S(1)}, s32[32,128]{1,0:T(8,128)S(4)}) custom-call(bf16[64,1024]{1,0:T(8,128)(2,1)S(1)} %get-tuple-element.51.s0.old0, bf16[64,1024]{1,0:T(8,128)(2,1)S(1)} %get-tuple-element.50.s1.old1, ...), custom_call_target="tpu_custom_call" | custom-call | flops 671088640 | bytes 10485760 | tf_op jit(solution)/shard_map/pallas_call | solution.py:408
  15.6 0.0 collective-permute-done.1.r1
  15.6 0.0 collective-permute-done.r0
  15.6 0.4 shard_map.60
  16.0 2.1 %collective-permute-start.3 = (bf16[64,1024]{1,0:T(8,128)(2,1)S(1)}, bf16[64,1024]{1,0:T(8,128)(2,1)S(1)}, u32[]{:S(2)}, u32[]{:S(2)}) collective-permute-start(bf16[64,1024]{1,0:T(8,128)(2,1)S(1)} %get-tuple-element.29.s1.old1), channel_id=1, source_target_pairs={{0,255},{1,2},{2,1},{3,4},{4,3},{5,6},{6,5},{7,8},{8,7},{9,10},{10... | collective-permute-start | bytes 393224 | tf_op jit(solution)/shard_map/ppermute | solution.py:392
  18.2 0.0 collective-permute-start.2
  18.2 2.4 %shard_map.61 = (f32[64,2048]{1,0:T(8,128)S(1)}, bf16[64,2048]{1,0:T(8,128)(2,1)S(1)}) custom-call(bf16[64,1024]{1,0:T(8,128)(2,1)S(1)} %get-tuple-element.29.s1.old1, bf16[64,2048]{1,0:T(8,128)(2,1)S(1)} %get-tuple-element.30.mid.old, bf16[64,1024]{1,0:T(8,128)(2,1)S(1)} %get-tuple-element.31.s0.old0, bf16[64,2048]{1,0:T(8,128)(2,1)S(1)} %get-tuple-element.32.old, ...), custom_call_target="tpu_custom_call" | custom-call | flops 671088640 | tf_op jit(solution)/shard_map/pallas_call | solution.py:446
  20.6 2.3 %collective-permute-done.3.r1 = bf16[64,1024]{1,0:T(8,128)(2,1)S(1)} collective-permute-done((bf16[64,1024]{1,0:T(8,128)(2,1)S(1)}, bf16[64,1024]{1,0:T(8,128)(2,1)S(1)}, u32[]{:S(2)}, u32[]{:S(2)}) %collective-permute-start.3) | collective-permute-done | bytes 131104 | tf_op jit(solution)/shard_map/ppermute | solution.py:392
  22.9 0.0 collective-permute-done.2.r0
  22.9 0.5 shard_map.62
  23.4 2.6 %collective-permute-start.5 = (bf16[64,1024]{1,0:T(8,128)(2,1)S(1)}, bf16[64,1024]{1,0:T(8,128)(2,1)S(1)}, u32[]{:S(2)}, u32[]{:S(2)}) collective-permute-start(bf16[64,1024]{1,0:T(8,128)(2,1)S(1)} %get-tuple-element.34.s1.old1), channel_id=1, source_target_pairs={{0,255},{1,2},{2,1},{3,4},{4,3},{5,6},{6,5},{7,8},{8,7},{9,10},{10... | collective-permute-start | bytes 393224 | tf_op jit(solution)/shard_map/ppermute | solution.py:392
  26.0 0.0 collective-permute-start.4
  26.0 2.4 %shard_map.63 = (f32[64,2048]{1,0:T(8,128)S(1)}, bf16[64,2048]{1,0:T(8,128)(2,1)S(1)}) custom-call(bf16[64,1024]{1,0:T(8,128)(2,1)S(1)} %get-tuple-element.34.s1.old1, bf16[64,2048]{1,0:T(8,128)(2,1)S(1)} %get-tuple-element.35.mid.old, bf16[64,1024]{1,0:T(8,128)(2,1)S(1)} %get-tuple-element.36.s0.old0, bf16[64,2048]{1,0:T(8,128)(2,1)S(1)} %get-tuple-element.30.mid.old, ...), custom_call_target="tpu_custom_call" | custom-call | flops 671088640 | tf_op jit(solution)/shard_map/pallas_call | solution.py:446
  28.4 0.9 %collective-permute-done.5.r1 = bf16[64,1024]{1,0:T(8,128)(2,1)S(1)} collective-permute-done((bf16[64,1024]{1,0:T(8,128)(2,1)S(1)}, bf16[64,1024]{1,0:T(8,128)(2,1)S(1)}, u32[]{:S(2)}, u32[]{:S(2)}) %collective-permute-start.5) | collective-permute-done | bytes 131104 | tf_op jit(solution)/shard_map/ppermute | solution.py:392
  29.4 0.7 collective-permute-done.4.r0
  30.1 0.5 shard_map.64
  30.6 1.8 %collective-permute-start.7 = (bf16[64,1024]{1,0:T(8,128)(2,1)S(1)}, bf16[64,1024]{1,0:T(8,128)(2,1)S(1)}, u32[]{:S(2)}, u32[]{:S(2)}) collective-permute-start(bf16[64,1024]{1,0:T(8,128)(2,1)S(1)} %get-tuple-element.38.s1), channel_id=1, source_target_pairs={{0,255},{1,2},{2,1},{3,4},{4,3},{5,6},{6,5},{7,8},{8,7},{9,10},{10... | collective-permute-start | bytes 393224 | tf_op jit(solution)/shard_map/ppermute | solution.py:392
  32.3 0.0 collective-permute-start.6
  32.3 2.4 %shard_map.65 = (f32[64,2048]{1,0:T(8,128)S(1)}, bf16[64,2048]{1,0:T(8,128)(2,1)S(1)}) custom-call(bf16[64,1024]{1,0:T(8,128)(2,1)S(1)} %get-tuple-element.38.s1, bf16[64,2048]{1,0:T(8,128)(2,1)S(1)} %get-tuple-element.39.mid, bf16[64,1024]{1,0:T(8,128)(2,1)S(1)} %get-tuple-element.40.s0, bf16[64,2048]{1,0:T(8,128)(2,1)S(1)} %get-tuple-element.35.mid.old, ...), custom_call_target="tpu_custom_call" | custom-call | flops 671088640 | tf_op jit(solution)/shard_map/pallas_call | solution.py:446
  34.8 1.7 %collective-permute-done.7.r1 = bf16[64,1024]{1,0:T(8,128)(2,1)S(1)} collective-permute-done((bf16[64,1024]{1,0:T(8,128)(2,1)S(1)}, bf16[64,1024]{1,0:T(8,128)(2,1)S(1)}, u32[]{:S(2)}, u32[]{:S(2)}) %collective-permute-start.7) | collective-permute-done | bytes 131104 | tf_op jit(solution)/shard_map/ppermute | solution.py:392
  36.4 0.0 collective-permute-done.6.r0
  36.4 0.5 shard_map.66
  36.9 15.8 %collective-permute-start.10 = (bf16[64,1024]{1,0:T(8,128)(2,1)S(1)}, bf16[64,1024]{1,0:T(8,128)(2,1)S(1)}, u32[]{:S(2)}, u32[]{:S(2)}) collective-permute-start(bf16[64,1024]{1,0:T(8,128)(2,1)S(1)} %get-tuple-element.42.s2), channel_id=1, source_target_pairs={{0,8},{1,9},{2,10},{3,11},{4,12},{5,13},{6,14},{7,15},{8,0},{9,1},... | collective-permute-start | bytes 393224 | tf_op jit(solution)/shard_map/ppermute | solution.py:443
  52.7 0.0 collective-permute-start.9
  52.7 0.0 collective-permute-start.8
  52.7 2.7 %shard_map.67 = (f32[64,2048]{1,0:T(8,128)S(1)}, f32[64,128]{1,0:T(8,128)S(1)}) custom-call(bf16[64,1024]{1,0:T(8,128)(2,1)S(1)} %get-tuple-element.42.s2, bf16[64,1024]{1,0:T(8,128)(2,1)S(1)} %get-tuple-element.43.s1, bf16[64,2048]{1,0:T(8,128)(2,1)S(1)} %get-tuple-element.44.mid, bf16[64,1024]{1,0:T(8,128)(2,1)S(1)} %get-tuple-element.45.s0, ...), custom_call_target="tpu_custom_call" | custom-call | flops 671088640 | tf_op jit(solution)/shard_map/pallas_call | solution.py:455
  55.5 0.0 collective-permute-done.10.r2
  55.5 2.9 %collective-permute-done.9.r1 = bf16[64,1024]{1,0:T(8,128)(2,1)S(1)} collective-permute-done((bf16[64,1024]{1,0:T(8,128)(2,1)S(1)}, bf16[64,1024]{1,0:T(8,128)(2,1)S(1)}, u32[]{:S(2)}, u32[]{:S(2)}) %collective-permute-start.9) | collective-permute-done | bytes 131104 | tf_op jit(solution)/shard_map/ppermute | solution.py:392
  58.3 0.0 collective-permute-done.8.r0
  58.3 0.7 shard_map.68
  59.0 0.6 collective-permute-start.11
  59.6 0.8 collective-permute-done.11
  60.5 10.3 %all_to_all.10 = f32[16,32,128]{2,1,0:T(8,128)S(1)} all-to-all(f32[16,32,128]{2,1,0:T(8,128)S(1)} %broadcast_in_dim.4), channel_id=1, replica_groups={{0,16,32,48,64,80,96,112,128,144,160,176,192,208,224,240},{1,17,33,49,6..., dimensions={0} | all-to-all | bytes 524288 | tf_op jit(solution)/shard_map/all_to_all | solution.py:361
  70.9 11.0 %all_to_all.11 = f32[8,32,128]{2,1,0:T(8,128)S(1)} all-to-all(f32[8,32,128]{2,1,0:T(8,128)S(1)} %broadcast_in_dim.5), channel_id=1, replica_groups=mesh['dom'=32,'board'=8] {'board'}, dimensions={0} | all-to-all | bytes 262144 | tf_op jit(solution)/shard_map/all_to_all | solution.py:363
  81.9 3.1 %collective-permute-start.12 = (f32[32,128]{1,0:T(8,128)S(1)}, f32[32,128]{1,0:T(8,128)S(1)}, u32[]{:S(2)}, u32[]{:S(2)}) collective-permute-start(f32[32,128]{1,0:T(8,128)S(1)} %reduce_sum.19.mine), channel_id=1, source_target_pairs={{0,8},{1,9},{2,10},{3,11},{4,12},{5,13},{6,14},{7,15},{8,0},{9,1},... | collective-permute-start | bytes 49160 | tf_op jit(solution)/shard_map/ppermute | solution.py:364
  85.0 0.8 collective-permute-done.12.other
  85.9 3.0 %shard_map.69 = (bf16[64,4096]{1,0:T(8,128)(2,1)}, f32[64,64]{1,0:T(8,128)}) custom-call(f32[32,128]{1,0:T(8,128)S(1)} %reduce_sum.19.mine, f32[32,128]{1,0:T(8,128)S(1)} %collective-permute-done.12.other, bf16[64,1024]{1,0:T(8,128)(2,1)S(1)} %get-tuple-element.45.s0, bf16[64,2048]{1,0:T(8,128)(2,1)S(1)} %get-tuple-element.44.mid, ...), custom_call_target="tpu_custom_call" | custom-call | flops 100663296 | tf_op jit(solution)/shard_map/pallas_call | solution.py:474
  (5 shorter events, 0.1 us)
Async XLA Ops:
  1.6 14.0 %collective-permute-start.1 = (bf16[64,1024]{1,0:T(8,128)(2,1)S(1)}, bf16[64,1024]{1,0:T(8,128)(2,1)S(1)}, u32[]{:S(2)}, u32[]{:S(2)}) collective-permute-start(bf16[64,1024]{1,0:T(8,128)(2,1)S(1)} %get-tuple-element.50.s1.old1), channel_id=1, source_target_pairs={{0,255},{1,2},{2,1},{3,4},{4,3},{5,6},{6,5},{7,8},{8,7},{9,10},{10... | collective-permute-start | bytes 393224 | tf_op jit(solution)/shard_map/ppermute | solution.py:392
  8.7 6.9 %collective-permute-start = (bf16[64,1024]{1,0:T(8,128)(2,1)S(1)}, bf16[64,1024]{1,0:T(8,128)(2,1)S(1)}, u32[]{:S(2)}, u32[]{:S(2)}) collective-permute-start(bf16[64,1024]{1,0:T(8,128)(2,1)S(1)} %get-tuple-element.51.s0.old0), channel_id=1, source_target_pairs={{0,1},{1,0},{2,3},{3,2},{4,5},{5,4},{6,7},{7,6},{8,9},{9,8},{10,11... | collective-permute-start | bytes 393224 | tf_op jit(solution)/shard_map/ppermute | solution.py:393
  16.0 6.9 %collective-permute-start.3 = (bf16[64,1024]{1,0:T(8,128)(2,1)S(1)}, bf16[64,1024]{1,0:T(8,128)(2,1)S(1)}, u32[]{:S(2)}, u32[]{:S(2)}) collective-permute-start(bf16[64,1024]{1,0:T(8,128)(2,1)S(1)} %get-tuple-element.29.s1.old1), channel_id=1, source_target_pairs={{0,255},{1,2},{2,1},{3,4},{4,3},{5,6},{6,5},{7,8},{8,7},{9,10},{10... | collective-permute-start | bytes 393224 | tf_op jit(solution)/shard_map/ppermute | solution.py:392
  18.2 4.7 %collective-permute-start.2 = (bf16[64,1024]{1,0:T(8,128)(2,1)S(1)}, bf16[64,1024]{1,0:T(8,128)(2,1)S(1)}, u32[]{:S(2)}, u32[]{:S(2)}) collective-permute-start(bf16[64,1024]{1,0:T(8,128)(2,1)S(1)} %get-tuple-element.31.s0.old0), channel_id=1, source_target_pairs={{0,1},{1,0},{2,3},{3,2},{4,5},{5,4},{6,7},{7,6},{8,9},{9,8},{10,11... | collective-permute-start | bytes 393224 | tf_op jit(solution)/shard_map/ppermute | solution.py:393
  23.4 6.0 %collective-permute-start.5 = (bf16[64,1024]{1,0:T(8,128)(2,1)S(1)}, bf16[64,1024]{1,0:T(8,128)(2,1)S(1)}, u32[]{:S(2)}, u32[]{:S(2)}) collective-permute-start(bf16[64,1024]{1,0:T(8,128)(2,1)S(1)} %get-tuple-element.34.s1.old1), channel_id=1, source_target_pairs={{0,255},{1,2},{2,1},{3,4},{4,3},{5,6},{6,5},{7,8},{8,7},{9,10},{10... | collective-permute-start | bytes 393224 | tf_op jit(solution)/shard_map/ppermute | solution.py:392
  26.0 4.1 %collective-permute-start.4 = (bf16[64,1024]{1,0:T(8,128)(2,1)S(1)}, bf16[64,1024]{1,0:T(8,128)(2,1)S(1)}, u32[]{:S(2)}, u32[]{:S(2)}) collective-permute-start(bf16[64,1024]{1,0:T(8,128)(2,1)S(1)} %get-tuple-element.36.s0.old0), channel_id=1, source_target_pairs={{0,1},{1,0},{2,3},{3,2},{4,5},{5,4},{6,7},{7,6},{8,9},{9,8},{10,11... | collective-permute-start | bytes 393224 | tf_op jit(solution)/shard_map/ppermute | solution.py:393
  30.6 5.9 %collective-permute-start.7 = (bf16[64,1024]{1,0:T(8,128)(2,1)S(1)}, bf16[64,1024]{1,0:T(8,128)(2,1)S(1)}, u32[]{:S(2)}, u32[]{:S(2)}) collective-permute-start(bf16[64,1024]{1,0:T(8,128)(2,1)S(1)} %get-tuple-element.38.s1), channel_id=1, source_target_pairs={{0,255},{1,2},{2,1},{3,4},{4,3},{5,6},{6,5},{7,8},{8,7},{9,10},{10... | collective-permute-start | bytes 393224 | tf_op jit(solution)/shard_map/ppermute | solution.py:392
  32.3 4.1 %collective-permute-start.6 = (bf16[64,1024]{1,0:T(8,128)(2,1)S(1)}, bf16[64,1024]{1,0:T(8,128)(2,1)S(1)}, u32[]{:S(2)}, u32[]{:S(2)}) collective-permute-start(bf16[64,1024]{1,0:T(8,128)(2,1)S(1)} %get-tuple-element.40.s0), channel_id=1, source_target_pairs={{0,1},{1,0},{2,3},{3,2},{4,5},{5,4},{6,7},{7,6},{8,9},{9,8},{10,11... | collective-permute-start | bytes 393224 | tf_op jit(solution)/shard_map/ppermute | solution.py:393
  36.9 18.5 %collective-permute-start.10 = (bf16[64,1024]{1,0:T(8,128)(2,1)S(1)}, bf16[64,1024]{1,0:T(8,128)(2,1)S(1)}, u32[]{:S(2)}, u32[]{:S(2)}) collective-permute-start(bf16[64,1024]{1,0:T(8,128)(2,1)S(1)} %get-tuple-element.42.s2), channel_id=1, source_target_pairs={{0,8},{1,9},{2,10},{3,11},{4,12},{5,13},{6,14},{7,15},{8,0},{9,1},... | collective-permute-start | bytes 393224 | tf_op jit(solution)/shard_map/ppermute | solution.py:443
  52.7 5.6 %collective-permute-start.9 = (bf16[64,1024]{1,0:T(8,128)(2,1)S(1)}, bf16[64,1024]{1,0:T(8,128)(2,1)S(1)}, u32[]{:S(2)}, u32[]{:S(2)}) collective-permute-start(bf16[64,1024]{1,0:T(8,128)(2,1)S(1)} %get-tuple-element.43.s1), channel_id=1, source_target_pairs={{0,64},{1,2},{2,1},{3,4},{4,3},{5,6},{6,5},{7,8},{8,7},{9,10},{10,... | collective-permute-start | bytes 393224 | tf_op jit(solution)/shard_map/ppermute | solution.py:392
  52.7 5.6 %collective-permute-start.8 = (bf16[64,1024]{1,0:T(8,128)(2,1)S(1)}, bf16[64,1024]{1,0:T(8,128)(2,1)S(1)}, u32[]{:S(2)}, u32[]{:S(2)}) collective-permute-start(bf16[64,1024]{1,0:T(8,128)(2,1)S(1)} %get-tuple-element.45.s0), channel_id=1, source_target_pairs={{0,1},{1,0},{2,3},{3,2},{4,5},{5,4},{6,7},{7,6},{8,9},{9,8},{10,11... | collective-permute-start | bytes 393224 | tf_op jit(solution)/shard_map/ppermute | solution.py:393
  59.0 1.4 %collective-permute-start.11 = (f32[32,128]{1,0:T(8,128)S(1)}, f32[32,128]{1,0:T(8,128)S(1)}, u32[]{:S(2)}, u32[]{:S(2)}) collective-permute-start(f32[32,128]{1,0:T(8,128)S(1)} %get-tuple-element.49), channel_id=1, source_target_pairs={{0,8},{1,9},{2,10},{3,11},{4,12},{5,13},{6,14},{7,15},{8,0},{9,1},... | collective-permute-start | bytes 49160 | tf_op jit(solution)/shard_map/ppermute | solution.py:358
  81.9 4.0 %collective-permute-start.12 = (f32[32,128]{1,0:T(8,128)S(1)}, f32[32,128]{1,0:T(8,128)S(1)}, u32[]{:S(2)}, u32[]{:S(2)}) collective-permute-start(f32[32,128]{1,0:T(8,128)S(1)} %reduce_sum.19.mine), channel_id=1, source_target_pairs={{0,8},{1,9},{2,10},{3,11},{4,12},{5,13},{6,14},{7,15},{8,0},{9,1},... | collective-permute-start | bytes 49160 | tf_op jit(solution)/shard_map/ppermute | solution.py:364

commit v6 on v5

--- a/solution.py
+++ b/solution.py
@@ -180,7 +180,7 @@
     own_products(src, held_pairs(tiles), tab, old, acc, new, True, slots, tiles.shape[0])
 
 
-def own_last_kernel(s2, s1, mid, s0, tiles, tab, acc, both, src, new, *, slots):
+def own_last_kernel(s2, s0, mid, s1, tiles, tab, acc, both, src, new, *, slots):
     gather_field(src, s0, mid, s1)
     own_products(src, held_pairs(tiles), tab, None, acc, new, False, slots, tiles.shape[0])
     edge, inner = s0.shape[1], mid.shape[1]
@@ -242,6 +242,8 @@
 
 def halo_kernel(acc, old0, old1, r0, r1, tiles, tab, *rest, cheb, slots):
     *again, s1, s0, halo, sums = rest
+    if again:
+        s0, s1 = s1, s0
     edge = GHOST * TB
     halo_products(acc, r0, r1, tiles, tab, halo, sums, slots)
     for side, old, new in ((0, old0, s0), (1, old1, s1)):
@@ -430,7 +432,7 @@
         old0, old_mid, old1 = older
         older = (s0, mid, s1)
         final = degree == DEG - 1
-        *again, s1, s0 = call(
+        *again, sa, sb = call(
             functools.partial(halo_kernel, cheb=degree > 0, slots=slots),
             [edge_shape] * (3 if final else 2),
             [VM, VM, VM, VM, VM, VM, SM],
@@ -438,6 +440,7 @@
             halo_scratch,
             flops=halo_flops,
         )(acc, old0, old1, r0, r1, tiles_v, tab)
+        s0, s1 = (sa, sb) if final else (sb, sa)
         mid = new
         if final:
             r2 = lax.ppermute(again[0], AX, third_pairs)
@@ -459,7 +462,7 @@
                 [VM, VM],
                 [field, pltpu.VMEM((size, inner), bf16)],
                 flops=own_flops,
-            )(again[0], s1, mid, s0, tiles_v, tab)
+            )(again[0], s0, mid, s1, tiles_v, tab)
 
     half_shape = shape((size // 2, 2 * size), f32)
     keep, give = call(

time: 89.2 us -> 89.9 us (level)
  starting transfers between devices: 33.1 us -> 34.4 us
    ppermute x5, waiting for transfers between devices: 0.73 us -> 3.74 us  [exchange(): r0 = lax.ppermute(s0, AX, even_pairs)]
    ppermute x5, waiting for transfers between devices: 7.75 us -> 5.12 us  [exchange(): r1 = lax.ppermute(s1, AX, odd_pairs)]
    ppermute x5, starting transfers between devices: 13.5 us -> 14.5 us  [exchange(): r1 = lax.ppermute(s1, AX, odd_pairs)]
  transfers between devices with their start and end apart: 13 -> 13, of which waited for: 7 -> 8; matrix products, arithmetic and copies ran while one was open for 0% -> 0% of each run, Pallas kernels for 19% -> 19%
where the time goes in v6:
time: 89.9 us
  starting transfers between devices  34.4 us (38%)
  Pallas kernels  22.5 us (25%)
  blocking collectives  20.7 us (23%)
  waiting for transfers between devices  10.5 us (12%)
  other arithmetic  1.03 us (1%)
    ppermute x1, starting transfers between devices, body(): r2 = lax.ppermute(again[0], AX, third_pairs)  16.1 us
    ppermute x5, starting transfers between devices, exchange(): r1 = lax.ppermute(s1, AX, odd_pairs)  14.5 us
    all_to_all x1, blocking collectives, all_sum(): x = lax.all_to_all(spread, AX, 0, 0, axis_index_groups=planes).sum(0)  10.3 us
    all_to_all x1, blocking collectives, all_sum(): x = lax.all_to_all(spread, 'board', 0, 0).sum(0)  10.3 us
    pallas_call x3, Pallas kernels, body(): call(functools.partial(own_kernel, slots=slots), [acc_shape, mid_shape],...  7.34 us
    pallas_call x1, Pallas kernels, body(): call(functools.partial(load_kernel, board=board), [shape((rows, slots * T...  6.9 us
    ppermute x5, waiting for transfers between devices, exchange(): r1 = lax.ppermute(s1, AX, odd_pairs)  5.12 us
    ppermute x5, waiting for transfers between devices, exchange(): r0 = lax.ppermute(s0, AX, even_pairs)  3.74 us
  transfers between devices with their start and end apart: 13, of which 8 were waited for; matrix products, arithmetic and copies ran while one was open for 0% of the time, Pallas kernels for 19%

profile of v6, /device:TPU:1, one launch (start us, length us, event | category | flops | bytes accessed | tf_op | source)
XLA Modules:
  0.0 89.9 jit_solution(3083888567926290974)
XLA Ops:
  0.6 1.0 %broadcast_select_fusion = (bf16[64,1024]{1,0:T(8,128)(2,1)S(1)}, bf16[64,1024]{1,0:T(8,128)(2,1)S(1)}) fusion(pred[]{:T(512)S(6)} %eq.6, bf16[64,4096]{1,0:T(8,128)(2,1)} %block.1), kind=kLoop, calls=%fused_computation | loop fusion | flops 131072 | bytes 524289 | tf_op jit(solution)/shard_map/jit(_where)/select_n | solution.py:399
  1.6 7.1 %collective-permute-start.1 = (bf16[64,1024]{1,0:T(8,128)(2,1)S(1)}, bf16[64,1024]{1,0:T(8,128)(2,1)S(1)}, u32[]{:S(2)}, u32[]{:S(2)}) collective-permute-start(bf16[64,1024]{1,0:T(8,128)(2,1)S(1)} %get-tuple-element.50.s1.old1), channel_id=1, source_target_pairs={{0,255},{1,2},{2,1},{3,4},{4,3},{5,6},{6,5},{7,8},{8,7},{9,10},{10... | collective-permute-start | bytes 393224 | tf_op jit(solution)/shard_map/ppermute | solution.py:394
  8.7 0.0 collective-permute-start
  8.7 6.9 %shard_map.59 = (bf16[32,1280,128]{2,1,0:T(8,128)(2,1)S(1)}, f32[64,2048]{1,0:T(8,128)S(1)}, bf16[64,2048]{1,0:T(8,128)(2,1)S(1)}, bf16[64,2048]{1,0:T(8,128)(2,1)S(1)}, s32[32,128]{1,0:T(8,128)S(4)}) custom-call(bf16[64,1024]{1,0:T(8,128)(2,1)S(1)} %get-tuple-element.51.s0.old0, bf16[64,1024]{1,0:T(8,128)(2,1)S(1)} %get-tuple-element.50.s1.old1, ...), custom_call_target="tpu_custom_call" | custom-call | flops 671088640 | bytes 10485760 | tf_op jit(solution)/shard_map/pallas_call | solution.py:410
  15.6 0.0 collective-permute-done.1.r1
  15.6 0.0 collective-permute-done.r0
  15.6 0.4 shard_map.60
  16.1 2.3 %collective-permute-start.3 = (bf16[64,1024]{1,0:T(8,128)(2,1)S(1)}, bf16[64,1024]{1,0:T(8,128)(2,1)S(1)}, u32[]{:S(2)}, u32[]{:S(2)}) collective-permute-start(bf16[64,1024]{1,0:T(8,128)(2,1)S(1)} %get-tuple-element.29.s1.old1), channel_id=1, source_target_pairs={{0,255},{1,2},{2,1},{3,4},{4,3},{5,6},{6,5},{7,8},{8,7},{9,10},{10... | collective-permute-start | bytes 393224 | tf_op jit(solution)/shard_map/ppermute | solution.py:394
  18.4 0.0 collective-permute-start.2
  18.4 2.4 %shard_map.61 = (f32[64,2048]{1,0:T(8,128)S(1)}, bf16[64,2048]{1,0:T(8,128)(2,1)S(1)}) custom-call(bf16[64,1024]{1,0:T(8,128)(2,1)S(1)} %get-tuple-element.29.s1.old1, bf16[64,2048]{1,0:T(8,128)(2,1)S(1)} %get-tuple-element.30.mid.old, bf16[64,1024]{1,0:T(8,128)(2,1)S(1)} %get-tuple-element.31.s0.old0, bf16[64,2048]{1,0:T(8,128)(2,1)S(1)} %get-tuple-element.32.old, ...), custom_call_target="tpu_custom_call" | custom-call | flops 671088640 | tf_op jit(solution)/shard_map/pallas_call | solution.py:449
  20.8 2.3 %collective-permute-done.3.r1 = bf16[64,1024]{1,0:T(8,128)(2,1)S(1)} collective-permute-done((bf16[64,1024]{1,0:T(8,128)(2,1)S(1)}, bf16[64,1024]{1,0:T(8,128)(2,1)S(1)}, u32[]{:S(2)}, u32[]{:S(2)}) %collective-permute-start.3) | collective-permute-done | bytes 131104 | tf_op jit(solution)/shard_map/ppermute | solution.py:394
  23.1 0.0 collective-permute-done.2.r0
  23.1 0.5 shard_map.62
  23.6 2.4 %collective-permute-start.5 = (bf16[64,1024]{1,0:T(8,128)(2,1)S(1)}, bf16[64,1024]{1,0:T(8,128)(2,1)S(1)}, u32[]{:S(2)}, u32[]{:S(2)}) collective-permute-start(bf16[64,1024]{1,0:T(8,128)(2,1)S(1)} %get-tuple-element.34.s1.old1), channel_id=1, source_target_pairs={{0,255},{1,2},{2,1},{3,4},{4,3},{5,6},{6,5},{7,8},{8,7},{9,10},{10... | collective-permute-start | bytes 393224 | tf_op jit(solution)/shard_map/ppermute | solution.py:394
  26.0 0.0 collective-permute-start.4
  26.0 2.4 %shard_map.63 = (f32[64,2048]{1,0:T(8,128)S(1)}, bf16[64,2048]{1,0:T(8,128)(2,1)S(1)}) custom-call(bf16[64,1024]{1,0:T(8,128)(2,1)S(1)} %get-tuple-element.34.s1.old1, bf16[64,2048]{1,0:T(8,128)(2,1)S(1)} %get-tuple-element.35.mid.old, bf16[64,1024]{1,0:T(8,128)(2,1)S(1)} %get-tuple-element.36.s0.old0, bf16[64,2048]{1,0:T(8,128)(2,1)S(1)} %get-tuple-element.30.mid.old, ...), custom_call_target="tpu_custom_call" | custom-call | flops 671088640 | tf_op jit(solution)/shard_map/pallas_call | solution.py:449
  28.4 1.6 %collective-permute-done.5.r1 = bf16[64,1024]{1,0:T(8,128)(2,1)S(1)} collective-permute-done((bf16[64,1024]{1,0:T(8,128)(2,1)S(1)}, bf16[64,1024]{1,0:T(8,128)(2,1)S(1)}, u32[]{:S(2)}, u32[]{:S(2)}) %collective-permute-start.5) | collective-permute-done | bytes 131104 | tf_op jit(solution)/shard_map/ppermute | solution.py:394
  30.1 0.0 collective-permute-done.4.r0
  30.1 0.5 shard_map.64
  30.6 2.8 %collective-permute-start.7 = (bf16[64,1024]{1,0:T(8,128)(2,1)S(1)}, bf16[64,1024]{1,0:T(8,128)(2,1)S(1)}, u32[]{:S(2)}, u32[]{:S(2)}) collective-permute-start(bf16[64,1024]{1,0:T(8,128)(2,1)S(1)} %get-tuple-element.38.s1), channel_id=1, source_target_pairs={{0,255},{1,2},{2,1},{3,4},{4,3},{5,6},{6,5},{7,8},{8,7},{9,10},{10... | collective-permute-start | bytes 393224 | tf_op jit(solution)/shard_map/ppermute | solution.py:394
  33.3 0.0 collective-permute-start.6
  33.3 2.4 %shard_map.65 = (f32[64,2048]{1,0:T(8,128)S(1)}, bf16[64,2048]{1,0:T(8,128)(2,1)S(1)}) custom-call(bf16[64,1024]{1,0:T(8,128)(2,1)S(1)} %get-tuple-element.38.s1, bf16[64,2048]{1,0:T(8,128)(2,1)S(1)} %get-tuple-element.39.mid, bf16[64,1024]{1,0:T(8,128)(2,1)S(1)} %get-tuple-element.40.s0, bf16[64,2048]{1,0:T(8,128)(2,1)S(1)} %get-tuple-element.35.mid.old, ...), custom_call_target="tpu_custom_call" | custom-call | flops 671088640 | tf_op jit(solution)/shard_map/pallas_call | solution.py:449
  35.8 0.7 collective-permute-done.7.r1
  36.4 1.4 %collective-permute-done.6.r0 = bf16[64,1024]{1,0:T(8,128)(2,1)S(1)} collective-permute-done((bf16[64,1024]{1,0:T(8,128)(2,1)S(1)}, bf16[64,1024]{1,0:T(8,128)(2,1)S(1)}, u32[]{:S(2)}, u32[]{:S(2)}) %collective-permute-start.6) | collective-permute-done | bytes 131104 | tf_op jit(solution)/shard_map/ppermute | solution.py:395
  37.8 0.5 shard_map.66
  38.3 16.1 %collective-permute-start.10 = (bf16[64,1024]{1,0:T(8,128)(2,1)S(1)}, bf16[64,1024]{1,0:T(8,128)(2,1)S(1)}, u32[]{:S(2)}, u32[]{:S(2)}) collective-permute-start(bf16[64,1024]{1,0:T(8,128)(2,1)S(1)} %get-tuple-element.42.s2), channel_id=1, source_target_pairs={{0,8},{1,9},{2,10},{3,11},{4,12},{5,13},{6,14},{7,15},{8,0},{9,1},... | collective-permute-start | bytes 393224 | tf_op jit(solution)/shard_map/ppermute | solution.py:446
  54.4 0.0 collective-permute-start.8
  54.4 0.0 collective-permute-start.9
  54.4 2.7 %shard_map.67 = (f32[64,2048]{1,0:T(8,128)S(1)}, f32[64,128]{1,0:T(8,128)S(1)}) custom-call(bf16[64,1024]{1,0:T(8,128)(2,1)S(1)} %get-tuple-element.42.s2, bf16[64,1024]{1,0:T(8,128)(2,1)S(1)} %get-tuple-element.43.s0, bf16[64,2048]{1,0:T(8,128)(2,1)S(1)} %get-tuple-element.44.mid, bf16[64,1024]{1,0:T(8,128)(2,1)S(1)} %get-tuple-element.45.s1, ...), custom_call_target="tpu_custom_call" | custom-call | flops 671088640 | tf_op jit(solution)/shard_map/pallas_call | solution.py:458
  57.2 0.0 collective-permute-done.10.r2
  57.2 2.3 %collective-permute-done.8.r0 = bf16[64,1024]{1,0:T(8,128)(2,1)S(1)} collective-permute-done((bf16[64,1024]{1,0:T(8,128)(2,1)S(1)}, bf16[64,1024]{1,0:T(8,128)(2,1)S(1)}, u32[]{:S(2)}, u32[]{:S(2)}) %collective-permute-start.8) | collective-permute-done | bytes 131104 | tf_op jit(solution)/shard_map/ppermute | solution.py:395
  59.5 0.5 collective-permute-done.9.r1
  60.0 0.7 shard_map.68
  60.7 0.8 collective-permute-start.11
  61.5 0.8 collective-permute-done.11
  62.4 10.3 %all_to_all.10 = f32[16,32,128]{2,1,0:T(8,128)S(1)} all-to-all(f32[16,32,128]{2,1,0:T(8,128)S(1)} %broadcast_in_dim.4), channel_id=1, replica_groups={{0,16,32,48,64,80,96,112,128,144,160,176,192,208,224,240},{1,17,33,49,6..., dimensions={0} | all-to-all | bytes 524288 | tf_op jit(solution)/shard_map/all_to_all | solution.py:363
  72.8 10.3 %all_to_all.11 = f32[8,32,128]{2,1,0:T(8,128)S(1)} all-to-all(f32[8,32,128]{2,1,0:T(8,128)S(1)} %broadcast_in_dim.5), channel_id=1, replica_groups=mesh['dom'=32,'board'=8] {'board'}, dimensions={0} | all-to-all | bytes 262144 | tf_op jit(solution)/shard_map/all_to_all | solution.py:365
  83.1 3.0 %collective-permute-start.12 = (f32[32,128]{1,0:T(8,128)S(1)}, f32[32,128]{1,0:T(8,128)S(1)}, u32[]{:S(2)}, u32[]{:S(2)}) collective-permute-start(f32[32,128]{1,0:T(8,128)S(1)} %reduce_sum.19.mine), channel_id=1, source_target_pairs={{0,8},{1,9},{2,10},{3,11},{4,12},{5,13},{6,14},{7,15},{8,0},{9,1},... | collective-permute-start | bytes 49160 | tf_op jit(solution)/shard_map/ppermute | solution.py:366
  86.1 0.8 collective-permute-done.12.other
  86.9 3.0 %shard_map.69 = (bf16[64,4096]{1,0:T(8,128)(2,1)}, f32[64,64]{1,0:T(8,128)}) custom-call(f32[32,128]{1,0:T(8,128)S(1)} %reduce_sum.19.mine, f32[32,128]{1,0:T(8,128)S(1)} %collective-permute-done.12.other, bf16[64,1024]{1,0:T(8,128)(2,1)S(1)} %get-tuple-element.43.s0, bf16[64,2048]{1,0:T(8,128)(2,1)S(1)} %get-tuple-element.44.mid, ...), custom_call_target="tpu_custom_call" | custom-call | flops 100663296 | tf_op jit(solution)/shard_map/pallas_call | solution.py:477
  (5 shorter events, 0.1 us)
Async XLA Ops:
  1.6 14.0 %collective-permute-start.1 = (bf16[64,1024]{1,0:T(8,128)(2,1)S(1)}, bf16[64,1024]{1,0:T(8,128)(2,1)S(1)}, u32[]{:S(2)}, u32[]{:S(2)}) collective-permute-start(bf16[64,1024]{1,0:T(8,128)(2,1)S(1)} %get-tuple-element.50.s1.old1), channel_id=1, source_target_pairs={{0,255},{1,2},{2,1},{3,4},{4,3},{5,6},{6,5},{7,8},{8,7},{9,10},{10... | collective-permute-start | bytes 393224 | tf_op jit(solution)/shard_map/ppermute | solution.py:394
  8.7 6.9 %collective-permute-start = (bf16[64,1024]{1,0:T(8,128)(2,1)S(1)}, bf16[64,1024]{1,0:T(8,128)(2,1)S(1)}, u32[]{:S(2)}, u32[]{:S(2)}) collective-permute-start(bf16[64,1024]{1,0:T(8,128)(2,1)S(1)} %get-tuple-element.51.s0.old0), channel_id=1, source_target_pairs={{0,1},{1,0},{2,3},{3,2},{4,5},{5,4},{6,7},{7,6},{8,9},{9,8},{10,11... | collective-permute-start | bytes 393224 | tf_op jit(solution)/shard_map/ppermute | solution.py:395
  16.1 7.1 %collective-permute-start.3 = (bf16[64,1024]{1,0:T(8,128)(2,1)S(1)}, bf16[64,1024]{1,0:T(8,128)(2,1)S(1)}, u32[]{:S(2)}, u32[]{:S(2)}) collective-permute-start(bf16[64,1024]{1,0:T(8,128)(2,1)S(1)} %get-tuple-element.29.s1.old1), channel_id=1, source_target_pairs={{0,255},{1,2},{2,1},{3,4},{4,3},{5,6},{6,5},{7,8},{8,7},{9,10},{10... | collective-permute-start | bytes 393224 | tf_op jit(solution)/shard_map/ppermute | solution.py:394
  18.4 4.8 %collective-permute-start.2 = (bf16[64,1024]{1,0:T(8,128)(2,1)S(1)}, bf16[64,1024]{1,0:T(8,128)(2,1)S(1)}, u32[]{:S(2)}, u32[]{:S(2)}) collective-permute-start(bf16[64,1024]{1,0:T(8,128)(2,1)S(1)} %get-tuple-element.31.s0.old0), channel_id=1, source_target_pairs={{0,1},{1,0},{2,3},{3,2},{4,5},{5,4},{6,7},{7,6},{8,9},{9,8},{10,11... | collective-permute-start | bytes 393224 | tf_op jit(solution)/shard_map/ppermute | solution.py:395
  23.6 6.5 %collective-permute-start.5 = (bf16[64,1024]{1,0:T(8,128)(2,1)S(1)}, bf16[64,1024]{1,0:T(8,128)(2,1)S(1)}, u32[]{:S(2)}, u32[]{:S(2)}) collective-permute-start(bf16[64,1024]{1,0:T(8,128)(2,1)S(1)} %get-tuple-element.34.s1.old1), channel_id=1, source_target_pairs={{0,255},{1,2},{2,1},{3,4},{4,3},{5,6},{6,5},{7,8},{8,7},{9,10},{10... | collective-permute-start | bytes 393224 | tf_op jit(solution)/shard_map/ppermute | solution.py:394
  26.0 4.1 %collective-permute-start.4 = (bf16[64,1024]{1,0:T(8,128)(2,1)S(1)}, bf16[64,1024]{1,0:T(8,128)(2,1)S(1)}, u32[]{:S(2)}, u32[]{:S(2)}) collective-permute-start(bf16[64,1024]{1,0:T(8,128)(2,1)S(1)} %get-tuple-element.36.s0.old0), channel_id=1, source_target_pairs={{0,1},{1,0},{2,3},{3,2},{4,5},{5,4},{6,7},{7,6},{8,9},{9,8},{10,11... | collective-permute-start | bytes 393224 | tf_op jit(solution)/shard_map/ppermute | solution.py:395
  30.6 5.9 %collective-permute-start.7 = (bf16[64,1024]{1,0:T(8,128)(2,1)S(1)}, bf16[64,1024]{1,0:T(8,128)(2,1)S(1)}, u32[]{:S(2)}, u32[]{:S(2)}) collective-permute-start(bf16[64,1024]{1,0:T(8,128)(2,1)S(1)} %get-tuple-element.38.s1), channel_id=1, source_target_pairs={{0,255},{1,2},{2,1},{3,4},{4,3},{5,6},{6,5},{7,8},{8,7},{9,10},{10... | collective-permute-start | bytes 393224 | tf_op jit(solution)/shard_map/ppermute | solution.py:394
  33.3 4.5 %collective-permute-start.6 = (bf16[64,1024]{1,0:T(8,128)(2,1)S(1)}, bf16[64,1024]{1,0:T(8,128)(2,1)S(1)}, u32[]{:S(2)}, u32[]{:S(2)}) collective-permute-start(bf16[64,1024]{1,0:T(8,128)(2,1)S(1)} %get-tuple-element.40.s0), channel_id=1, source_target_pairs={{0,1},{1,0},{2,3},{3,2},{4,5},{5,4},{6,7},{7,6},{8,9},{9,8},{10,11... | collective-permute-start | bytes 393224 | tf_op jit(solution)/shard_map/ppermute | solution.py:395
  38.3 18.9 %collective-permute-start.10 = (bf16[64,1024]{1,0:T(8,128)(2,1)S(1)}, bf16[64,1024]{1,0:T(8,128)(2,1)S(1)}, u32[]{:S(2)}, u32[]{:S(2)}) collective-permute-start(bf16[64,1024]{1,0:T(8,128)(2,1)S(1)} %get-tuple-element.42.s2), channel_id=1, source_target_pairs={{0,8},{1,9},{2,10},{3,11},{4,12},{5,13},{6,14},{7,15},{8,0},{9,1},... | collective-permute-start | bytes 393224 | tf_op jit(solution)/shard_map/ppermute | solution.py:446
  54.4 5.1 %collective-permute-start.8 = (bf16[64,1024]{1,0:T(8,128)(2,1)S(1)}, bf16[64,1024]{1,0:T(8,128)(2,1)S(1)}, u32[]{:S(2)}, u32[]{:S(2)}) collective-permute-start(bf16[64,1024]{1,0:T(8,128)(2,1)S(1)} %get-tuple-element.43.s0), channel_id=1, source_target_pairs={{0,1},{1,0},{2,3},{3,2},{4,5},{5,4},{6,7},{7,6},{8,9},{9,8},{10,11... | collective-permute-start | bytes 393224 | tf_op jit(solution)/shard_map/ppermute | solution.py:395
  54.4 5.6 %collective-permute-start.9 = (bf16[64,1024]{1,0:T(8,128)(2,1)S(1)}, bf16[64,1024]{1,0:T(8,128)(2,1)S(1)}, u32[]{:S(2)}, u32[]{:S(2)}) collective-permute-start(bf16[64,1024]{1,0:T(8,128)(2,1)S(1)} %get-tuple-element.45.s1), channel_id=1, source_target_pairs={{0,64},{1,2},{2,1},{3,4},{4,3},{5,6},{6,5},{7,8},{8,7},{9,10},{10,... | collective-permute-start | bytes 393224 | tf_op jit(solution)/shard_map/ppermute | solution.py:394
  60.7 1.6 %collective-permute-start.11 = (f32[32,128]{1,0:T(8,128)S(1)}, f32[32,128]{1,0:T(8,128)S(1)}, u32[]{:S(2)}, u32[]{:S(2)}) collective-permute-start(f32[32,128]{1,0:T(8,128)S(1)} %get-tuple-element.49), channel_id=1, source_target_pairs={{0,8},{1,9},{2,10},{3,11},{4,12},{5,13},{6,14},{7,15},{8,0},{9,1},... | collective-permute-start | bytes 49160 | tf_op jit(solution)/shard_map/ppermute | solution.py:360
  83.1 3.8 %collective-permute-start.12 = (f32[32,128]{1,0:T(8,128)S(1)}, f32[32,128]{1,0:T(8,128)S(1)}, u32[]{:S(2)}, u32[]{:S(2)}) collective-permute-start(f32[32,128]{1,0:T(8,128)S(1)} %reduce_sum.19.mine), channel_id=1, source_target_pairs={{0,8},{1,9},{2,10},{3,11},{4,12},{5,13},{6,14},{7,15},{8,0},{9,1},... | collective-permute-start | bytes 49160 | tf_op jit(solution)/shard_map/ppermute | solution.py:366
